TPU v7x, 32 devices: a whole 2x2x4 slice. The times are simulated.
32 devices in a mesh: group: 2 (over x), lat: 16 (over z, y, core).
Axes of the slice: x: 2, y: 2, z: 4, core: 2. Of those that a mesh axis runs over, the one named last changes fastest.
Arguments:
- features: bfloat16 [96, 1440, 256], P(('group', 'lat')), parts along dimension 0, may hold values from -6 to 6
- disco_rows: int32 [48, 9], P('lat'), may hold values from 0 to 47, as said below
- disco_cols: int32 [48, 9], P('lat'), may hold values from -16 to 16
- disco_basis: bfloat16 [3, 48, 9], P(None, 'lat'), may hold values from -1 to 1
- disco_weight: bfloat16 [3, 256, 256], replicated, may hold values from -0.21875 to 0.21875
- spectral_gain: float32 [48, 256], replicated, may hold values from 0.5 to 2
- grad_output: bfloat16 [96, 1440, 256], P(('group', 'lat')), parts along dimension 0, may hold values from -6 to 6
Outputs:
- output: bfloat16 [96, 1440, 256], P(('group', 'lat')), parts along dimension 0
- grad_features: bfloat16 [96, 1440, 256], P(('group', 'lat')), parts along dimension 0
- grad_weight: float32 [6, 256, 256], P('group'), parts along dimension 0
- grad_gain: float32 [96, 256], P('group'), parts along dimension 0
There are 2 independent parts, one for each index of `group`. A program takes and returns all parts, laid end to end along the dimension named above; an argument that names none is the same for every part. Nothing has to cross between parts.
Inputs may be any that keep to these rules, and one draw needn't show every extreme that they name: disco_rows[i, t] lies within 1 row of row i.
All inputs are finite; a program needn't handle non-finite values.
Results may differ from a plain program's by a relative error of at most 0.0083.
Values may be sent and summed in bfloat16 or wider, within the bound.
No kernel may reach another device: no remote copies, remote signals or barrier semaphores. Data moves between devices by JAX's collectives and lax.ppermute only.
A program may use at most 192 MiB of HBM per device.

v0:
```python
import math

import jax
import jax.numpy as jnp
import numpy as np
from jax import lax
from jax.sharding import PartitionSpec as P

MM_DEV = 3
HALO = 1


def padded(cells, sides, width):
    for axis, dim in sides:
        count = lax.axis_size(axis)
        ends = count - 1
        head = lax.slice_in_dim(cells, 0, width, axis=dim)
        tail = lax.slice_in_dim(cells, cells.shape[dim] - width, cells.shape[dim], axis=dim)
        cells = jnp.concatenate(
            [
                lax.ppermute(tail, axis, [(i, (i + 1) % count) for i in range(ends)]),
                cells,
                lax.ppermute(head, axis, [((i + 1) % count, i) for i in range(ends)]),
            ],
            axis=dim,
        )
    return cells


def passed_along(array, axis, by):
    length = lax.axis_size(axis)
    pairs = [(i, i + by) for i in range(length) if 0 <= i + by < length]
    return lax.ppermute(array, axis, pairs)


def legendre_pair(nodes, lat_count):
    before = nodes * 0.0 + 1.0
    current = nodes * 1.0
    for degree in range(2, lat_count + 1):
        following = ((2.0 * degree - 1.0) * nodes * current - (degree - 1.0) * before) / degree
        before = current
        current = following
    return (before, current)


def gauss_grid(lat_count):
    counter = np.arange(1, lat_count + 1) * 1.0
    nodes = np.cos(np.pi * (counter - 0.25) / (lat_count + 0.5))
    for sweep in range(12):
        before, current = legendre_pair(nodes, lat_count)
        slope = lat_count * (nodes * current - before) / (nodes * nodes - 1.0)
        nodes = nodes - current / slope
    before, current = legendre_pair(nodes, lat_count)
    slope = lat_count * (nodes * current - before) / (nodes * nodes - 1.0)
    weights = 2.0 / ((1.0 - nodes * nodes) * slope * slope)
    return (nodes, weights)


def diagonal_table(order_count, latitude_nodes):
    sine_values = np.sqrt(1.0 - latitude_nodes * latitude_nodes)
    orders = np.arange(order_count)
    positive = np.arange(1, order_count)
    log_steps = np.concatenate(
        [np.zeros(1), 0.5 * np.cumsum(np.log((2.0 * positive + 1.0) / (2.0 * positive)))]
    )
    log_values = (
        0.5 * np.log(0.5) + log_steps[:, None] + orders[:, None] * np.log(sine_values)[None, :]
    )
    return np.exp(log_values)


def legendre_block(orders, order_count, degrees, lat_count):
    latitude_nodes, weights = gauss_grid(lat_count)
    diagonal_start = jnp.asarray(diagonal_table(order_count, latitude_nodes), jnp.float32)[orders]
    node_row = jnp.asarray(latitude_nodes, jnp.float32)[None, :]
    order_column = orders.astype(jnp.float32)[:, None]

    def block_step(carry, block_index):
        previous, earlier = carry
        produced = []
        for offset in range(16):
            degree = (block_index * 16 + offset).astype(jnp.float32)
            squared = degree * degree
            order_squared = order_column * order_column
            forward_factor = jnp.sqrt(
                jnp.maximum(4.0 * squared - 1.0, 1.0) / jnp.maximum(squared - order_squared, 1.0)
            )
            lower = (degree - 1.0) * (degree - 1.0)
            back_factor = jnp.sqrt(
                jnp.maximum(lower - order_squared, 0.0) / jnp.maximum(4.0 * lower - 1.0, 1.0)
            )
            recurred = forward_factor * (node_row * previous - back_factor * earlier)
            fresh = jnp.where(
                degree < order_column,
                0.0,
                jnp.where(degree == order_column, diagonal_start, recurred),
            )
            earlier = previous
            previous = fresh
            produced.append(fresh)
        return ((previous, earlier), jnp.stack(produced))

    zeros = jnp.zeros((orders.shape[0], lat_count), jnp.float32)
    _, blocks = lax.scan(block_step, (zeros, zeros), jnp.arange(degrees // 16, dtype=jnp.int32))
    legendre = blocks.reshape(degrees, orders.shape[0], lat_count)
    return jnp.transpose(legendre, (1, 0, 2))


def fourier_tables(lon_count, order_count):
    frequency = lax.broadcasted_iota(jnp.int32, (lon_count, order_count), 1)
    column = lax.broadcasted_iota(jnp.int32, (lon_count, order_count), 0)
    phases = 2.0 * math.pi / lon_count * (frequency * column % lon_count).astype(jnp.float32)
    cosine = jnp.cos(phases)
    sine_part = jnp.sin(phases)
    forward_table = (
        (jnp.stack([cosine, -sine_part], axis=2) / lon_count)
        .reshape(lon_count, 2 * order_count)
        .astype(jnp.bfloat16)
    )
    weight_m = jnp.where(frequency == 0, 1.0, 2.0).astype(jnp.float32)
    inverse_table = jnp.stack([weight_m * cosine, -weight_m * sine_part], axis=2).reshape(
        lon_count, 2 * order_count
    )
    return (forward_table, jnp.transpose(inverse_table).astype(jnp.bfloat16))


def local(features, disco_rows, disco_cols, disco_basis, disco_weight, spectral_gain, grad_output):
    lat_dev, lon_count, channels = features.shape
    devices = lax.axis_size("lat")
    position = lax.axis_index("lat")
    order_count = MM_DEV * devices
    lat_count = lat_dev * devices
    kernel_count = disco_weight.shape[0]
    forward_table, inverse_table = fourier_tables(lon_count, order_count)
    _, gauss_weights = gauss_grid(lat_count)
    weights = jnp.asarray(gauss_weights, jnp.float32)
    extended = padded(features, (("lat", 0),), HALO)
    row_offset = position * lat_dev - HALO
    local_rows = disco_rows - row_offset
    basis_rows = jnp.transpose(disco_basis, (1, 0, 2))

    def longitudes(col_shift):
        return (
            lax.broadcasted_iota(jnp.int32, (col_shift.shape[0], lon_count), 1) + col_shift[:, None]
        ) % lon_count

    def disco_row(packed):
        row_index, col_shift, basis = packed
        gathered = extended[row_index[:, None], longitudes(col_shift)]
        mixed = jnp.einsum(
            "kt,tjc->kjc", basis, gathered, preferred_element_type=jnp.float32
        ).astype(jnp.bfloat16)
        row_term = jnp.einsum(
            "kjc,kcd->jd", mixed, disco_weight, preferred_element_type=jnp.float32
        )
        return (mixed, row_term)

    mixed, disco_term = lax.map(disco_row, (local_rows, disco_cols, basis_rows))
    coefficients = jnp.einsum(
        "ijc,jq->iqc", features, forward_table, preferred_element_type=jnp.float32
    ).astype(jnp.bfloat16)
    coefficients = coefficients.reshape(lat_dev, order_count, 2 * channels)
    owned = lax.all_to_all(coefficients, "lat", split_axis=1, concat_axis=0, tiled=True)
    orders = position * MM_DEV + jnp.arange(MM_DEV, dtype=jnp.int32)
    legendre = legendre_block(orders, order_count, order_count, lat_count)
    plain_half = legendre.astype(jnp.bfloat16)
    weighted_half = (legendre * weights[None, None, :]).astype(jnp.bfloat16)
    gain_pair = jnp.concatenate([spectral_gain, spectral_gain], axis=1)
    analysed = jnp.einsum("rln,nrq->rlq", weighted_half, owned, preferred_element_type=jnp.float32)
    scaled = (analysed * gain_pair[None]).astype(jnp.bfloat16)
    synthesized = jnp.einsum(
        "rln,rlq->nrq", plain_half, scaled, preferred_element_type=jnp.float32
    ).astype(jnp.bfloat16)
    returned = lax.all_to_all(synthesized, "lat", split_axis=0, concat_axis=1, tiled=True)
    returned = returned.reshape(lat_dev, 2 * order_count, channels)
    spectral_term = jnp.einsum(
        "iqc,qj->ijc", returned, inverse_table, preferred_element_type=jnp.float32
    )
    total = disco_term + spectral_term
    output, gelu_pull = jax.vjp(jax.nn.gelu, total)
    grad_total = gelu_pull(grad_output.astype(jnp.float32))[0].astype(jnp.bfloat16)
    grad_synth = jnp.einsum(
        "ijc,qj->iqc", grad_total, inverse_table, preferred_element_type=jnp.float32
    ).astype(jnp.bfloat16)
    grad_synth = grad_synth.reshape(lat_dev, order_count, 2 * channels)
    grad_owned = lax.all_to_all(grad_synth, "lat", split_axis=1, concat_axis=0, tiled=True)
    grad_scaled = jnp.einsum(
        "rln,nrq->rlq", plain_half, grad_owned, preferred_element_type=jnp.float32
    )
    gain_terms = jnp.sum(analysed * grad_scaled, axis=0)
    gain_part = gain_terms[:, :channels] + gain_terms[:, channels:]
    grad_analysed = (gain_pair[None] * grad_scaled).astype(jnp.bfloat16)
    grad_coeff = jnp.einsum(
        "rln,rlq->nrq", weighted_half, grad_analysed, preferred_element_type=jnp.float32
    ).astype(jnp.bfloat16)
    grad_bands = lax.all_to_all(grad_coeff, "lat", split_axis=0, concat_axis=1, tiled=True)
    grad_bands = grad_bands.reshape(lat_dev, 2 * order_count, channels)
    grad_spectral = jnp.einsum(
        "iqc,jq->ijc", grad_bands, forward_table, preferred_element_type=jnp.float32
    )

    def spread_taps(ext_grad, row_index, col_shift, basis, grad_row):
        grad_mixed = jnp.einsum(
            "jd,kcd->kjc", grad_row, disco_weight, preferred_element_type=jnp.float32
        )
        tap_grad = jnp.einsum(
            "kt,kjc->tjc", basis.astype(jnp.float32), grad_mixed, precision=lax.Precision.HIGHEST
        )
        return ext_grad.at[row_index[:, None], longitudes(col_shift)].add(tap_grad)

    def adjoint_row(carry, packed):
        weight_acc, ext_grad = carry
        row_index, col_shift, basis, mixed_row, grad_row = packed
        weight_acc = weight_acc + jnp.einsum(
            "kjc,jd->kcd", mixed_row, grad_row, preferred_element_type=jnp.float32
        )
        ext_grad = spread_taps(ext_grad, row_index, col_shift, basis, grad_row)
        return ((weight_acc, ext_grad), None)

    start_carry = (
        jnp.zeros((kernel_count, channels, channels), jnp.float32),
        jnp.zeros((lat_dev + 2 * HALO, lon_count, channels), jnp.float32),
    )
    (weight_part, ext_grad), _ = lax.scan(
        adjoint_row, start_carry, (local_rows, disco_cols, basis_rows, mixed, grad_total)
    )
    interior = ext_grad[HALO : HALO + lat_dev]
    top_rim = ext_grad[:HALO]
    bottom_rim = ext_grad[HALO + lat_dev :]
    from_below = passed_along(top_rim.astype(jnp.bfloat16), "lat", -1).astype(top_rim.dtype)
    from_above = passed_along(bottom_rim, "lat", 1)
    disco_grad = interior.at[:HALO].add(from_above).at[lat_dev - HALO :].add(from_below)
    grad_features = (grad_spectral + disco_grad).astype(jnp.bfloat16)
    grad_weight, grad_gain = lax.psum((weight_part, gain_part), "lat")
    return (output.astype(jnp.bfloat16), grad_features, grad_weight, grad_gain)


def solution(mesh):
    return jax.shard_map(
        local,
        mesh=mesh,
        in_specs=(
            P(("group", "lat"), None, None),
            P("lat", None),
            P("lat", None),
            P(None, "lat", None),
            P(),
            P(),
            P(("group", "lat"), None, None),
        ),
        out_specs=(
            P(("group", "lat"), None, None),
            P(("group", "lat"), None, None),
            P("group", None, None),
            P("group", None),
        ),
        check_vma=False,
    )
```

profile of v0, /device:TPU:0, one launch (start us, length us, event | category | flops | bytes accessed | tf_op | source)
XLA Modules:
  0.0 1178.7 jit_solution(12015740489970665359)
XLA Ops:
  12.1 7.5 all-to-all-start
  26.0 10.3 while.53
  41.1 7.4 all-to-all-start.1
  49.1 8.3 all-to-all-done.1
  63.7 618.2 %while.51 = (s32[]{:T(128)}, bf16[3,3,1440,256]{3,2,1,0:T(8,128)(2,1)}, f32[3,1440,256]{2,1,0:T(8,128)}, bf16[3,3,9]{2,1,0:T(4,128)(2,1)S(1)}, s32[3,9]{1,0:T(4,...) while((s32[]{:T(128)}, ...), condition=%wide.region_1.2_spmd, body=%wide.region_0.1_spmd.sunk | while | flops 587412032 | bytes 67009032 | solution.py:158
  64.0 195.1 %gather_fusion = bf16[12960,256]{1,0:T(8,128)(2,1)} fusion(bf16[5,1440,256]{2,1,0:T(8,128)(2,1)} %get-tuple-element.1128, s32[12960]{0:T(1024)S(1)} %reshape.1415), kind=kCustom, calls=%fused_computation.clone.1 | custom fusion | bytes 13374720 | tf_op jit(solution)/shard_map/while/body/eval_jaxpr/gather | solution.py:149
  259.1 7.3 fusion.120
  270.2 195.1 %gather_fusion = bf16[12960,256]{1,0:T(8,128)(2,1)} fusion(bf16[5,1440,256]{2,1,0:T(8,128)(2,1)} %get-tuple-element.1128, s32[12960]{0:T(1024)S(1)} %reshape.1415), kind=kCustom, calls=%fused_computation.clone.1 | custom fusion | bytes 13374720 | tf_op jit(solution)/shard_map/while/body/eval_jaxpr/gather | solution.py:149
  465.3 7.3 fusion.120
  476.4 194.8 %gather_fusion = bf16[12960,256]{1,0:T(8,128)(2,1)} fusion(bf16[5,1440,256]{2,1,0:T(8,128)(2,1)} %get-tuple-element.1128, s32[12960]{0:T(1024)S(1)} %reshape.1415), kind=kCustom, calls=%fused_computation.clone.1 | custom fusion | bytes 13374720 | tf_op jit(solution)/shard_map/while/body/eval_jaxpr/gather | solution.py:149
  671.2 7.3 fusion.120
  681.9 7.2 fusion.47
  689.1 3.6 broadcast_in_dim.439
  692.6 343.2 %while.52 = (s32[]{:T(128)}, f32[3,256,256]{2,1,0:T(8,128)}, f32[5,1440,256]{2,1,0:T(8,128)}, bf16[3,3,1440,256]{3,2,1,0:T(8,128)(2,1)}, bf16[3,1440,256]{2,1,0:...) while((s32[]{:T(128)}, f32[3,256,256]{2,1,0:T(8,128)}, ...), condition=%wide.region_6.7_spmd.clone, body=%wide.region_4.6_spmd.clone.sunk | while | flops 1255936384 | bytes 94777024 | solution.py:224
  706.0 3.3 fusion.128
  710.2 14.5 %fusion.130 = f32[9,1440,256]{2,0,1:T(8,128)S(1)} fusion(f32[3,1440,256]{2,1,0:T(8,128)S(1)} %convolution_bitcast_fusion.3, bf16[3,3,9]{2,1,0:T(4,128)(2,1)S(1)} %get-tuple-element.1251, s32[]{:T(128)S(6)} %copy.190), kind=kOutput, calls=%fused_computation.30.clone.1 | convolution fusion | flops 119439360 | bytes 17695748 | tf_op jit(solution)/shard_map/while/body/eval_jaxpr/kt,kjc->tjc/dot_general | solution.py:206
  724.7 12.5 %copy.146 = f32[9,1440,256]{2,1,0:T(8,128)} copy(f32[9,1440,256]{2,0,1:T(8,128)S(1)} %fusion.130) | data formatting | bytes 26542080 | tf_op jit(solution)/shard_map/while/body/eval_jaxpr/kt,kjc->tjc/dot_general | solution.py:206
  737.1 77.9 %scatter_fusion = f32[7200,256]{1,0:T(8,128)} fusion(f32[7200,256]{1,0:T(8,128)} %bitcast.462, s32[12960]{0:T(1024)S(1)} %reshape.1418, f32[12960,256]{1,0:T(8,128)} %bitcast.464), kind=kCustom, calls=%fused_computation.2.clone.clone.1 | custom fusion | flops 3317760 | bytes 39864960 | tf_op jit(solution)/shard_map/while
  816.2 3.5 fusion.128
  820.5 14.5 %fusion.130 = f32[9,1440,256]{2,0,1:T(8,128)S(1)} fusion(f32[3,1440,256]{2,1,0:T(8,128)S(1)} %convolution_bitcast_fusion.3, bf16[3,3,9]{2,1,0:T(4,128)(2,1)S(1)} %get-tuple-element.1251, s32[]{:T(128)S(6)} %copy.190), kind=kOutput, calls=%fused_computation.30.clone.1 | convolution fusion | flops 119439360 | bytes 17695748 | tf_op jit(solution)/shard_map/while/body/eval_jaxpr/kt,kjc->tjc/dot_general | solution.py:206
  835.0 12.5 %copy.146 = f32[9,1440,256]{2,1,0:T(8,128)} copy(f32[9,1440,256]{2,0,1:T(8,128)S(1)} %fusion.130) | data formatting | bytes 26542080 | tf_op jit(solution)/shard_map/while/body/eval_jaxpr/kt,kjc->tjc/dot_general | solution.py:206
  847.4 77.9 %scatter_fusion = f32[7200,256]{1,0:T(8,128)} fusion(f32[7200,256]{1,0:T(8,128)} %bitcast.462, s32[12960]{0:T(1024)S(1)} %reshape.1418, f32[12960,256]{1,0:T(8,128)} %bitcast.464), kind=kCustom, calls=%fused_computation.2.clone.clone.1 | custom fusion | flops 3317760 | bytes 39864960 | tf_op jit(solution)/shard_map/while
  926.5 3.5 fusion.128
  930.8 14.5 %fusion.130 = f32[9,1440,256]{2,0,1:T(8,128)S(1)} fusion(f32[3,1440,256]{2,1,0:T(8,128)S(1)} %convolution_bitcast_fusion.3, bf16[3,3,9]{2,1,0:T(4,128)(2,1)S(1)} %get-tuple-element.1251, s32[]{:T(128)S(6)} %copy.190), kind=kOutput, calls=%fused_computation.30.clone.1 | convolution fusion | flops 119439360 | bytes 17695748 | tf_op jit(solution)/shard_map/while/body/eval_jaxpr/kt,kjc->tjc/dot_general | solution.py:206
  945.3 12.5 %copy.146 = f32[9,1440,256]{2,1,0:T(8,128)} copy(f32[9,1440,256]{2,0,1:T(8,128)S(1)} %fusion.130) | data formatting | bytes 26542080 | tf_op jit(solution)/shard_map/while/body/eval_jaxpr/kt,kjc->tjc/dot_general | solution.py:206
  957.7 77.9 %scatter_fusion = f32[7200,256]{1,0:T(8,128)} fusion(f32[7200,256]{1,0:T(8,128)} %bitcast.462, s32[12960]{0:T(1024)S(1)} %reshape.1418, f32[12960,256]{1,0:T(8,128)} %bitcast.464), kind=kCustom, calls=%fused_computation.2.clone.clone.1 | custom fusion | flops 3317760 | bytes 39864960 | tf_op jit(solution)/shard_map/while
  1041.6 11.6 all_to_all.66
  1055.6 13.8 %all-to-all-start.3 = ((bf16[48,3,512]{2,1,0:T(4,128)(2,1)}), bf16[48,3,512]{2,1,0:T(4,128)(2,1)S(1)}, u32[]{:S(2)}, u32[]{:S(2)}) async-start(bf16[48,3,512]{2,1,0:T(4,128)(2,1)} %copy.103), calls=%async_computation.3 | async-start | bytes 393216 | tf_op jit(solution)/shard_map/all_to_all | solution.py:196
  1070.9 4.6 slice.73
  1076.8 64.4 %psum.15 = f32[48,256]{1,0:T(8,128)} all-reduce(f32[48,256]{1,0:T(8,128)S(1)} %slice_add_fusion.1), channel_id=1, replica_groups=mesh['group'=2,'lat'=16] {'lat'}, use_global_device_ids=true, to_apply=%region_9.10 | all-reduce | flops 12288 | bytes 98304 | tf_op jit(solution)/shard_map/psum | solution.py:234
  1147.3 4.4 fusion.55
  1151.7 17.8 %all-reduce.2.cloned.1.call-done = f32[3,256,256]{2,1,0:T(8,128)} async-done(((f32[3,256,256]{2,1,0:T(8,128)}), f32[3,256,256]{2,1,0:T(8,128)}) %all-reduce.2.cloned.1.call-update) | async-done | bytes 786448 | tf_op jit(solution)/shard_map/psum | solution.py:234
  (318 shorter events, 65.7 us)
Async XLA Ops:
  7.2 12.5 %copy-start.1 = (bf16[3,1440,256]{2,1,0:T(8,128)(2,1)S(1)}, bf16[3,1440,256]{2,1,0:T(8,128)(2,1)}, u32[]{:S(2)}) copy-start(bf16[3,1440,256]{2,1,0:T(8,128)(2,1)} %param.20) | copy-start | bytes 6635524
  8.4 17.0 %copy-start.19 = (f32[48,48]{1,0:T(8,128)S(1)}, f32[48,48]{1,0:T(8,128)}, u32[]{:S(2)}) copy-start(f32[48,48]{1,0:T(8,128)} %constant.403.clone) | copy-start | bytes 27652
  8.4 17.6 %copy-start.4 = (f32[48]{0:T(128)S(1)}, f32[48]{0:T(128)}, u32[]{:S(2)}) copy-start(f32[48]{0:T(128)} %constant.669) | copy-start | bytes 580
  9.0 17.0 %copy-start.5 = (bf16[1440,96,1]{0,1,2:T(8,128)(2,1)}, bf16[1440,96,1]{0,1,2:T(8,128)(2,1)S(1)}, u32[]{:S(2)}) copy-start(bf16[1440,96,1]{0,1,2:T(8,128)(2,1)S(1)} %reshape.1403) | copy-start | bytes 829444
  12.1 26.7 %copy-start.16 = (f32[48,256]{1,0:T(8,128)S(1)}, f32[48,256]{1,0:T(8,128)}, u32[]{:S(2)}) copy-start(f32[48,256]{1,0:T(8,128)} %param.25) | copy-start | bytes 147460
  12.1 26.7 %all-to-all-start = ((bf16[3,48,512]{2,0,1:T(4,128)(2,1)}), bf16[3,48,512]{2,0,1:T(4,128)(2,1)S(1)}, u32[]{:S(2)}, u32[]{:S(2)}) async-start(bf16[3,48,512]{2,0,1:T(4,128)(2,1)} %copy.91), calls=%async_computation | async-start | bytes 393216 | tf_op jit(solution)/shard_map/all_to_all | solution.py:163
  19.6 19.4 %copy-start.22 = (f32[48]{0:T(128)S(1)}, f32[48]{0:T(128)}, u32[]{:S(2)}) copy-start(f32[48]{0:T(128)} %constant.402.clone) | copy-start | bytes 580
  20.9 39.7 %collective-permute-start = (bf16[1,1440,256]{2,1,0:T(8,128)(2,1)}, bf16[1,1440,256]{2,1,0:T(8,128)(2,1)}, u32[]{:S(2)}, u32[]{:S(2)}) collective-permute-start(bf16[1,1440,256]{2,1,0:T(8,128)(2,1)} %get-tuple-element.757), channel_id=1, source_target_pairs={{0,1},{1,2},{2,3},{3,4},{4,5},{5,6},{6,7},{7,8},{8,9},{9,10},{10,1... | collective-permute-start | bytes 2211848 | tf_op jit(solution)/shard_map/ppermute | solution.py:21
  24.0 36.5 %collective-permute-start.1 = (bf16[1,1440,256]{2,1,0:T(8,128)(2,1)}, bf16[1,1440,256]{2,1,0:T(8,128)(2,1)}, u32[]{:S(2)}, u32[]{:S(2)}) collective-permute-start(bf16[1,1440,256]{2,1,0:T(8,128)(2,1)} %get-tuple-element.758), channel_id=1, source_target_pairs={{1,0},{2,1},{3,2},{4,3},{5,4},{6,5},{7,6},{8,7},{9,8},{10,9},{11,1... | collective-permute-start | bytes 2211848 | tf_op jit(solution)/shard_map/ppermute | solution.py:23
  25.4 23.2 %copy-start.20 = (bf16[3,3,9]{2,1,0:T(4,128)(2,1)S(1)}, bf16[3,3,9]{2,1,0:T(4,128)(2,1)}, u32[]{:S(2)}) copy-start(bf16[3,3,9]{2,1,0:T(4,128)(2,1)} %param.23) | copy-start | bytes 490
  26.0 23.1 %copy-start.21 = (s32[3,9]{1,0:T(4,128)S(1)}, s32[3,9]{1,0:T(4,128)}, u32[]{:S(2)}) copy-start(s32[3,9]{1,0:T(4,128)} %param.21) | copy-start | bytes 328
  36.4 4.8 copy-start.15
  38.8 9.8 copy-start.13
  41.1 16.3 %all-to-all-start.1 = ((bf16[48,3,512]{2,1,0:T(4,128)(2,1)}), bf16[48,3,512]{2,1,0:T(4,128)(2,1)S(1)}, u32[]{:S(2)}, u32[]{:S(2)}) async-start(bf16[48,3,512]{2,1,0:T(4,128)(2,1)} %copy.97), calls=%async_computation.1 | async-start | bytes 393216 | tf_op jit(solution)/shard_map/all_to_all | solution.py:174
  49.1 8.6 copy-start.7
  60.6 3.2 copy-start
  60.6 3.2 copy-start.24
  259.1 7.3 copy-start.2
  465.3 7.3 copy-start.2
  671.2 7.3 copy-start.2
  689.1 3.6 copy-start.17
  689.1 3.6 copy-start.18
  692.6 348.3 %copy-start.8 = (bf16[1440,96,1]{0,1,2:T(8,128)(2,1)S(1)}, bf16[1440,96,1]{0,1,2:T(8,128)(2,1)}, u32[]{:S(2)}) copy-start(bf16[1440,96,1]{0,1,2:T(8,128)(2,1)} %copy-done.7) | copy-start | bytes 829444
  1035.9 17.6 %copy-start.10 = (f32[3,48,512]{2,1,0:T(8,128)S(1)}, f32[3,48,512]{2,1,0:T(8,128)}, u32[]{:S(2)}) copy-start(f32[3,48,512]{2,1,0:T(8,128)} %copy-done.9) | copy-start | bytes 884740
  1035.9 18.6 %copy-start.12 = (f32[48,512]{1,0:T(8,128)S(1)}, f32[48,512]{1,0:T(8,128)}, u32[]{:S(2)}) copy-start(f32[48,512]{1,0:T(8,128)} %copy-done.11) | copy-start | bytes 294916
  1035.9 18.6 %copy-start.14 = (f32[48,3,48]{0,2,1:T(8,128)S(1)}, f32[48,3,48]{0,2,1:T(8,128)}, u32[]{:S(2)}) copy-start(f32[48,3,48]{0,2,1:T(8,128)} %copy-done.13) | copy-start | bytes 82948
  1035.9 18.6 %copy-start.23 = (f32[48]{0:T(128)S(1)}, f32[48]{0:T(128)}, u32[]{:S(2)}) copy-start(f32[48]{0:T(128)} %constant.402.clone) | copy-start | bytes 580
  1038.5 102.9 %collective-permute-start.2 = (f32[1,1440,256]{2,1,0:T(8,128)}, f32[1,1440,256]{2,1,0:T(8,128)}, u32[]{:S(2)}, u32[]{:S(2)}) collective-permute-start(f32[1,1440,256]{2,1,0:T(8,128)} %slice.75), channel_id=1, source_target_pairs={{0,1},{1,2},{2,3},{3,4},{4,5},{5,6},{6,7},{7,8},{8,9},{9,10},{10,1... | collective-permute-start | bytes 4423688 | tf_op jit(solution)/shard_map/ppermute | solution.py:33
  1055.6 85.6 %all-to-all-start.3 = ((bf16[48,3,512]{2,1,0:T(4,128)(2,1)}), bf16[48,3,512]{2,1,0:T(4,128)(2,1)S(1)}, u32[]{:S(2)}, u32[]{:S(2)}) async-start(bf16[48,3,512]{2,1,0:T(4,128)(2,1)} %copy.103), calls=%async_computation.3 | async-start | bytes 393216 | tf_op jit(solution)/shard_map/all_to_all | solution.py:196
  1069.4 100.2 %all-reduce.2.cloned.1.call-start = ((), (), s32[]{:S(2)}) async-start(), calls=%async_computation.4 | async-start | bytes 1572864 | tf_op jit(solution)/shard_map/psum | solution.py:234
  1075.5 69.1 %collective-permute-start.3 = (bf16[1,1440,256]{2,1,0:T(8,128)(2,1)S(1)}, bf16[1,1440,256]{2,1,0:T(8,128)(2,1)S(1)}, u32[]{:S(2)}, u32[]{:S(2)}) collective-permute-start(bf16[1,1440,256]{2,1,0:T(8,128)(2,1)S(1)} %slice.95), channel_id=1, source_target_pairs={{1,0},{2,1},{3,2},{4,3},{5,4},{6,5},{7,6},{8,7},{9,8},{10,9},{11,1... | collective-permute-start | bytes 2211848 | tf_op jit(solution)/shard_map/ppermute | solution.py:33
  1141.2 6.1 copy-start.6
  (5 other events, 11.2 us)
Sparse Core Ops, SparseCore 0:
  1075.6 93.8 all-reduce.1
where the time goes:
time: 1180 us
  local copies, waits for them, and re-layouts  655 us (56%)
  other arithmetic  262 us (22%)
  matrix products  92 us (8%)
  blocking collectives  76 us (6%)
  starting transfers between devices  36.8 us (3%)
  waiting for transfers between devices  26.2 us (2%)
  loops' own time  15.8 us (1%)
  between operations  14.9 us (1%)
    gather x3, local copies, waits for them, and re-layouts, disco_row(): gathered = extended[row_index[:, None], longitudes(col_shift)]  585 us
    while x57, other arithmetic  239 us
    psum x1, blocking collectives, local(): grad_weight, grad_gain = lax.psum((weight_part, gain_part), 'lat')  64.4 us
    dot_general x3, matrix products, spread_taps(): jnp.einsum('kt,kjc->tjc', basis.astype(jnp.float32), grad_mixed, precisio...  43.5 us
    dot_general x3, local copies, waits for them, and re-layouts, spread_taps(): jnp.einsum('kt,kjc->tjc', basis.astype(jnp.float32), grad_mixed, precisio...  37.4 us
  transfers between devices with their start and end apart: 8, of which 2 were waited for; matrix products, arithmetic and copies ran while one was open for 3% of the time, Pallas kernels for 0%

commit v1 on v0

v1 whole, which is shorter than its diff:
```python
import math

import jax
import jax.numpy as jnp
import numpy as np
from jax import lax
from jax.experimental import pallas as pl
from jax.experimental.pallas import tpu as pltpu
from jax.sharding import PartitionSpec as P

HALO = 1
SPAN = 16
STEP = 48
WIN = STEP + 2 * SPAN
GROUP = 8
NONE = -4096
ROOT = math.sqrt(2.0 / math.pi)
CUBE = 0.044715
F32 = jnp.float32
BF16 = jnp.bfloat16
MIB = 1 << 20
TABLE_CAP = 1 << 22


def legendre_pair(nodes, lat_count):
    before = nodes * 0.0 + 1.0
    current = nodes * 1.0
    for degree in range(2, lat_count + 1):
        following = ((2.0 * degree - 1.0) * nodes * current - (degree - 1.0) * before) / degree
        before = current
        current = following
    return (before, current)


def gauss_grid(lat_count):
    counter = np.arange(1, lat_count + 1) * 1.0
    nodes = np.cos(np.pi * (counter - 0.25) / (lat_count + 0.5))
    for sweep in range(12):
        before, current = legendre_pair(nodes, lat_count)
        slope = lat_count * (nodes * current - before) / (nodes * nodes - 1.0)
        nodes = nodes - current / slope
    before, current = legendre_pair(nodes, lat_count)
    slope = lat_count * (nodes * current - before) / (nodes * nodes - 1.0)
    weights = 2.0 / ((1.0 - nodes * nodes) * slope * slope)
    return (nodes, weights)


def diagonal_table(order_count, latitude_nodes):
    sine_values = np.sqrt(1.0 - latitude_nodes * latitude_nodes)
    orders = np.arange(order_count)
    positive = np.arange(1, order_count)
    log_steps = np.concatenate(
        [np.zeros(1), 0.5 * np.cumsum(np.log((2.0 * positive + 1.0) / (2.0 * positive)))]
    )
    log_values = (
        0.5 * np.log(0.5) + log_steps[:, None] + orders[:, None] * np.log(sine_values)[None, :]
    )
    return np.exp(log_values)


def legendre_block(orders, order_count, degrees, lat_count):
    latitude_nodes, weights = gauss_grid(lat_count)
    diagonal_start = jnp.asarray(diagonal_table(order_count, latitude_nodes), jnp.float32)[orders]
    node_row = jnp.asarray(latitude_nodes, jnp.float32)[None, :]
    order_column = orders.astype(jnp.float32)[:, None]

    def block_step(carry, block_index):
        previous, earlier = carry
        produced = []
        for offset in range(16):
            degree = (block_index * 16 + offset).astype(jnp.float32)
            squared = degree * degree
            order_squared = order_column * order_column
            forward_factor = jnp.sqrt(
                jnp.maximum(4.0 * squared - 1.0, 1.0) / jnp.maximum(squared - order_squared, 1.0)
            )
            lower = (degree - 1.0) * (degree - 1.0)
            back_factor = jnp.sqrt(
                jnp.maximum(lower - order_squared, 0.0) / jnp.maximum(4.0 * lower - 1.0, 1.0)
            )
            recurred = forward_factor * (node_row * previous - back_factor * earlier)
            fresh = jnp.where(
                degree < order_column,
                0.0,
                jnp.where(degree == order_column, diagonal_start, recurred),
            )
            earlier = previous
            previous = fresh
            produced.append(fresh)
        return ((previous, earlier), jnp.stack(produced))

    zeros = jnp.zeros((orders.shape[0], lat_count), jnp.float32)
    _, blocks = lax.scan(block_step, (zeros, zeros), jnp.arange(degrees // 16, dtype=jnp.int32))
    legendre = blocks.reshape(degrees, orders.shape[0], lat_count)
    return jnp.transpose(legendre, (1, 0, 2))


def legendre_table(order_count, degrees, lat_count):
    nodes, weights = gauss_grid(lat_count)
    start = diagonal_table(order_count, nodes).astype(np.float32)
    node_row = nodes.astype(np.float32)[None, :]
    order = np.arange(order_count, dtype=np.float32)[:, None]
    one = np.float32(1.0)
    four = np.float32(4.0)
    previous = np.zeros((order_count, lat_count), np.float32)
    earlier = previous
    produced = []
    for step in range(degrees):
        degree = np.float32(step)
        squared = degree * degree
        lower = (degree - one) * (degree - one)
        ahead = np.sqrt(
            np.maximum(four * squared - one, one) / np.maximum(squared - order * order, one)
        )
        back = np.sqrt(
            np.maximum(lower - order * order, np.float32(0.0))
            / np.maximum(four * lower - one, one)
        )
        recurred = ahead * (node_row * previous - back * earlier)
        fresh = np.where(degree < order, np.float32(0.0), np.where(degree == order, start, recurred))
        earlier = previous
        previous = fresh.astype(np.float32)
        produced.append(previous)
    legendre = np.stack(produced, axis=1)
    weighted = legendre * weights.astype(np.float32)[None, None, :]
    return (legendre.astype(BF16), weighted.astype(BF16))


def fourier_tables(lon_count, order_count, devices):
    angle = 2.0 * np.pi / lon_count * (np.outer(np.arange(lon_count), np.arange(order_count)) % lon_count)
    cosine = np.cos(angle)
    sine = np.sin(angle)
    doubled = np.where(np.arange(order_count) == 0, 1.0, 2.0)[None, :]
    owned = order_count // devices
    group = -(-2 * owned // GROUP) * GROUP

    def grouped(real, imaginary):
        pairs = np.stack([real, imaginary], axis=2).reshape(lon_count, devices, 2 * owned)
        pairs = np.pad(pairs, ((0, 0), (0, 0), (0, group - 2 * owned)))
        return pairs.reshape(lon_count, devices * group).astype(np.float32).astype(BF16)

    forward = grouped(cosine / lon_count, -sine / lon_count)
    inverse = grouped(doubled * cosine, -doubled * sine)
    return (forward, inverse)


def spectral_table(table, devices, lat_dev, group):
    orders, degrees, lats = table.shape
    owned = orders // devices
    split = np.asarray(table, np.float32).reshape(devices, owned, degrees, devices, lat_dev)
    full = np.zeros((devices, owned, 2, degrees, lat_dev, devices, group), np.float32)
    for r in range(owned):
        for p in range(2):
            full[:, r, p, :, :, :, 2 * r + p] = np.transpose(split[:, r], (0, 1, 3, 2))
    return full.reshape(devices, owned * 2 * degrees, lat_dev * devices * group).astype(BF16)


def params(limit, **kwargs):
    return pltpu.CompilerParams(vmem_limit_bytes=limit * MIB, **kwargs)


def cost(flops, nbytes):
    return pl.CostEstimate(flops=int(flops), bytes_accessed=int(nbytes), transcendentals=0)


def dot(a, b):
    return jnp.dot(a, b, preferred_element_type=F32)


def dot_t(a, b):
    return lax.dot_general(a, b, (((0,), (0,)), ((), ())), preferred_element_type=F32)


def transform(features, table):
    lat_dev, lon, channels = features.shape
    rows = table.shape[0]

    def body(x_ref, t_ref, o_ref):
        o_ref[...] = dot(t_ref[...], x_ref[0]).astype(BF16)

    return pl.pallas_call(
        body,
        grid=(lat_dev,),
        in_specs=[
            pl.BlockSpec((1, lon, channels), lambda i: (i, 0, 0)),
            pl.BlockSpec((rows, lon), lambda i: (0, 0)),
        ],
        out_specs=pl.BlockSpec((rows, channels), lambda i: (0, i)),
        out_shape=jax.ShapeDtypeStruct((rows, lat_dev * channels), BF16),
        compiler_params=params(24),
        cost_estimate=cost(2 * rows * lon * channels * lat_dev, features.size * 2),
        name="transform",
    )(features, table)


def filtered(middle, north, south, shifts, taps, weights, keep):
    lat_dev, lon, channels = middle.shape
    kernels = taps.shape[0]
    count = taps.shape[2]
    wide = kernels * channels
    per = 5
    chunk = per * STEP
    rows = lat_dev + 2

    def body(shift_ref, tap_ref, mid_ref, north_ref, south_ref, w_ref, *rest):
        if keep:
            mixed_ref, out_ref, ext, sem = rest
        else:
            out_ref, mixed_ref, ext, sem = rest
        row = pl.program_id(0)

        def copies():
            made = []
            for e in range(rows):
                src = north_ref.at[0] if e == 0 else (south_ref.at[0] if e == rows - 1 else mid_ref.at[e - 1])
                for a, b, n in ((0, SPAN, lon), (lon - SPAN, 0, SPAN), (0, lon + SPAN, SPAN)):
                    made.append(
                        pltpu.make_async_copy(
                            src.at[pl.ds(a, n)], ext.at[e, pl.ds(b, n)], sem.at[len(made)]
                        )
                    )
            return made

        @pl.when(row == 0)
        def _():
            for copy in copies():
                copy.start()

        across = lax.broadcasted_iota(jnp.int32, (STEP, 3 * WIN), 1)
        down = lax.broadcasted_iota(jnp.int32, (STEP, 3 * WIN), 0)
        delta = across - down
        band = [jnp.zeros((STEP, 3 * WIN), F32) for _ in range(kernels)]
        for t in range(count):
            hit = delta == shift_ref[row, t]
            for k in range(kernels):
                band[k] = band[k] + jnp.where(hit, tap_ref[k, row, t], 0.0)
        band = jnp.concatenate(band, axis=0).astype(BF16)

        @pl.when(row == 0)
        def _():
            for copy in copies():
                copy.wait()

        def step(c, carry):
            for b in range(per):
                start = pl.multiple_of(c * chunk + b * STEP, STEP)
                window = jnp.concatenate(
                    [ext[row + e, pl.ds(start, WIN), :] for e in range(3)], axis=0
                )
                sums = dot(band, window).astype(BF16)
                for k in range(kernels):
                    place = (pl.ds(start, STEP), pl.ds(k * channels, channels))
                    if keep:
                        mixed_ref[(0,) + place] = sums[k * STEP : (k + 1) * STEP]
                    else:
                        mixed_ref[pl.ds(b * STEP, STEP), pl.ds(k * channels, channels)] = sums[
                            k * STEP : (k + 1) * STEP
                        ]
            start = pl.multiple_of(c * chunk, chunk)
            if keep:
                block = mixed_ref[0, pl.ds(start, chunk), :]
            else:
                block = mixed_ref[...]
            out_ref[0, pl.ds(start, chunk), :] = dot(block, w_ref[...])
            return carry

        lax.fori_loop(0, lon // chunk, step, 0)

    out_specs = [pl.BlockSpec((1, lon, channels), lambda i: (i, 0, 0))]
    out_shape = [jax.ShapeDtypeStruct((lat_dev, lon, channels), F32)]
    scratch = []
    if keep:
        out_specs.insert(0, pl.BlockSpec((1, lon, wide), lambda i: (i, 0, 0)))
        out_shape.insert(0, jax.ShapeDtypeStruct((lat_dev, lon, wide), BF16))
    else:
        scratch.append(pltpu.VMEM((chunk, wide), BF16))
    result = pl.pallas_call(
        body,
        grid=(lat_dev,),
        in_specs=[
            pl.BlockSpec(memory_space=pltpu.SMEM),
            pl.BlockSpec(memory_space=pltpu.SMEM),
            pl.BlockSpec(memory_space=pl.ANY),
            pl.BlockSpec(memory_space=pl.ANY),
            pl.BlockSpec(memory_space=pl.ANY),
            pl.BlockSpec((wide, channels), lambda i: (0, 0)),
        ],
        out_specs=out_specs,
        out_shape=out_shape,
        scratch_shapes=scratch
        + [pltpu.VMEM((rows, lon + 2 * SPAN, channels), BF16), pltpu.SemaphoreType.DMA((3 * rows,))],
        compiler_params=params(32),
        cost_estimate=cost(
            2 * lat_dev * lon * channels * (3 * wide + 3 * WIN * kernels), middle.size * 10
        ),
        name="filtered",
    )(shifts, taps, middle, north, south, weights)
    return result if keep else result[0]


def spectral_forward(position, owned, table_in, table_out, gain):
    group_rows, width = owned.shape
    _, rows, depth = table_in.shape
    degrees, channels = gain.shape
    lat_dev = width // channels

    def body(p_ref, x_ref, a_ref, b_ref, g_ref, analysed_ref, o_ref):
        analysed = jnp.zeros((rows, channels), F32)
        for i in range(lat_dev):
            analysed = analysed + dot(
                a_ref[0, :, i * group_rows : (i + 1) * group_rows],
                x_ref[:, i * channels : (i + 1) * channels],
            )
        analysed_ref[...] = analysed
        gain_rows = jnp.concatenate([g_ref[...]] * (rows // degrees), axis=0)
        scaled = (analysed * gain_rows).astype(BF16)
        for i in range(lat_dev):
            o_ref[:, i * channels : (i + 1) * channels] = dot_t(
                b_ref[0, :, i * group_rows : (i + 1) * group_rows], scaled
            ).astype(BF16)

    table_spec = pl.BlockSpec((1, rows, depth), lambda g, p: (p[0], 0, 0))
    return pl.pallas_call(
        body,
        grid_spec=pltpu.PrefetchScalarGridSpec(
            num_scalar_prefetch=1,
            grid=(1,),
            in_specs=[
                pl.BlockSpec((group_rows, width), lambda g, p: (0, 0)),
                table_spec,
                table_spec,
                pl.BlockSpec((degrees, channels), lambda g, p: (0, 0)),
            ],
            out_specs=[
                pl.BlockSpec((rows, channels), lambda g, p: (0, 0)),
                pl.BlockSpec((group_rows, width), lambda g, p: (0, 0)),
            ],
        ),
        out_shape=[
            jax.ShapeDtypeStruct((rows, channels), F32),
            jax.ShapeDtypeStruct((group_rows, width), BF16),
        ],
        compiler_params=params(16),
        name="spectral_forward",
    )(position, owned, table_in, table_out, gain)


def spectral_adjoint(position, owned, table_in, table_out, gain, analysed):
    group_rows, width = owned.shape
    _, rows, depth = table_in.shape
    degrees, channels = gain.shape
    lat_dev = width // channels

    def body(p_ref, x_ref, b_ref, a_ref, g_ref, analysed_ref, gain_ref, o_ref):
        scaled = jnp.zeros((rows, channels), F32)
        for i in range(lat_dev):
            scaled = scaled + dot(
                b_ref[0, :, i * group_rows : (i + 1) * group_rows],
                x_ref[:, i * channels : (i + 1) * channels],
            )
        terms = analysed_ref[...] * scaled
        total = jnp.zeros((degrees, channels), F32)
        for s in range(rows // degrees):
            total = total + terms[s * degrees : (s + 1) * degrees]
        gain_ref[...] = total
        gain_rows = jnp.concatenate([g_ref[...]] * (rows // degrees), axis=0)
        grad = (gain_rows * scaled).astype(BF16)
        for i in range(lat_dev):
            o_ref[:, i * channels : (i + 1) * channels] = dot_t(
                a_ref[0, :, i * group_rows : (i + 1) * group_rows], grad
            ).astype(BF16)

    table_spec = pl.BlockSpec((1, rows, depth), lambda g, p: (p[0], 0, 0))
    return pl.pallas_call(
        body,
        grid_spec=pltpu.PrefetchScalarGridSpec(
            num_scalar_prefetch=1,
            grid=(1,),
            in_specs=[
                pl.BlockSpec((group_rows, width), lambda g, p: (0, 0)),
                table_spec,
                table_spec,
                pl.BlockSpec((degrees, channels), lambda g, p: (0, 0)),
                pl.BlockSpec((rows, channels), lambda g, p: (0, 0)),
            ],
            out_specs=[
                pl.BlockSpec((degrees, channels), lambda g, p: (0, 0)),
                pl.BlockSpec((group_rows, width), lambda g, p: (0, 0)),
            ],
        ),
        out_shape=[
            jax.ShapeDtypeStruct((degrees, channels), F32),
            jax.ShapeDtypeStruct((group_rows, width), BF16),
        ],
        compiler_params=params(16),
        name="spectral_adjoint",
    )(position, owned, table_in, table_out, gain, analysed)


def activation(disco, returned, grad_output, inverse, inverse_t):
    lat_dev, lon, channels = disco.shape
    group_rows = returned.shape[0]
    chunk = 240

    def body(d_ref, y_ref, g_ref, inv_ref, invt_ref, o_ref, gt_ref, x_ref):
        def step(c, carry):
            place = pl.ds(pl.multiple_of(c * chunk, chunk), chunk)
            total = d_ref[0, place, :] + dot(inv_ref[place, :], y_ref[...])
            square = total * total
            half = 0.5 + 0.5 * jnp.tanh(total * (ROOT + ROOT * CUBE * square))
            value = total * half
            slope = half + value * (1.0 - half) * (2.0 * ROOT + 6.0 * ROOT * CUBE * square)
            o_ref[0, place, :] = value.astype(BF16)
            gt_ref[0, place, :] = (g_ref[0, place, :].astype(F32) * slope).astype(BF16)
            return carry

        lax.fori_loop(0, lon // chunk, step, 0)
        x_ref[...] = dot(invt_ref[...], gt_ref[0]).astype(BF16)

    row_spec = pl.BlockSpec((1, lon, channels), lambda i: (i, 0, 0))
    column_spec = pl.BlockSpec((group_rows, channels), lambda i: (0, i))
    return pl.pallas_call(
        body,
        grid=(lat_dev,),
        in_specs=[
            row_spec,
            column_spec,
            row_spec,
            pl.BlockSpec((lon, group_rows), lambda i: (0, 0)),
            pl.BlockSpec((group_rows, lon), lambda i: (0, 0)),
        ],
        out_specs=[row_spec, row_spec, column_spec],
        out_shape=[
            jax.ShapeDtypeStruct((lat_dev, lon, channels), BF16),
            jax.ShapeDtypeStruct((lat_dev, lon, channels), BF16),
            jax.ShapeDtypeStruct((group_rows, lat_dev * channels), BF16),
        ],
        compiler_params=params(32),
        cost_estimate=cost(4 * disco.size * group_rows, disco.size * 10),
        name="activation",
    )(disco, returned, grad_output, inverse, inverse_t)


def weight_terms(mixed, grad_total):
    lat_dev, lon, wide = mixed.shape
    channels = grad_total.shape[2]

    def body(m_ref, g_ref, o_ref, acc):
        row = pl.program_id(0)
        part = dot(jnp.transpose(g_ref[0]), m_ref[0])

        @pl.when(row == 0)
        def _():
            acc[...] = part

        @pl.when(row > 0)
        def _():
            acc[...] += part

        @pl.when(row == lat_dev - 1)
        def _():
            o_ref[...] = jnp.transpose(acc[...]).astype(BF16)

    return pl.pallas_call(
        body,
        grid=(lat_dev,),
        in_specs=[
            pl.BlockSpec((1, lon, wide), lambda i: (i, 0, 0)),
            pl.BlockSpec((1, lon, channels), lambda i: (i, 0, 0)),
        ],
        out_specs=pl.BlockSpec((wide, channels), lambda i: (0, 0)),
        out_shape=jax.ShapeDtypeStruct((wide, channels), BF16),
        scratch_shapes=[pltpu.VMEM((channels, wide), F32)],
        compiler_params=params(32),
        cost_estimate=cost(2 * mixed.size * channels, mixed.size * 2),
        name="weight_terms",
    )(mixed, grad_total)


def final(bands, forward, grad_disco):
    lat_dev, lon, channels = grad_disco.shape
    group_rows = bands.shape[0]

    def body(y_ref, f_ref, d_ref, o_ref):
        o_ref[0] = (d_ref[0] + dot(f_ref[...], y_ref[...])).astype(BF16)

    row_spec = pl.BlockSpec((1, lon, channels), lambda i: (i, 0, 0))
    return pl.pallas_call(
        body,
        grid=(lat_dev,),
        in_specs=[
            pl.BlockSpec((group_rows, channels), lambda i: (0, i)),
            pl.BlockSpec((lon, group_rows), lambda i: (0, 0)),
            row_spec,
        ],
        out_specs=row_spec,
        out_shape=jax.ShapeDtypeStruct((lat_dev, lon, channels), BF16),
        compiler_params=params(24),
        cost_estimate=cost(2 * grad_disco.size * group_rows, grad_disco.size * 6),
        name="final",
    )(bands, forward, grad_disco)


def stages(count):
    found = []
    stride = 1
    while stride < count:
        factor = 4 if (count // stride) % 4 == 0 else 2
        found.append((stride, factor))
        stride *= factor
    return found


def partner(array, count, stride, by):
    return lax.ppermute(array, "lat", [(i, i ^ (by * stride)) for i in range(count)])


def sum_scatter_gather(array):
    count = lax.axis_size("lat")
    position = lax.axis_index("lat")
    plan = stages(count)
    for stride, factor in plan:
        digit = (position // stride) % factor
        pieces = array.reshape(factor, array.shape[0] // factor, array.shape[1])
        total = lax.dynamic_index_in_dim(pieces, digit, 0, False).astype(F32)
        for by in range(1, factor):
            piece = lax.dynamic_index_in_dim(pieces, digit ^ by, 0, False)
            total = total + partner(piece, count, stride, by).astype(F32)
        array = total.astype(BF16)
    for stride, factor in reversed(plan):
        digit = (position // stride) % factor
        whole = jnp.zeros((factor,) + array.shape, BF16)
        for by in range(factor):
            part = partner(array, count, stride, by) if by else array
            whole = lax.dynamic_update_index_in_dim(whole, part, digit ^ by, 0)
        array = whole.reshape(-1, array.shape[1])
    return array


def sum_everywhere(array):
    count = lax.axis_size("lat")
    for stride, factor in stages(count):
        parts = [array] + [partner(array, count, stride, by) for by in range(1, factor)]
        while len(parts) > 1:
            parts = [parts[k] + parts[k + 1] for k in range(0, len(parts), 2)]
        array = parts[0]
    return array


def neighbours(north_edge, south_edge):
    count = lax.axis_size("lat")
    from_north = lax.ppermute(south_edge, "lat", [(i, i + 1) for i in range(count - 1)])
    from_south = lax.ppermute(north_edge, "lat", [(i + 1, i) for i in range(count - 1)])
    return (from_north, from_south)


def exchange(array):
    count = lax.axis_size("lat")
    rows, width = array.shape
    blocks = array.reshape(count, rows // count, width)
    blocks = lax.all_to_all(blocks, "lat", split_axis=0, concat_axis=0, tiled=True)
    return blocks.reshape(rows, width)


def local(features, disco_rows, disco_cols, disco_basis, disco_weight, spectral_gain, grad_output):
    lat_dev, lon, channels = features.shape
    devices = lax.axis_size("lat")
    position = lax.axis_index("lat")
    degrees = spectral_gain.shape[0]
    lat_count = lat_dev * devices
    order_count = lat_count
    owned_orders = order_count // devices
    kernels, _, taps = disco_basis.shape
    forward, inverse = fourier_tables(lon, order_count, devices)
    group = forward.shape[1] // devices
    forward_t = jnp.asarray(np.ascontiguousarray(forward.T))
    inverse_t = jnp.asarray(np.ascontiguousarray(inverse.T))
    forward = jnp.asarray(forward)
    inverse = jnp.asarray(inverse)
    place = position.astype(jnp.int32).reshape(1)
    small = order_count * owned_orders * 2 * degrees * lat_dev * devices * group <= TABLE_CAP * 4

    north, south = neighbours(features[:HALO], features[lat_dev - HALO :])
    coefficients = transform(features, forward_t)
    owned = exchange(coefficients)

    packed = jnp.concatenate(
        [
            disco_rows.astype(F32)[:, None, :],
            disco_cols.astype(F32)[:, None, :],
            jnp.transpose(disco_basis, (1, 0, 2)).astype(F32),
        ],
        axis=1,
    )
    packed_north, packed_south = neighbours(packed[:HALO], packed[lat_dev - HALO :])
    packed_all = jnp.concatenate([packed_north, packed, packed_south], axis=0)
    band_rows = position * lat_dev + jnp.arange(lat_dev, dtype=jnp.int32)[:, None]
    shifts = (disco_rows - band_rows + 1) * WIN + SPAN + disco_cols
    rows_all = packed_all[:, 0].astype(jnp.int32)
    cols_all = packed_all[:, 1].astype(jnp.int32)
    back_shifts = []
    back_taps = []
    for e in range(3):
        aimed = rows_all[e : e + lat_dev] == band_rows
        back_shifts.append(jnp.where(aimed, e * WIN + SPAN - cols_all[e : e + lat_dev], NONE))
        back_taps.append(jnp.transpose(packed_all[e : e + lat_dev, 2:], (1, 0, 2)))
    back_shifts = jnp.concatenate(back_shifts, axis=1)
    back_taps = jnp.concatenate(back_taps, axis=2)
    weight_rows = disco_weight.reshape(kernels * channels, channels)
    weight_back = jnp.transpose(disco_weight, (0, 2, 1)).reshape(kernels * channels, channels)

    mixed, disco = filtered(
        features, north, south, shifts, disco_basis.astype(F32), weight_rows, True
    )

    if small:
        plain, weighted = legendre_table(order_count, degrees, lat_count)
        plain = jnp.asarray(spectral_table(plain, devices, lat_dev, group))
        weighted = jnp.asarray(spectral_table(weighted, devices, lat_dev, group))
        analysed, synthesized = spectral_forward(place, owned, weighted, plain, spectral_gain)
    else:
        _, gauss_weights = gauss_grid(lat_count)
        orders = position * owned_orders + jnp.arange(owned_orders, dtype=jnp.int32)
        legendre = legendre_block(orders, order_count, degrees, lat_count)
        plain = legendre.astype(BF16).reshape(owned_orders, degrees, devices, lat_dev)
        weighted = (legendre * jnp.asarray(gauss_weights, F32)[None, None, :]).astype(BF16)
        weighted = weighted.reshape(owned_orders, degrees, devices, lat_dev)

        def opened(array):
            array = array.reshape(devices, group, lat_dev, channels)[:, : 2 * owned_orders]
            return array.reshape(devices, owned_orders, 2, lat_dev, channels)

        def closed(array):
            array = array.reshape(devices, 2 * owned_orders, lat_dev * channels)
            array = jnp.pad(array, ((0, 0), (0, group - 2 * owned_orders), (0, 0)))
            return array.reshape(devices * group, lat_dev * channels).astype(BF16)

        analysed = jnp.einsum(
            "rlsi,srpic->rplc", weighted, opened(owned), preferred_element_type=F32
        )
        scaled = (analysed * spectral_gain).astype(BF16)
        synthesized = closed(
            jnp.einsum("rlsi,rplc->srpic", plain, scaled, preferred_element_type=F32)
        )

    returned = exchange(synthesized)
    output, grad_total, grad_synth = activation(disco, returned, grad_output, inverse, inverse_t)
    grad_owned = exchange(grad_synth)
    grad_north, grad_south = neighbours(grad_total[:HALO], grad_total[lat_dev - HALO :])
    weight_part = weight_terms(mixed, grad_total)

    if small:
        gain_part, grad_coeff = spectral_adjoint(
            place, grad_owned, plain, weighted, spectral_gain, analysed
        )
    else:
        grad_scaled = jnp.einsum(
            "rlsi,srpic->rplc", plain, opened(grad_owned), preferred_element_type=F32
        )
        gain_part = jnp.sum(analysed * grad_scaled, axis=(0, 1))
        grad_analysed = (grad_scaled * spectral_gain).astype(BF16)
        grad_coeff = closed(
            jnp.einsum("rlsi,rplc->srpic", weighted, grad_analysed, preferred_element_type=F32)
        )

    grad_bands = exchange(grad_coeff)
    grad_disco = filtered(
        grad_total, grad_north, grad_south, back_shifts, back_taps, weight_back, False
    )
    grad_features = final(grad_bands, forward, grad_disco)
    grad_weight = sum_scatter_gather(weight_part).astype(F32)
    grad_gain = sum_everywhere(gain_part)
    return (
        output,
        grad_features,
        grad_weight.reshape(kernels, channels, channels),
        grad_gain,
    )


def solution(mesh):
    return jax.shard_map(
        local,
        mesh=mesh,
        in_specs=(
            P(("group", "lat"), None, None),
            P("lat", None),
            P("lat", None),
            P(None, "lat", None),
            P(),
            P(),
            P(("group", "lat"), None, None),
        ),
        out_specs=(
            P(("group", "lat"), None, None),
            P(("group", "lat"), None, None),
            P("group", None, None),
            P("group", None),
        ),
        check_vma=False,
    )
```

time: 1180 us -> 174 us (0.15)
  local copies, waits for them, and re-layouts: 655 us -> 42.4 us
  other arithmetic: 262 us -> 8.31 us
  matrix products: 92 us -> 0 us
  blocking collectives: 76 us -> 0 us
  Pallas kernels: 0 us -> 43 us
  starting transfers between devices: 36.8 us -> 57.9 us
  loops' own time: 15.8 us -> 0 us
  between operations: 14.9 us -> 1.14 us
    gather x4 -> x0, local copies, waits for them, and re-layouts: 586 us -> none  [the longest x3 585 us: disco_row(): gathered = extended[row_index[:, None], longitudes(col_shift)]]
    while x57 -> x0, other arithmetic: 239 us -> none
    dot_general x23 -> x0, matrix products: 92 us -> none  [the longest x3 43.5 us: spread_taps(): jnp.einsum('kt,kjc->tjc', basis.astype(jnp.float32), grad_mixed, precisio...]
    psum x1 -> x0, blocking collectives: 64.4 us -> none  [local(): grad_weight, grad_gain = lax.psum((weight_part, gain_part), 'lat')]
    pallas_call x0 -> x8, Pallas kernels: none -> 43 us  [the longest x2 25.1 us: filtered(): pl.pallas_call(body, grid=(lat_dev,), in_specs=[pl.BlockSpec(memory_space...]
    dot_general x3 -> x0, local copies, waits for them, and re-layouts: 37.4 us -> none  [spread_taps(): jnp.einsum('kt,kjc->tjc', basis.astype(jnp.float32), grad_mixed, precisio...]
    unnamed x48 -> x74, local copies, waits for them, and re-layouts: 2.87 us -> 28.2 us
    ppermute x4 -> x24, starting transfers between devices: 8.15 us -> 32.8 us  [the longest x18 19.4 us: partner(): lax.ppermute(array, 'lat', [(i, i ^ by * stride) for i in range(count)])]
  transfers between devices with their start and end apart: 8 -> 28, of which waited for: 2 -> 9; matrix products, arithmetic and copies ran while one was open for 3% -> 11% of each run, Pallas kernels for 0% -> 17%
where the time goes in v1:
time: 174 us; the launch traced here: 172 us
  starting transfers between devices  57.9 us (33%)
  Pallas kernels  43 us (25%)
  local copies, waits for them, and re-layouts  42.4 us (24%)
  waiting for transfers between devices  19.7 us (11%)
  other arithmetic  8.31 us (5%)
    unnamed x74, local copies, waits for them, and re-layouts  28.2 us
    all_to_all x4, starting transfers between devices, exchange(): lax.all_to_all(blocks, 'lat', split_axis=0, concat_axis=0, tiled=True)  25.1 us
    pallas_call x2, Pallas kernels, filtered(): pl.pallas_call(body, grid=(lat_dev,), in_specs=[pl.BlockSpec(memory_space...  25.1 us
    ppermute x18, starting transfers between devices, partner(): lax.ppermute(array, 'lat', [(i, i ^ by * stride) for i in range(count)])  19.4 us
    ppermute x18, waiting for transfers between devices, partner(): lax.ppermute(array, 'lat', [(i, i ^ by * stride) for i in range(count)])  19 us
    ppermute x3, starting transfers between devices, neighbours(): lax.ppermute(south_edge, 'lat', [(i, i + 1) for i in range(count - 1)])  9.51 us
    pallas_call x1, Pallas kernels, activation(): pl.pallas_call(body, grid=(lat_dev,), in_specs=[row_spec, column_spec, ro...  7.71 us
    dynamic_update_slice x7, local copies, waits for them, and re-layouts, sum_scatter_gather(): whole = lax.dynamic_update_index_in_dim(whole, part, digit ^ by, 0)  6.9 us
  transfers between devices with their start and end apart: 28, of which 9 were waited for; matrix products, arithmetic and copies ran while one was open for 11% of the time, Pallas kernels for 17%

profile of v1, /device:TPU:0, one launch (start us, length us, event | category | flops | bytes accessed | tf_op | source)
XLA Modules:
  0.0 172.5 jit_solution(16491612926548072775)
XLA Ops:
  0.7 2.7 %fusion.11 = (bf16[1,1440,256]{2,1,0:T(8,128)(2,1)}, bf16[1,1440,256]{2,1,0:T(8,128)(2,1)}) fusion(bf16[3,1440,256]{2,1,0:T(8,128)(2,1)} %x_ref.1), kind=kLoop, calls=%fused_computation.55 | loop fusion | bytes 2949120 | tf_op jit(solution)/shard_map/slice | solution.py:583
  3.4 3.5 %collective-permute-start = (bf16[1,1440,256]{2,1,0:T(8,128)(2,1)}, bf16[1,1440,256]{2,1,0:T(8,128)(2,1)}, u32[]{:S(2)}, u32[]{:S(2)}) collective-permute-start(bf16[1,1440,256]{2,1,0:T(8,128)(2,1)} %get-tuple-element.27), channel_id=1, source_target_pairs={{0,1},{1,2},{2,3},{3,4},{4,5},{5,6},{6,7},{7,8},{8,9},{9,10},{10,1... | collective-permute-start | bytes 2211848 | tf_op jit(solution)/shard_map/ppermute | solution.py:552
  9.8 8.4 %all-to-all-start = ((bf16[16,8,768]{2,1,0:T(8,128)(2,1)}), bf16[16,8,768]{2,1,0:T(8,128)(2,1)}, u32[]{:S(2)}, u32[]{:S(2)}) async-start(bf16[16,8,768]{2,1,0:T(8,128)(2,1)} %bitcast.83), calls=%async_computation | async-start | bytes 393216 | tf_op jit(solution)/shard_map/all_to_all | solution.py:561
  19.8 2.8 %collective-permute-start.2 = (f32[1,5,9]{2,0,1:T(1,128)}, f32[1,5,9]{2,0,1:T(1,128)}, u32[]{:S(2)}, u32[]{:S(2)}) collective-permute-start(f32[1,5,9]{2,0,1:T(1,128)} %get-tuple-element.38), channel_id=1, source_target_pairs={{0,1},{1,2},{2,3},{3,4},{4,5},{5,6},{6,7},{7,8},{8,9},{9,10},{10,1... | collective-permute-start | bytes 548 | tf_op jit(solution)/shard_map/ppermute | solution.py:552
  24.0 1.9 %copy.17 = bf16[3,256,256]{2,1,0:T(8,128)(2,1)} copy(bf16[3,256,256]{1,2,0:T(8,128)(2,1)} %bitcast.84) | data formatting | bytes 786432 | tf_op jit(solution)/shard_map/transpose | solution.py:610
  30.0 2.0 %copy-done.1 = bf16[16,288,384]{2,1,0:T(8,128)(2,1)S(1)} copy-done((bf16[16,288,384]{2,1,0:T(8,128)(2,1)S(1)}, bf16[16,288,384]{2,1,0:T(8,128)(2,1)}, u32[]{:S(2)}) %copy-start.1) | copy-done | bytes 3538968
  35.8 7.5 %all-to-all-start.1 = ((bf16[16,8,768]{2,1,0:T(8,128)(2,1)}), bf16[16,8,768]{2,1,0:T(8,128)(2,1)}, u32[]{:S(2)}, u32[]{:S(2)}) async-start(bf16[16,8,768]{2,1,0:T(8,128)(2,1)} %bitcast.89), calls=%async_computation.1 | async-start | bytes 393216 | tf_op jit(solution)/shard_map/all_to_all | solution.py:561
  46.0 13.0 %filtered.2 = (bf16[3,1440,768]{2,1,0:T(8,128)(2,1)S(1)}, f32[3,1440,256]{2,1,0:T(8,128)S(1)}) custom-call(s32[3,9]{1,0:T(4,128)S(1)} %get-tuple-element.46.shift_ref, f32[3,3,9]{2,1,0:T(4,128)S(1)} %get-tuple-element.44.tap_ref, bf16[3,1440,256]{2,1,0:T(8,128)(2,1)S(1)} %copy-done.6, bf16[1,1440,256]{2,1,0:T(8,128)(2,1)} %collective-permute-done.north_ref, ...), custom_call_target="tpu_custom_call" | custom-call | flops 6688604160 | bytes 11059200 | tf_op jit(solution)/shard_map/filtered/pallas_call | solution.py:277
  59.0 2.7 %copy-done.3 = bf16[3,1440,768]{2,1,0:T(8,128)(2,1)} copy-done((bf16[3,1440,768]{2,1,0:T(8,128)(2,1)}, bf16[3,1440,768]{2,1,0:T(8,128)(2,1)S(1)}, u32[]{:S(2)}) %copy-start.3) | copy-done | bytes 6635544
  61.6 2.1 %copy-done.9 = f32[3,1440,256]{2,1,0:T(8,128)} copy-done((f32[3,1440,256]{2,1,0:T(8,128)}, f32[3,1440,256]{2,1,0:T(8,128)S(1)}, u32[]{:S(2)}) %copy-start.9) | copy-done | bytes 4423704
  63.7 2.3 %copy-done.10 = f32[3,1440,256]{2,1,0:T(8,128)S(1)} copy-done((f32[3,1440,256]{2,1,0:T(8,128)S(1)}, f32[3,1440,256]{2,1,0:T(8,128)}, u32[]{:S(2)}) %copy-start.10) | copy-done | bytes 4423704
  66.0 1.6 copy-done.13
  69.6 7.7 %activation.1 = (bf16[3,1440,256]{2,1,0:T(8,128)(2,1)}, bf16[3,1440,256]{2,1,0:T(8,128)(2,1)S(1)}, bf16[128,768]{1,0:T(8,128)(2,1)S(1)}) custom-call(f32[3,1440,256]{2,1,0:T(8,128)S(1)} %copy-done.10, bf16[128,768]{1,0:T(8,128)(2,1)} %bitcast.5.y_ref, bf16[3,1440,256]{2,1,0:T(8,128)(2,1)S(1)} %copy-done.13, bf16[1440,128]{1,0:T(8,128)(2,1)S(1)} %copy-done.20, ...), custom_call_target="tpu_custom_call" | custom-call | flops 566231040 | bytes 11059200 | tf_op jit(solution)/shard_map/activation/pallas_call | solution.py:422
  77.3 2.9 %weight_terms.1 = bf16[768,256]{1,0:T(8,128)(2,1)S(1)} custom-call(bf16[3,1440,768]{2,1,0:T(8,128)(2,1)S(1)} %copy-done.4, bf16[3,1440,256]{2,1,0:T(8,128)(2,1)S(1)} %get-tuple-element.19.mid_ref.g_ref), custom_call_target="tpu_custom_call" | custom-call | flops 1698693120 | bytes 6635520 | tf_op jit(solution)/shard_map/weight_terms/pallas_call | solution.py:464
  80.7 1.7 collective-permute-start.7
  82.5 3.5 %collective-permute-done.7 = bf16[192,256]{1,0:T(8,128)(2,1)S(1)} collective-permute-done((bf16[192,256]{1,0:T(8,128)(2,1)S(1)}, bf16[192,256]{1,0:T(8,128)(2,1)S(1)}, u32[]{:S(2)}, u32[]{:S(2)}) %collective-permute-start.7) | collective-permute-done | bytes 98336 | tf_op jit(solution)/shard_map/ppermute | solution.py:515
  87.6 2.5 %collective-permute-start.10 = (bf16[48,256]{1,0:T(8,128)(2,1)S(1)}, bf16[48,256]{1,0:T(8,128)(2,1)S(1)}, u32[]{:S(2)}, u32[]{:S(2)}) collective-permute-start(bf16[48,256]{1,0:T(8,128)(2,1)S(1)} %get-tuple-element.33), channel_id=1, source_target_pairs={{0,8},{1,9},{2,10},{3,11},{4,12},{5,13},{6,14},{7,15},{8,0},{9,1},... | collective-permute-start | bytes 73736 | tf_op jit(solution)/shard_map/ppermute | solution.py:515
  92.4 3.3 %collective-permute-done.11 = bf16[48,256]{1,0:T(8,128)(2,1)S(1)} collective-permute-done((bf16[48,256]{1,0:T(8,128)(2,1)S(1)}, bf16[48,256]{1,0:T(8,128)(2,1)S(1)}, u32[]{:S(2)}, u32[]{:S(2)}) %collective-permute-start.11) | collective-permute-done | bytes 24608 | tf_op jit(solution)/shard_map/ppermute | solution.py:515
  98.2 4.9 %all-to-all-start.2 = ((bf16[16,8,768]{2,1,0:T(8,128)(2,1)}), bf16[16,8,768]{2,1,0:T(8,128)(2,1)}, u32[]{:S(2)}, u32[]{:S(2)}) async-start(bf16[16,8,768]{2,1,0:T(8,128)(2,1)} %bitcast.87), calls=%async_computation.2 | async-start | bytes 393216 | tf_op jit(solution)/shard_map/all_to_all | solution.py:561
  103.1 3.1 %collective-permute-start.4 = (bf16[1,1440,256]{2,1,0:T(8,128)(2,1)}, bf16[1,1440,256]{2,1,0:T(8,128)(2,1)}, u32[]{:S(2)}, u32[]{:S(2)}) collective-permute-start(bf16[1,1440,256]{2,1,0:T(8,128)(2,1)} %get-tuple-element.25), channel_id=1, source_target_pairs={{0,1},{1,2},{2,3},{3,4},{4,5},{5,6},{6,7},{7,8},{8,9},{9,10},{10,1... | collective-permute-start | bytes 2211848 | tf_op jit(solution)/shard_map/ppermute | solution.py:552
  107.5 4.9 %collective-permute-start.13 = (bf16[48,256]{1,0:T(8,128)(2,1)}, bf16[48,256]{1,0:T(8,128)(2,1)S(1)}, u32[]{:S(2)}, u32[]{:S(2)}) collective-permute-start(bf16[48,256]{1,0:T(8,128)(2,1)} %get-tuple-element.23), channel_id=1, source_target_pairs={{0,8},{1,9},{2,10},{3,11},{4,12},{5,13},{6,14},{7,15},{8,0},{9,1},... | collective-permute-start | bytes 73736 | tf_op jit(solution)/shard_map/ppermute | solution.py:515
  115.2 7.5 %collective-permute-done.13 = bf16[48,256]{1,0:T(8,128)(2,1)S(1)} collective-permute-done((bf16[48,256]{1,0:T(8,128)(2,1)}, bf16[48,256]{1,0:T(8,128)(2,1)S(1)}, u32[]{:S(2)}, u32[]{:S(2)}) %collective-permute-start.13) | collective-permute-done | bytes 24608 | tf_op jit(solution)/shard_map/ppermute | solution.py:515
  127.2 2.0 %copy-done.2 = bf16[16,288,384]{2,1,0:T(8,128)(2,1)S(1)} copy-done((bf16[16,288,384]{2,1,0:T(8,128)(2,1)S(1)}, bf16[16,288,384]{2,1,0:T(8,128)(2,1)}, u32[]{:S(2)}) %copy-start.2) | copy-done | bytes 3538968
  133.2 1.8 %collective-permute-start.19 = (f32[48,256]{1,0:T(8,128)S(1)}, f32[48,256]{1,0:T(8,128)S(1)}, u32[]{:S(2)}, u32[]{:S(2)}) collective-permute-start(f32[48,256]{1,0:T(8,128)S(1)} %get-tuple-element.21), channel_id=1, source_target_pairs={{0,2},{1,3},{2,0},{3,1},{4,6},{5,7},{6,4},{7,5},{8,10},{9,11},{10,... | collective-permute-start | bytes 147464 | tf_op jit(solution)/shard_map/ppermute | solution.py:515
  136.5 1.7 %collective-permute-start.17 = (bf16[192,256]{1,0:T(8,128)(2,1)}, bf16[192,256]{1,0:T(8,128)(2,1)S(1)}, u32[]{:S(2)}, u32[]{:S(2)}) collective-permute-start(bf16[192,256]{1,0:T(8,128)(2,1)} %bitcast.38), channel_id=1, source_target_pairs={{0,3},{1,2},{2,1},{3,0},{4,7},{5,6},{6,5},{7,4},{8,11},{9,10},{10,... | collective-permute-start | bytes 294920 | tf_op jit(solution)/shard_map/ppermute | solution.py:515
  141.3 1.9 %collective-permute-start.23 = (f32[48,256]{1,0:T(8,128)S(1)}, f32[48,256]{1,0:T(8,128)S(1)}, u32[]{:S(2)}, u32[]{:S(2)}) collective-permute-start(f32[48,256]{1,0:T(8,128)S(1)} %add_add_fusion.1), channel_id=1, source_target_pairs={{0,12},{1,13},{2,14},{3,15},{4,8},{5,9},{6,10},{7,11},{8,4},{9,5},... | collective-permute-start | bytes 147464 | tf_op jit(solution)/shard_map/ppermute | solution.py:515
  143.9 1.9 %convert.6 = f32[3,256,256]{2,1,0:T(8,128)} convert(bf16[3,256,256]{2,1,0:T(8,128)(2,1)} %bitcast.45) | non-fusion elementwise | flops 196608 | bytes 1179648 | tf_op jit(solution)/shard_map/convert_element_type | solution.py:671
  145.9 4.2 %all-to-all-start.3 = ((bf16[16,8,768]{2,1,0:T(8,128)(2,1)}), bf16[16,8,768]{2,1,0:T(8,128)(2,1)}, u32[]{:S(2)}, u32[]{:S(2)}) async-start(bf16[16,8,768]{2,1,0:T(8,128)(2,1)} %bitcast.88), calls=%async_computation.3 | async-start | bytes 393216 | tf_op jit(solution)/shard_map/all_to_all | solution.py:561
  151.8 12.1 %filtered.3.d_ref = f32[3,1440,256]{2,1,0:T(8,128)S(1)} custom-call(s32[3,27]{1,0:T(4,128)S(1)} %pad_add_fusion.shift_ref, f32[3,3,27]{2,1,0:T(4,128)S(1)} %pad_maximum_fusion.6.tap_ref, bf16[3,1440,256]{2,1,0:T(8,128)(2,1)S(1)} %copy-done.8, bf16[1,1440,256]{2,1,0:T(8,128)(2,1)} %collective-permute-done.4.north_ref, ...), custom_call_target="tpu_custom_call" | custom-call | flops 6688604160 | bytes 11059200 | tf_op jit(solution)/shard_map/filtered/pallas_call | solution.py:277
  163.9 2.1 %copy-done.11 = f32[3,1440,256]{2,1,0:T(8,128)} copy-done((f32[3,1440,256]{2,1,0:T(8,128)}, f32[3,1440,256]{2,1,0:T(8,128)S(1)}, u32[]{:S(2)}) %copy-start.11) | copy-done | bytes 4423704
  166.0 2.3 %copy-done.12 = f32[3,1440,256]{2,1,0:T(8,128)S(1)} copy-done((f32[3,1440,256]{2,1,0:T(8,128)S(1)}, f32[3,1440,256]{2,1,0:T(8,128)}, u32[]{:S(2)}) %copy-start.12) | copy-done | bytes 4423704
  169.2 3.3 %final.1 = bf16[3,1440,256]{2,1,0:T(8,128)(2,1)} custom-call(bf16[128,768]{1,0:T(8,128)(2,1)} %bitcast.9.y_ref, bf16[1440,128]{1,0:T(8,128)(2,1)S(1)} %copy-done.19, f32[3,1440,256]{2,1,0:T(8,128)S(1)} %copy-done.12), custom_call_target="tpu_custom_call" | custom-call | flops 283115520 | bytes 6635520 | tf_op jit(solution)/shard_map/final/pallas_call | solution.py:488
  (134 shorter events, 45.5 us)
Async XLA Ops:
  0.7 17.6 %copy-start.35 = (bf16[3,3,9]{2,1,0:T(4,128)(2,1)S(1)}, bf16[3,3,9]{2,1,0:T(4,128)(2,1)}, u32[]{:S(2)}) copy-start(bf16[3,3,9]{2,1,0:T(4,128)(2,1)} %param.16) | copy-start | bytes 490
  3.4 26.6 %copy-start = (bf16[16,288,384]{2,1,0:T(8,128)(2,1)S(1)}, bf16[16,288,384]{2,1,0:T(8,128)(2,1)}, u32[]{:S(2)}) copy-start(bf16[16,288,384]{2,1,0:T(8,128)(2,1)} %constant.123.clone.b_ref) | copy-start | bytes 10616836
  3.4 40.0 %collective-permute-start = (bf16[1,1440,256]{2,1,0:T(8,128)(2,1)}, bf16[1,1440,256]{2,1,0:T(8,128)(2,1)}, u32[]{:S(2)}, u32[]{:S(2)}) collective-permute-start(bf16[1,1440,256]{2,1,0:T(8,128)(2,1)} %get-tuple-element.27), channel_id=1, source_target_pairs={{0,1},{1,2},{2,3},{3,4},{4,5},{5,6},{6,7},{7,8},{8,9},{9,10},{10,1... | collective-permute-start | bytes 2211848 | tf_op jit(solution)/shard_map/ppermute | solution.py:552
  6.9 36.5 %collective-permute-start.1 = (bf16[1,1440,256]{2,1,0:T(8,128)(2,1)}, bf16[1,1440,256]{2,1,0:T(8,128)(2,1)}, u32[]{:S(2)}, u32[]{:S(2)}) collective-permute-start(bf16[1,1440,256]{2,1,0:T(8,128)(2,1)} %get-tuple-element.26), channel_id=1, source_target_pairs={{1,0},{2,1},{3,2},{4,3},{5,4},{6,5},{7,6},{8,7},{9,8},{10,9},{11,1... | collective-permute-start | bytes 2211848 | tf_op jit(solution)/shard_map/ppermute | solution.py:553
  9.8 20.2 %all-to-all-start = ((bf16[16,8,768]{2,1,0:T(8,128)(2,1)}), bf16[16,8,768]{2,1,0:T(8,128)(2,1)}, u32[]{:S(2)}, u32[]{:S(2)}) async-start(bf16[16,8,768]{2,1,0:T(8,128)(2,1)} %bitcast.83), calls=%async_computation | async-start | bytes 393216 | tf_op jit(solution)/shard_map/all_to_all | solution.py:561
  19.8 6.1 %collective-permute-start.2 = (f32[1,5,9]{2,0,1:T(1,128)}, f32[1,5,9]{2,0,1:T(1,128)}, u32[]{:S(2)}, u32[]{:S(2)}) collective-permute-start(f32[1,5,9]{2,0,1:T(1,128)} %get-tuple-element.38), channel_id=1, source_target_pairs={{0,1},{1,2},{2,3},{3,4},{4,5},{5,6},{6,7},{7,8},{8,9},{9,10},{10,1... | collective-permute-start | bytes 548 | tf_op jit(solution)/shard_map/ppermute | solution.py:552
  22.6 3.9 %collective-permute-start.3 = (f32[1,5,9]{2,0,1:T(1,128)}, f32[1,5,9]{2,0,1:T(1,128)}, u32[]{:S(2)}, u32[]{:S(2)}) collective-permute-start(f32[1,5,9]{2,0,1:T(1,128)} %get-tuple-element.39), channel_id=1, source_target_pairs={{1,0},{2,1},{3,2},{4,3},{5,4},{6,5},{7,6},{8,7},{9,8},{10,9},{11,1... | collective-permute-start | bytes 548 | tf_op jit(solution)/shard_map/ppermute | solution.py:553
  35.8 27.9 %all-to-all-start.1 = ((bf16[16,8,768]{2,1,0:T(8,128)(2,1)}), bf16[16,8,768]{2,1,0:T(8,128)(2,1)}, u32[]{:S(2)}, u32[]{:S(2)}) async-start(bf16[16,8,768]{2,1,0:T(8,128)(2,1)} %bitcast.89), calls=%async_computation.1 | async-start | bytes 393216 | tf_op jit(solution)/shard_map/all_to_all | solution.py:561
  77.3 19.7 %copy-start.7 = (bf16[3,1440,256]{2,1,0:T(8,128)(2,1)}, bf16[3,1440,256]{2,1,0:T(8,128)(2,1)S(1)}, u32[]{:S(2)}) copy-start(bf16[3,1440,256]{2,1,0:T(8,128)(2,1)S(1)} %get-tuple-element.19.mid_ref.g_ref) | copy-start | bytes 6635524
  80.3 2.2 %collective-permute-start.6 = (bf16[192,256]{1,0:T(8,128)(2,1)S(1)}, bf16[192,256]{1,0:T(8,128)(2,1)S(1)}, u32[]{:S(2)}, u32[]{:S(2)}) collective-permute-start(bf16[192,256]{1,0:T(8,128)(2,1)S(1)} %get-tuple-element.28), channel_id=1, source_target_pairs={{0,1},{1,0},{2,3},{3,2},{4,5},{5,4},{6,7},{7,6},{8,9},{9,8},{10,11... | collective-permute-start | bytes 294920 | tf_op jit(solution)/shard_map/ppermute | solution.py:515
  80.7 5.3 %collective-permute-start.7 = (bf16[192,256]{1,0:T(8,128)(2,1)S(1)}, bf16[192,256]{1,0:T(8,128)(2,1)S(1)}, u32[]{:S(2)}, u32[]{:S(2)}) collective-permute-start(bf16[192,256]{1,0:T(8,128)(2,1)S(1)} %get-tuple-element.30), channel_id=1, source_target_pairs={{0,2},{1,3},{2,0},{3,1},{4,6},{5,7},{6,4},{7,5},{8,10},{9,11},{10,... | collective-permute-start | bytes 294920 | tf_op jit(solution)/shard_map/ppermute | solution.py:515
  82.4 5.1 %collective-permute-start.8 = (bf16[192,256]{1,0:T(8,128)(2,1)S(1)}, bf16[192,256]{1,0:T(8,128)(2,1)S(1)}, u32[]{:S(2)}, u32[]{:S(2)}) collective-permute-start(bf16[192,256]{1,0:T(8,128)(2,1)S(1)} %get-tuple-element.29), channel_id=1, source_target_pairs={{0,3},{1,2},{2,1},{3,0},{4,7},{5,6},{6,5},{7,4},{8,11},{9,10},{10,... | collective-permute-start | bytes 294920 | tf_op jit(solution)/shard_map/ppermute | solution.py:515
  87.6 4.8 %collective-permute-start.10 = (bf16[48,256]{1,0:T(8,128)(2,1)S(1)}, bf16[48,256]{1,0:T(8,128)(2,1)S(1)}, u32[]{:S(2)}, u32[]{:S(2)}) collective-permute-start(bf16[48,256]{1,0:T(8,128)(2,1)S(1)} %get-tuple-element.33), channel_id=1, source_target_pairs={{0,8},{1,9},{2,10},{3,11},{4,12},{5,13},{6,14},{7,15},{8,0},{9,1},... | collective-permute-start | bytes 73736 | tf_op jit(solution)/shard_map/ppermute | solution.py:515
  90.0 5.6 %collective-permute-start.11 = (bf16[48,256]{1,0:T(8,128)(2,1)S(1)}, bf16[48,256]{1,0:T(8,128)(2,1)S(1)}, u32[]{:S(2)}, u32[]{:S(2)}) collective-permute-start(bf16[48,256]{1,0:T(8,128)(2,1)S(1)} %get-tuple-element.32), channel_id=1, source_target_pairs={{0,12},{1,13},{2,14},{3,15},{4,8},{5,9},{6,10},{7,11},{8,4},{9,5},... | collective-permute-start | bytes 73736 | tf_op jit(solution)/shard_map/ppermute | solution.py:515
  91.5 4.2 %collective-permute-start.9 = (bf16[48,256]{1,0:T(8,128)(2,1)S(1)}, bf16[48,256]{1,0:T(8,128)(2,1)S(1)}, u32[]{:S(2)}, u32[]{:S(2)}) collective-permute-start(bf16[48,256]{1,0:T(8,128)(2,1)S(1)} %get-tuple-element.31), channel_id=1, source_target_pairs={{0,4},{1,5},{2,6},{3,7},{4,0},{5,1},{6,2},{7,3},{8,12},{9,13},{10,... | collective-permute-start | bytes 73736 | tf_op jit(solution)/shard_map/ppermute | solution.py:515
  96.9 16.9 %collective-permute-start.12 = (bf16[48,256]{1,0:T(8,128)(2,1)}, bf16[48,256]{1,0:T(8,128)(2,1)}, u32[]{:S(2)}, u32[]{:S(2)}) collective-permute-start(bf16[48,256]{1,0:T(8,128)(2,1)} %get-tuple-element.23), channel_id=1, source_target_pairs={{0,4},{1,5},{2,6},{3,7},{4,0},{5,1},{6,2},{7,3},{8,12},{9,13},{10,... | collective-permute-start | bytes 73736 | tf_op jit(solution)/shard_map/ppermute | solution.py:515
  98.2 29.0 %all-to-all-start.2 = ((bf16[16,8,768]{2,1,0:T(8,128)(2,1)}), bf16[16,8,768]{2,1,0:T(8,128)(2,1)}, u32[]{:S(2)}, u32[]{:S(2)}) async-start(bf16[16,8,768]{2,1,0:T(8,128)(2,1)} %bitcast.87), calls=%async_computation.2 | async-start | bytes 393216 | tf_op jit(solution)/shard_map/all_to_all | solution.py:561
  103.1 47.7 %collective-permute-start.4 = (bf16[1,1440,256]{2,1,0:T(8,128)(2,1)}, bf16[1,1440,256]{2,1,0:T(8,128)(2,1)}, u32[]{:S(2)}, u32[]{:S(2)}) collective-permute-start(bf16[1,1440,256]{2,1,0:T(8,128)(2,1)} %get-tuple-element.25), channel_id=1, source_target_pairs={{0,1},{1,2},{2,3},{3,4},{4,5},{5,6},{6,7},{7,8},{8,9},{9,10},{10,1... | collective-permute-start | bytes 2211848 | tf_op jit(solution)/shard_map/ppermute | solution.py:552
  106.2 44.5 %collective-permute-start.5 = (bf16[1,1440,256]{2,1,0:T(8,128)(2,1)}, bf16[1,1440,256]{2,1,0:T(8,128)(2,1)}, u32[]{:S(2)}, u32[]{:S(2)}) collective-permute-start(bf16[1,1440,256]{2,1,0:T(8,128)(2,1)} %get-tuple-element.24), channel_id=1, source_target_pairs={{1,0},{2,1},{3,2},{4,3},{5,4},{6,5},{7,6},{8,7},{9,8},{10,9},{11,1... | collective-permute-start | bytes 2211848 | tf_op jit(solution)/shard_map/ppermute | solution.py:553
  107.5 15.2 %collective-permute-start.13 = (bf16[48,256]{1,0:T(8,128)(2,1)}, bf16[48,256]{1,0:T(8,128)(2,1)S(1)}, u32[]{:S(2)}, u32[]{:S(2)}) collective-permute-start(bf16[48,256]{1,0:T(8,128)(2,1)} %get-tuple-element.23), channel_id=1, source_target_pairs={{0,8},{1,9},{2,10},{3,11},{4,12},{5,13},{6,14},{7,15},{8,0},{9,1},... | collective-permute-start | bytes 73736 | tf_op jit(solution)/shard_map/ppermute | solution.py:515
  112.4 11.3 %collective-permute-start.14 = (bf16[48,256]{1,0:T(8,128)(2,1)}, bf16[48,256]{1,0:T(8,128)(2,1)S(1)}, u32[]{:S(2)}, u32[]{:S(2)}) collective-permute-start(bf16[48,256]{1,0:T(8,128)(2,1)} %get-tuple-element.23), channel_id=1, source_target_pairs={{0,12},{1,13},{2,14},{3,15},{4,8},{5,9},{6,10},{7,11},{8,4},{9,5},... | collective-permute-start | bytes 73736 | tf_op jit(solution)/shard_map/ppermute | solution.py:515
  124.3 2.3 %collective-permute-start.15 = (bf16[192,256]{1,0:T(8,128)(2,1)}, bf16[192,256]{1,0:T(8,128)(2,1)S(1)}, u32[]{:S(2)}, u32[]{:S(2)}) collective-permute-start(bf16[192,256]{1,0:T(8,128)(2,1)} %bitcast.38), channel_id=1, source_target_pairs={{0,1},{1,0},{2,3},{3,2},{4,5},{5,4},{6,7},{7,6},{8,9},{9,8},{10,11... | collective-permute-start | bytes 294920 | tf_op jit(solution)/shard_map/ppermute | solution.py:515
  124.3 10.7 %collective-permute-start.16 = (bf16[192,256]{1,0:T(8,128)(2,1)}, bf16[192,256]{1,0:T(8,128)(2,1)}, u32[]{:S(2)}, u32[]{:S(2)}) collective-permute-start(bf16[192,256]{1,0:T(8,128)(2,1)} %bitcast.38), channel_id=1, source_target_pairs={{0,2},{1,3},{2,0},{3,1},{4,6},{5,7},{6,4},{7,5},{8,10},{9,11},{10,... | collective-permute-start | bytes 294920 | tf_op jit(solution)/shard_map/ppermute | solution.py:515
  132.6 18.2 %copy-start.8 = (bf16[3,1440,256]{2,1,0:T(8,128)(2,1)S(1)}, bf16[3,1440,256]{2,1,0:T(8,128)(2,1)}, u32[]{:S(2)}) copy-start(bf16[3,1440,256]{2,1,0:T(8,128)(2,1)} %copy-done.7) | copy-start | bytes 6635524
  132.6 3.9 %collective-permute-start.18 = (f32[48,256]{1,0:T(8,128)S(1)}, f32[48,256]{1,0:T(8,128)S(1)}, u32[]{:S(2)}, u32[]{:S(2)}) collective-permute-start(f32[48,256]{1,0:T(8,128)S(1)} %get-tuple-element.21), channel_id=1, source_target_pairs={{0,1},{1,0},{2,3},{3,2},{4,5},{5,4},{6,7},{7,6},{8,9},{9,8},{10,11... | collective-permute-start | bytes 147464 | tf_op jit(solution)/shard_map/ppermute | solution.py:515
  133.2 5.0 %collective-permute-start.19 = (f32[48,256]{1,0:T(8,128)S(1)}, f32[48,256]{1,0:T(8,128)S(1)}, u32[]{:S(2)}, u32[]{:S(2)}) collective-permute-start(f32[48,256]{1,0:T(8,128)S(1)} %get-tuple-element.21), channel_id=1, source_target_pairs={{0,2},{1,3},{2,0},{3,1},{4,6},{5,7},{6,4},{7,5},{8,10},{9,11},{10,... | collective-permute-start | bytes 147464 | tf_op jit(solution)/shard_map/ppermute | solution.py:515
  134.9 3.9 %collective-permute-start.20 = (f32[48,256]{1,0:T(8,128)S(1)}, f32[48,256]{1,0:T(8,128)S(1)}, u32[]{:S(2)}, u32[]{:S(2)}) collective-permute-start(f32[48,256]{1,0:T(8,128)S(1)} %get-tuple-element.21), channel_id=1, source_target_pairs={{0,3},{1,2},{2,1},{3,0},{4,7},{5,6},{6,5},{7,4},{8,11},{9,10},{10,... | collective-permute-start | bytes 147464 | tf_op jit(solution)/shard_map/ppermute | solution.py:515
  136.5 4.8 %collective-permute-start.17 = (bf16[192,256]{1,0:T(8,128)(2,1)}, bf16[192,256]{1,0:T(8,128)(2,1)S(1)}, u32[]{:S(2)}, u32[]{:S(2)}) collective-permute-start(bf16[192,256]{1,0:T(8,128)(2,1)} %bitcast.38), channel_id=1, source_target_pairs={{0,3},{1,2},{2,1},{3,0},{4,7},{5,6},{6,5},{7,4},{8,11},{9,10},{10,... | collective-permute-start | bytes 294920 | tf_op jit(solution)/shard_map/ppermute | solution.py:515
  138.8 11.3 %collective-permute-start.21 = (f32[48,256]{1,0:T(8,128)S(1)}, f32[48,256]{1,0:T(8,128)S(1)}, u32[]{:S(2)}, u32[]{:S(2)}) collective-permute-start(f32[48,256]{1,0:T(8,128)S(1)} %add_add_fusion.1), channel_id=1, source_target_pairs={{0,4},{1,5},{2,6},{3,7},{4,0},{5,1},{6,2},{7,3},{8,12},{9,13},{10,... | collective-permute-start | bytes 147464 | tf_op jit(solution)/shard_map/ppermute | solution.py:515
  139.8 10.3 %collective-permute-start.22 = (f32[48,256]{1,0:T(8,128)S(1)}, f32[48,256]{1,0:T(8,128)S(1)}, u32[]{:S(2)}, u32[]{:S(2)}) collective-permute-start(f32[48,256]{1,0:T(8,128)S(1)} %add_add_fusion.1), channel_id=1, source_target_pairs={{0,8},{1,9},{2,10},{3,11},{4,12},{5,13},{6,14},{7,15},{8,0},{9,1},... | collective-permute-start | bytes 147464 | tf_op jit(solution)/shard_map/ppermute | solution.py:515
  141.3 8.8 %collective-permute-start.23 = (f32[48,256]{1,0:T(8,128)S(1)}, f32[48,256]{1,0:T(8,128)S(1)}, u32[]{:S(2)}, u32[]{:S(2)}) collective-permute-start(f32[48,256]{1,0:T(8,128)S(1)} %add_add_fusion.1), channel_id=1, source_target_pairs={{0,12},{1,13},{2,14},{3,15},{4,8},{5,9},{6,10},{7,11},{8,4},{9,5},... | collective-permute-start | bytes 147464 | tf_op jit(solution)/shard_map/ppermute | solution.py:515
  145.9 20.1 %all-to-all-start.3 = ((bf16[16,8,768]{2,1,0:T(8,128)(2,1)}), bf16[16,8,768]{2,1,0:T(8,128)(2,1)}, u32[]{:S(2)}, u32[]{:S(2)}) async-start(bf16[16,8,768]{2,1,0:T(8,128)(2,1)} %bitcast.88), calls=%async_computation.3 | async-start | bytes 393216 | tf_op jit(solution)/shard_map/all_to_all | solution.py:561
  (33 other events, 123.0 us)

commit v2 on v1

--- a/solution.py
+++ b/solution.py
@@ -14,6 +14,9 @@
 WIN = STEP + 2 * SPAN
 GROUP = 8
 NONE = -4096
+META = 16
+PER = 5
+CHUNK = 240
 ROOT = math.sqrt(2.0 / math.pi)
 CUBE = 0.044715
 F32 = jnp.float32
@@ -171,60 +174,160 @@
     return lax.dot_general(a, b, (((0,), (0,)), ((), ())), preferred_element_type=F32)
 
 
-def transform(features, table):
+def in_hbm(array):
+    return pltpu.with_memory_space_constraint(array, pltpu.HBM)
+
+
+def every(*shape):
+    return pl.BlockSpec(shape, lambda *g: (0,) * len(shape))
+
+
+VMEM = pl.BlockSpec(memory_space=pltpu.VMEM)
+SMEM = pl.BlockSpec(memory_space=pltpu.SMEM)
+ANYWHERE = pl.BlockSpec(memory_space=pl.ANY)
+
+
+def transform(position, features, table, rows, cols, basis):
     lat_dev, lon, channels = features.shape
-    rows = table.shape[0]
-
-    def body(x_ref, t_ref, o_ref):
-        o_ref[...] = dot(t_ref[...], x_ref[0]).astype(BF16)
+    depth = table.shape[0]
+    kernels, _, taps = basis.shape
+    edges = (0, lat_dev - 1)
+
+    def body(p_ref, x_ref, t_ref, row_ref, col_ref, basis_ref, o_ref, first_ref, last_ref, *rest):
+        edge_refs = (first_ref, last_ref)
+        held, table_held, wide, meta, sem, edge_sem, small_sem = rest[:7]
+        small_held = rest[7:]
+        table_copy = pltpu.make_async_copy(t_ref, table_held, small_sem.at[3])
+        copies = [
+            pltpu.make_async_copy(x_ref.at[i], held.at[i], sem.at[i]) for i in range(lat_dev)
+        ]
+        small_copies = [
+            pltpu.make_async_copy(ref, to, small_sem.at[n])
+            for n, (ref, to) in enumerate(zip((row_ref, col_ref, basis_ref), small_held, strict=True))
+        ]
+        for copy in [*small_copies, table_copy, *copies]:
+            copy.start()
+        for copy in small_copies:
+            copy.wait()
+        rows_held, cols_held, basis_held = small_held
+        sent = []
+        for n, edge in enumerate(edges):
+            wide[...] = jnp.zeros_like(wide)
+            own = rows_held[edge : edge + 1, :] - (p_ref[0] * lat_dev + edge)
+            wide[0:1, 0:taps] = own.astype(F32)
+            wide[1:2, 0:taps] = cols_held[edge : edge + 1, :].astype(F32)
+            for k in range(kernels):
+                wide[2 + k : 3 + k, 0:taps] = basis_held[k, edge : edge + 1, :].astype(F32)
+            meta[n] = wide[...].astype(BF16)
+            sent.append(
+                pltpu.make_async_copy(
+                    meta.at[n], edge_refs[n].at[pl.ds(lon, META)], edge_sem.at[n, 1]
+                )
+            )
+            sent[-1].start()
+        table_copy.wait()
+        for i, copy in enumerate(copies):
+            copy.wait()
+            for n, edge in enumerate(edges):
+                if i == edge:
+                    sent.append(
+                        pltpu.make_async_copy(
+                            held.at[i], edge_refs[n].at[pl.ds(0, lon)], edge_sem.at[n, 0]
+                        )
+                    )
+                    sent[-1].start()
+            o_ref[:, i * channels : (i + 1) * channels] = dot(table_held[...], held[i]).astype(BF16)
+        for copy in sent:
+            copy.wait()
 
     return pl.pallas_call(
         body,
-        grid=(lat_dev,),
-        in_specs=[
-            pl.BlockSpec((1, lon, channels), lambda i: (i, 0, 0)),
-            pl.BlockSpec((rows, lon), lambda i: (0, 0)),
+        in_specs=[SMEM] + [ANYWHERE] * 5,
+        out_specs=[VMEM, ANYWHERE, ANYWHERE],
+        out_shape=[
+            pltpu.HBM((depth, lat_dev * channels), BF16),
+            pltpu.HBM((lon + META, channels), BF16),
+            pltpu.HBM((lon + META, channels), BF16),
         ],
-        out_specs=pl.BlockSpec((rows, channels), lambda i: (0, i)),
-        out_shape=jax.ShapeDtypeStruct((rows, lat_dev * channels), BF16),
-        compiler_params=params(24),
-        cost_estimate=cost(2 * rows * lon * channels * lat_dev, features.size * 2),
+        scratch_shapes=[
+            pltpu.VMEM((lat_dev, lon, channels), BF16),
+            pltpu.VMEM(table.shape, BF16),
+            pltpu.VMEM((META, channels), F32),
+            pltpu.VMEM((2, META, channels), BF16),
+            pltpu.SemaphoreType.DMA((lat_dev,)),
+            pltpu.SemaphoreType.DMA((2, 2)),
+            pltpu.SemaphoreType.DMA((4,)),
+            pltpu.VMEM(rows.shape, rows.dtype),
+            pltpu.VMEM(cols.shape, cols.dtype),
+            pltpu.VMEM(basis.shape, basis.dtype),
+        ],
+        compiler_params=params(16),
+        cost_estimate=cost(2 * depth * lon * channels * lat_dev, features.size * 2),
         name="transform",
-    )(features, table)
-
-
-def filtered(middle, north, south, shifts, taps, weights, keep):
-    lat_dev, lon, channels = middle.shape
+    )(
+        position,
+        in_hbm(features),
+        in_hbm(table),
+        in_hbm(rows),
+        in_hbm(cols),
+        in_hbm(basis),
+    )
+
+
+def filtered(middle, north, south, shifts, taps, weights, rows, before=None):
+    first, stride, total = rows
+    lat_dev = shifts.shape[0]
+    lon, channels = middle[0].shape[-2:]
     kernels = taps.shape[0]
     count = taps.shape[2]
     wide = kernels * channels
-    per = 5
+    per = PER
     chunk = per * STEP
-    rows = lat_dev + 2
-
-    def body(shift_ref, tap_ref, mid_ref, north_ref, south_ref, w_ref, *rest):
-        if keep:
-            mixed_ref, out_ref, ext, sem = rest
-        else:
-            out_ref, mixed_ref, ext, sem = rest
-        row = pl.program_id(0)
-
-        def copies():
+    edges = north is not None
+    keep = weights is None
+
+    def body(shift_ref, tap_ref, *rest):
+        rest = list(rest)
+        mid_refs = [rest.pop(0) for _ in middle]
+        if len(middle) == 1:
+            mid_refs = [mid_refs[0].at[i] for i in range(lat_dev)]
+        north_ref, south_ref = (rest.pop(0), rest.pop(0)) if edges else (None, None)
+        w_ref = None if keep else rest.pop(0)
+        if before is not None:
+            rest.pop(0)
+        out_ref, ext, sem = rest[:3]
+        mixed_ref = None if keep else rest[3]
+        step_id = pl.program_id(0)
+        row = first + stride * step_id
+
+        def copies(which):
             made = []
-            for e in range(rows):
-                src = north_ref.at[0] if e == 0 else (south_ref.at[0] if e == rows - 1 else mid_ref.at[e - 1])
-                for a, b, n in ((0, SPAN, lon), (lon - SPAN, 0, SPAN), (0, lon + SPAN, SPAN)):
+            for e in which:
+                src = (
+                    north_ref if e == 0 else south_ref if e == lat_dev + 1 else mid_refs[e - 1]
+                )
+                for n, (a, b, size) in enumerate(
+                    ((0, SPAN, lon), (lon - SPAN, 0, SPAN), (0, lon + SPAN, SPAN))
+                ):
                     made.append(
                         pltpu.make_async_copy(
-                            src.at[pl.ds(a, n)], ext.at[e, pl.ds(b, n)], sem.at[len(made)]
+                            src.at[pl.ds(a, size)], ext.at[e, pl.ds(b, size)], sem.at[e, n]
                         )
                     )
             return made
 
-        @pl.when(row == 0)
+        needed = []
+        seen = set()
+        for g in range(total):
+            now = [e for e in range(first + stride * g, first + stride * g + 3) if e not in seen]
+            seen.update(now)
+            needed.append(now)
+
+        @pl.when(step_id == 0)
         def _():
-            for copy in copies():
-                copy.start()
+            for now in needed:
+                for copy in copies(now):
+                    copy.start()
 
         across = lax.broadcasted_iota(jnp.int32, (STEP, 3 * WIN), 1)
         down = lax.broadcasted_iota(jnp.int32, (STEP, 3 * WIN), 0)
@@ -236,66 +339,77 @@
                 band[k] = band[k] + jnp.where(hit, tap_ref[k, row, t], 0.0)
         band = jnp.concatenate(band, axis=0).astype(BF16)
 
-        @pl.when(row == 0)
-        def _():
-            for copy in copies():
-                copy.wait()
-
-        def step(c, carry):
+        for g, now in enumerate(needed):
+
+            @pl.when(step_id == g)
+            def _(now=now):
+                for copy in copies(now):
+                    copy.wait()
+
+        for c in range(lon // chunk):
             for b in range(per):
-                start = pl.multiple_of(c * chunk + b * STEP, STEP)
+                start = c * chunk + b * STEP
                 window = jnp.concatenate(
-                    [ext[row + e, pl.ds(start, WIN), :] for e in range(3)], axis=0
+                    [ext[row + e, start : start + WIN, :] for e in range(3)], axis=0
                 )
                 sums = dot(band, window).astype(BF16)
                 for k in range(kernels):
-                    place = (pl.ds(start, STEP), pl.ds(k * channels, channels))
+                    part = sums[k * STEP : (k + 1) * STEP]
+                    lanes = slice(k * channels, (k + 1) * channels)
                     if keep:
-                        mixed_ref[(0,) + place] = sums[k * STEP : (k + 1) * STEP]
+                        out_ref[0, start : start + STEP, lanes] = part
                     else:
-                        mixed_ref[pl.ds(b * STEP, STEP), pl.ds(k * channels, channels)] = sums[
-                            k * STEP : (k + 1) * STEP
-                        ]
-            start = pl.multiple_of(c * chunk, chunk)
-            if keep:
-                block = mixed_ref[0, pl.ds(start, chunk), :]
-            else:
-                block = mixed_ref[...]
-            out_ref[0, pl.ds(start, chunk), :] = dot(block, w_ref[...])
-            return carry
-
-        lax.fori_loop(0, lon // chunk, step, 0)
-
-    out_specs = [pl.BlockSpec((1, lon, channels), lambda i: (i, 0, 0))]
-    out_shape = [jax.ShapeDtypeStruct((lat_dev, lon, channels), F32)]
-    scratch = []
-    if keep:
-        out_specs.insert(0, pl.BlockSpec((1, lon, wide), lambda i: (i, 0, 0)))
-        out_shape.insert(0, jax.ShapeDtypeStruct((lat_dev, lon, wide), BF16))
-    else:
-        scratch.append(pltpu.VMEM((chunk, wide), BF16))
-    result = pl.pallas_call(
+                        mixed_ref[c % 2, b * STEP : (b + 1) * STEP, lanes] = part
+            if not keep:
+                out_ref[0, c * chunk : (c + 1) * chunk, :] = sum(
+                    lax.dot_general(
+                        mixed_ref[c % 2, :, k * channels : (k + 1) * channels],
+                        w_ref[k * channels : (k + 1) * channels, :],
+                        (((1,), (1,)), ((), ())),
+                        preferred_element_type=F32,
+                    )
+                    for k in range(kernels)
+                ).astype(BF16)
+
+    depth = wide if keep else channels
+    operands = [shifts, taps, *(in_hbm(array) for array in middle)]
+    in_specs = [SMEM, SMEM] + [ANYWHERE] * len(middle)
+    scratch = [
+        pltpu.VMEM((lat_dev + 2, lon + 2 * SPAN, channels), BF16),
+        pltpu.SemaphoreType.DMA((lat_dev + 2, 3)),
+    ]
+    if edges:
+        operands += [in_hbm(north), in_hbm(south)]
+        in_specs += [ANYWHERE, ANYWHERE]
+    if not keep:
+        operands.append(in_hbm(weights))
+        in_specs.append(every(wide, channels))
+        scratch.append(pltpu.VMEM((2, chunk, wide), BF16))
+    aliases = {}
+    if before is not None:
+        aliases[len(operands)] = 0
+        operands.append(before)
+        in_specs.append(ANYWHERE)
+    return pl.pallas_call(
         body,
-        grid=(lat_dev,),
-        in_specs=[
-            pl.BlockSpec(memory_space=pltpu.SMEM),
-            pl.BlockSpec(memory_space=pltpu.SMEM),
-            pl.BlockSpec(memory_space=pl.ANY),
-            pl.BlockSpec(memory_space=pl.ANY),
-            pl.BlockSpec(memory_space=pl.ANY),
-            pl.BlockSpec((wide, channels), lambda i: (0, 0)),
-        ],
-        out_specs=out_specs,
-        out_shape=out_shape,
-        scratch_shapes=scratch
-        + [pltpu.VMEM((rows, lon + 2 * SPAN, channels), BF16), pltpu.SemaphoreType.DMA((3 * rows,))],
-        compiler_params=params(32),
+        grid=(total,),
+        in_specs=in_specs,
+        out_specs=pl.BlockSpec((1, lon, depth), lambda g: (first + stride * g, 0, 0)),
+        out_shape=pltpu.HBM((lat_dev, lon, depth), BF16),
+        input_output_aliases=aliases,
+        scratch_shapes=scratch,
+        compiler_params=params(24),
         cost_estimate=cost(
-            2 * lat_dev * lon * channels * (3 * wide + 3 * WIN * kernels), middle.size * 10
+            2 * total * lon * channels * (wide * (0 if keep else 1) + 3 * WIN * kernels),
+            total * lon * channels * 8,
         ),
-        name="filtered",
-    )(shifts, taps, middle, north, south, weights)
-    return result if keep else result[0]
+        name="filtered" if keep else "filtered_back",
+    )(*operands)
+
+
+def blocks_of(ref, start, rows, lanes):
+    block = ref[:, start : start + rows, lanes].astype(F32)
+    return block.reshape(block.shape[0] * rows, block.shape[2]).astype(BF16)
 
 
 def spectral_forward(position, owned, table_in, table_out, gain):
@@ -337,37 +451,43 @@
             ],
         ),
         out_shape=[
-            jax.ShapeDtypeStruct((rows, channels), F32),
-            jax.ShapeDtypeStruct((group_rows, width), BF16),
+            pltpu.HBM((rows, channels), F32),
+            pltpu.HBM((group_rows, width), BF16),
         ],
         compiler_params=params(16),
         name="spectral_forward",
-    )(position, owned, table_in, table_out, gain)
-
-
-def spectral_adjoint(position, owned, table_in, table_out, gain, analysed):
-    group_rows, width = owned.shape
+    )(position, owned, in_hbm(table_in), in_hbm(table_out), in_hbm(gain))
+
+
+def spectral_adjoint(position, received, table_in, table_out, gain, analysed, terms):
+    devices, block_rows, width = received.shape
+    group = block_rows - terms
+    group_rows = devices * group
     _, rows, depth = table_in.shape
     degrees, channels = gain.shape
     lat_dev = width // channels
 
     def body(p_ref, x_ref, b_ref, a_ref, g_ref, analysed_ref, gain_ref, o_ref):
+        summed = jnp.sum(x_ref[:, 0:terms, :].astype(F32), axis=0).astype(BF16)
+        for d in range(devices):
+            o_ref[d, 0:terms, :] = summed
         scaled = jnp.zeros((rows, channels), F32)
         for i in range(lat_dev):
             scaled = scaled + dot(
                 b_ref[0, :, i * group_rows : (i + 1) * group_rows],
-                x_ref[:, i * channels : (i + 1) * channels],
+                blocks_of(x_ref, terms, group, slice(i * channels, (i + 1) * channels)),
             )
-        terms = analysed_ref[...] * scaled
+        products = analysed_ref[...] * scaled
         total = jnp.zeros((degrees, channels), F32)
         for s in range(rows // degrees):
-            total = total + terms[s * degrees : (s + 1) * degrees]
+            total = total + products[s * degrees : (s + 1) * degrees]
         gain_ref[...] = total
         gain_rows = jnp.concatenate([g_ref[...]] * (rows // degrees), axis=0)
         grad = (gain_rows * scaled).astype(BF16)
         for i in range(lat_dev):
-            o_ref[:, i * channels : (i + 1) * channels] = dot_t(
-                a_ref[0, :, i * group_rows : (i + 1) * group_rows], grad
+            part = dot_t(a_ref[0, :, i * group_rows : (i + 1) * group_rows], grad)
+            o_ref[:, terms:block_rows, i * channels : (i + 1) * channels] = part.reshape(
+                devices, group, channels
             ).astype(BF16)
 
     table_spec = pl.BlockSpec((1, rows, depth), lambda g, p: (p[0], 0, 0))
@@ -377,7 +497,7 @@
             num_scalar_prefetch=1,
             grid=(1,),
             in_specs=[
-                pl.BlockSpec((group_rows, width), lambda g, p: (0, 0)),
+                pl.BlockSpec((devices, block_rows, width), lambda g, p: (0, 0, 0)),
                 table_spec,
                 table_spec,
                 pl.BlockSpec((degrees, channels), lambda g, p: (0, 0)),
@@ -385,69 +505,61 @@
             ],
             out_specs=[
                 pl.BlockSpec((degrees, channels), lambda g, p: (0, 0)),
-                pl.BlockSpec((group_rows, width), lambda g, p: (0, 0)),
+                pl.BlockSpec((devices, block_rows, width), lambda g, p: (0, 0, 0)),
             ],
         ),
         out_shape=[
             jax.ShapeDtypeStruct((degrees, channels), F32),
-            jax.ShapeDtypeStruct((group_rows, width), BF16),
+            pltpu.HBM((devices, block_rows, width), BF16),
         ],
         compiler_params=params(16),
         name="spectral_adjoint",
-    )(position, owned, table_in, table_out, gain, analysed)
-
-
-def activation(disco, returned, grad_output, inverse, inverse_t):
-    lat_dev, lon, channels = disco.shape
+    )(
+        position,
+        received,
+        in_hbm(table_in),
+        in_hbm(table_out),
+        in_hbm(gain),
+        in_hbm(analysed),
+    )
+
+
+def activation(mixed, weights, returned, grad_output, inverse, inverse_t, devices, terms):
+    lat_dev, lon, wide = mixed.shape
+    channels = grad_output.shape[2]
     group_rows = returned.shape[0]
-    chunk = 240
-
-    def body(d_ref, y_ref, g_ref, inv_ref, invt_ref, o_ref, gt_ref, x_ref):
-        def step(c, carry):
-            place = pl.ds(pl.multiple_of(c * chunk, chunk), chunk)
-            total = d_ref[0, place, :] + dot(inv_ref[place, :], y_ref[...])
+    group = group_rows // devices
+    chunk = CHUNK
+    piece = wide // devices // lat_dev
+
+    def body(m_ref, w_ref, y_ref, g_ref, inv_ref, invt_ref, *rest):
+        o_ref, row_refs = rest[0], rest[1 : 1 + lat_dev]
+        rest = rest[1 + lat_dev :]
+        acc, held, sem = rest[-3:]
+        row = pl.program_id(0)
+        gt_ref = held.at[row]
+        for c in range(lon // chunk):
+            place = slice(c * chunk, (c + 1) * chunk)
+            total = dot(m_ref[0, place, :], w_ref[...]) + dot(inv_ref[place, :], y_ref[...])
             square = total * total
             half = 0.5 + 0.5 * jnp.tanh(total * (ROOT + ROOT * CUBE * square))
             value = total * half
             slope = half + value * (1.0 - half) * (2.0 * ROOT + 6.0 * ROOT * CUBE * square)
             o_ref[0, place, :] = value.astype(BF16)
-            gt_ref[0, place, :] = (g_ref[0, place, :].astype(F32) * slope).astype(BF16)
-            return carry
-
-        lax.fori_loop(0, lon // chunk, step, 0)
-        x_ref[...] = dot(invt_ref[...], gt_ref[0]).astype(BF16)
-
-    row_spec = pl.BlockSpec((1, lon, channels), lambda i: (i, 0, 0))
-    column_spec = pl.BlockSpec((group_rows, channels), lambda i: (0, i))
-    return pl.pallas_call(
-        body,
-        grid=(lat_dev,),
-        in_specs=[
-            row_spec,
-            column_spec,
-            row_spec,
-            pl.BlockSpec((lon, group_rows), lambda i: (0, 0)),
-            pl.BlockSpec((group_rows, lon), lambda i: (0, 0)),
-        ],
-        out_specs=[row_spec, row_spec, column_spec],
-        out_shape=[
-            jax.ShapeDtypeStruct((lat_dev, lon, channels), BF16),
-            jax.ShapeDtypeStruct((lat_dev, lon, channels), BF16),
-            jax.ShapeDtypeStruct((group_rows, lat_dev * channels), BF16),
-        ],
-        compiler_params=params(32),
-        cost_estimate=cost(4 * disco.size * group_rows, disco.size * 10),
-        name="activation",
-    )(disco, returned, grad_output, inverse, inverse_t)
-
-
-def weight_terms(mixed, grad_total):
-    lat_dev, lon, wide = mixed.shape
-    channels = grad_total.shape[2]
-
-    def body(m_ref, g_ref, o_ref, acc):
-        row = pl.program_id(0)
-        part = dot(jnp.transpose(g_ref[0]), m_ref[0])
+            gt_ref[place, :] = (g_ref[0, place, :].astype(F32) * slope).astype(BF16)
+        for i in range(lat_dev):
+
+            @pl.when(row == i)
+            def _(i=i):
+                pltpu.make_async_copy(held.at[i], row_refs[i], sem.at[i]).start()
+
+        spectrum = dot(invt_ref[...], gt_ref[...])
+        part = dot(jnp.transpose(gt_ref[...]), m_ref[0])
+
+        @pl.when(row == lat_dev - 1)
+        def _():
+            for i in range(lat_dev - 1):
+                pltpu.make_async_copy(held.at[i], row_refs[i], sem.at[i]).wait()
 
         @pl.when(row == 0)
         def _():
@@ -457,48 +569,113 @@
         def _():
             acc[...] += part
 
+        if not terms:
+            x_ref, weight_ref = rest[0:2]
+            x_ref[...] = spectrum.astype(BF16)
+
+            @pl.when(row == lat_dev - 1)
+            def _():
+                weight_ref[...] = jnp.transpose(acc[...]).astype(BF16)
+                pltpu.make_async_copy(held.at[row], row_refs[-1], sem.at[row]).wait()
+
+            return
+        x_ref = rest[0]
+        spectrum = spectrum.reshape(devices, group, channels).astype(BF16)
+        for i in range(lat_dev):
+
+            @pl.when(row == i)
+            def _(i=i):
+                x_ref[:, terms : terms + group, i * channels : (i + 1) * channels] = spectrum
+
         @pl.when(row == lat_dev - 1)
         def _():
-            o_ref[...] = jnp.transpose(acc[...]).astype(BF16)
-
+            weight = jnp.transpose(acc[...]).astype(BF16)
+            for d in range(devices):
+                for i in range(lat_dev):
+                    at = (d * lat_dev + i) * piece
+                    x_ref[d, 0:piece, i * channels : (i + 1) * channels] = weight[at : at + piece]
+            pltpu.make_async_copy(held.at[row], row_refs[-1], sem.at[row]).wait()
+
+    row_spec = pl.BlockSpec((1, lon, channels), lambda i: (i, 0, 0))
+    column_spec = pl.BlockSpec((group_rows, channels), lambda i: (0, i))
+    if terms:
+        last_specs = [pl.BlockSpec((devices, terms + group, lat_dev * channels), lambda i: (0, 0, 0))]
+        last_shapes = [pltpu.HBM((devices, terms + group, lat_dev * channels), BF16)]
+    else:
+        last_specs = [column_spec, pl.BlockSpec((wide, channels), lambda i: (0, 0))]
+        last_shapes = [
+            jax.ShapeDtypeStruct((group_rows, lat_dev * channels), BF16),
+            jax.ShapeDtypeStruct((wide, channels), BF16),
+        ]
     return pl.pallas_call(
         body,
         grid=(lat_dev,),
         in_specs=[
             pl.BlockSpec((1, lon, wide), lambda i: (i, 0, 0)),
-            pl.BlockSpec((1, lon, channels), lambda i: (i, 0, 0)),
+            every(wide, channels),
+            column_spec,
+            row_spec,
+            every(lon, group_rows),
+            every(group_rows, lon),
         ],
-        out_specs=pl.BlockSpec((wide, channels), lambda i: (0, 0)),
-        out_shape=jax.ShapeDtypeStruct((wide, channels), BF16),
-        scratch_shapes=[pltpu.VMEM((channels, wide), F32)],
-        compiler_params=params(32),
-        cost_estimate=cost(2 * mixed.size * channels, mixed.size * 2),
-        name="weight_terms",
-    )(mixed, grad_total)
-
-
-def final(bands, forward, grad_disco):
+        out_specs=[row_spec] + [ANYWHERE] * lat_dev + last_specs,
+        out_shape=[
+            pltpu.HBM((lat_dev, lon, channels), BF16),
+        ]
+        + [pltpu.HBM((lon, channels), BF16)] * lat_dev
+        + last_shapes,
+        scratch_shapes=[
+            pltpu.VMEM((channels, wide), F32),
+            pltpu.VMEM((lat_dev, lon, channels), BF16),
+            pltpu.SemaphoreType.DMA((lat_dev,)),
+        ],
+        compiler_params=params(40),
+        cost_estimate=cost(
+            4 * grad_output.size * (group_rows + wide), grad_output.size * 14
+        ),
+        name="activation",
+    )(
+        in_hbm(mixed),
+        in_hbm(weights),
+        returned,
+        in_hbm(grad_output),
+        in_hbm(inverse),
+        in_hbm(inverse_t),
+    )
+
+
+def final(received, forward, grad_disco, terms):
     lat_dev, lon, channels = grad_disco.shape
-    group_rows = bands.shape[0]
-
-    def body(y_ref, f_ref, d_ref, o_ref):
-        o_ref[0] = (d_ref[0] + dot(f_ref[...], y_ref[...])).astype(BF16)
-
     row_spec = pl.BlockSpec((1, lon, channels), lambda i: (i, 0, 0))
+    out_specs = [row_spec]
+    out_shape = [pltpu.HBM((lat_dev, lon, channels), BF16)]
+    if terms:
+        devices, block_rows, _ = received.shape
+        first_spec = pl.BlockSpec((devices, block_rows, channels), lambda i: (0, 0, i))
+        out_specs.append(pl.BlockSpec((devices, 1, terms, channels), lambda i: (0, i, 0, 0)))
+        out_shape.append(pltpu.HBM((devices, lat_dev, terms, channels), F32))
+    else:
+        first_spec = pl.BlockSpec((received.shape[0], channels), lambda i: (0, i))
+    depth = forward.shape[1]
+
+    def body(y_ref, f_ref, d_ref, o_ref, *rest):
+        if terms:
+            rest[0][:, 0] = y_ref[:, 0:terms, :].astype(F32)
+            bands = blocks_of(y_ref, terms, block_rows - terms, slice(0, channels))
+        else:
+            bands = y_ref[...]
+        o_ref[0] = (d_ref[0].astype(F32) + dot(f_ref[...], bands)).astype(BF16)
+
     return pl.pallas_call(
         body,
         grid=(lat_dev,),
-        in_specs=[
-            pl.BlockSpec((group_rows, channels), lambda i: (0, i)),
-            pl.BlockSpec((lon, group_rows), lambda i: (0, 0)),
-            row_spec,
-        ],
-        out_specs=row_spec,
-        out_shape=jax.ShapeDtypeStruct((lat_dev, lon, channels), BF16),
+        in_specs=[first_spec, pl.BlockSpec((lon, depth), lambda i: (0, 0)), row_spec],
+        out_specs=out_specs,
+        out_shape=out_shape,
         compiler_params=params(24),
-        cost_estimate=cost(2 * grad_disco.size * group_rows, grad_disco.size * 6),
+        cost_estimate=cost(2 * grad_disco.size * depth, grad_disco.size * 6),
         name="final",
-    )(bands, forward, grad_disco)
+    )(received, in_hbm(forward), in_hbm(grad_disco))
 
 
 def stages(count):
@@ -537,14 +714,17 @@
     return array
 
 
-def sum_everywhere(array):
+def sum_everywhere(array, between):
     count = lax.axis_size("lat")
-    for stride, factor in stages(count):
+    plan = stages(count)
+    for n, (stride, factor) in enumerate(plan):
+        if n == len(plan) - 1:
+            array, between = lax.optimization_barrier((array, between))
         parts = [array] + [partner(array, count, stride, by) for by in range(1, factor)]
         while len(parts) > 1:
             parts = [parts[k] + parts[k + 1] for k in range(0, len(parts), 2)]
         array = parts[0]
-    return array
+    return (array, between)
 
 
 def neighbours(north_edge, south_edge):
@@ -554,12 +734,14 @@
     return (from_north, from_south)
 
 
-def exchange(array):
+def exchange(blocks):
+    return lax.all_to_all(blocks, "lat", split_axis=0, concat_axis=0, tiled=True)
+
+
+def exchange_rows(array):
     count = lax.axis_size("lat")
     rows, width = array.shape
-    blocks = array.reshape(count, rows // count, width)
-    blocks = lax.all_to_all(blocks, "lat", split_axis=0, concat_axis=0, tiled=True)
-    return blocks.reshape(rows, width)
+    return exchange(array.reshape(count, rows // count, width)).reshape(rows, width)
 
 
 def local(features, disco_rows, disco_cols, disco_basis, disco_weight, spectral_gain, grad_output):
@@ -571,6 +753,7 @@
     order_count = lat_count
     owned_orders = order_count // devices
     kernels, _, taps = disco_basis.shape
+    wide = kernels * channels
     forward, inverse = fourier_tables(lon, order_count, devices)
     group = forward.shape[1] // devices
     forward_t = jnp.asarray(np.ascontiguousarray(forward.T))
@@ -578,40 +761,56 @@
     forward = jnp.asarray(forward)
     inverse = jnp.asarray(inverse)
     place = position.astype(jnp.int32).reshape(1)
-    small = order_count * owned_orders * 2 * degrees * lat_dev * devices * group <= TABLE_CAP * 4
-
-    north, south = neighbours(features[:HALO], features[lat_dev - HALO :])
-    coefficients = transform(features, forward_t)
-    owned = exchange(coefficients)
+    piece = wide // devices // lat_dev
+    small = (
+        order_count * owned_orders * 2 * degrees * lat_dev * devices * group <= TABLE_CAP * 4
+        and piece * devices * lat_dev == wide
+        and piece % 16 == 0
+    )
+    terms = piece if small else 0
+    inner = (1, 1, lat_dev - 2)
+    outer = (0, lat_dev - 1, 2)
+
+    coefficients, first_row, last_row = transform(
+        place, features, forward_t, disco_rows, disco_cols, disco_basis
+    )
+    north, south = neighbours(first_row, last_row)
+    owned = exchange_rows(coefficients)
+
+    band_rows = position * lat_dev + jnp.arange(lat_dev, dtype=jnp.int32)[:, None]
+    basis = disco_basis.astype(F32)
+    offsets = disco_rows - band_rows
+    shifts = (offsets + 1) * WIN + SPAN + disco_cols
+    weight_rows = disco_weight.reshape(wide, channels)
+    mixed = filtered([features], None, None, shifts, basis, None, inner)
+    owned, mixed = lax.optimization_barrier((owned, mixed))
+    mixed = filtered([features], north, south, shifts, basis, None, outer, mixed)
 
     packed = jnp.concatenate(
         [
-            disco_rows.astype(F32)[:, None, :],
+            offsets.astype(F32)[:, None, :],
             disco_cols.astype(F32)[:, None, :],
-            jnp.transpose(disco_basis, (1, 0, 2)).astype(F32),
+            jnp.transpose(basis, (1, 0, 2)),
         ],
         axis=1,
     )
-    packed_north, packed_south = neighbours(packed[:HALO], packed[lat_dev - HALO :])
-    packed_all = jnp.concatenate([packed_north, packed, packed_south], axis=0)
-    band_rows = position * lat_dev + jnp.arange(lat_dev, dtype=jnp.int32)[:, None]
-    shifts = (disco_rows - band_rows + 1) * WIN + SPAN + disco_cols
-    rows_all = packed_all[:, 0].astype(jnp.int32)
-    cols_all = packed_all[:, 1].astype(jnp.int32)
+    packed_all = jnp.concatenate(
+        [
+            north[None, lon : lon + 2 + kernels, :taps].astype(F32),
+            packed,
+            south[None, lon : lon + 2 + kernels, :taps].astype(F32),
+        ],
+        axis=0,
+    )
     back_shifts = []
     back_taps = []
     for e in range(3):
-        aimed = rows_all[e : e + lat_dev] == band_rows
-        back_shifts.append(jnp.where(aimed, e * WIN + SPAN - cols_all[e : e + lat_dev], NONE))
+        aimed = packed_all[e : e + lat_dev, 0] == 1.0 - e
+        columns = packed_all[e : e + lat_dev, 1].astype(jnp.int32)
+        back_shifts.append(jnp.where(aimed, e * WIN + SPAN - columns, NONE))
         back_taps.append(jnp.transpose(packed_all[e : e + lat_dev, 2:], (1, 0, 2)))
     back_shifts = jnp.concatenate(back_shifts, axis=1)
     back_taps = jnp.concatenate(back_taps, axis=2)
-    weight_rows = disco_weight.reshape(kernels * channels, channels)
-    weight_back = jnp.transpose(disco_weight, (0, 2, 1)).reshape(kernels * channels, channels)
-
-    mixed, disco = filtered(
-        features, north, south, shifts, disco_basis.astype(F32), weight_rows, True
-    )
 
     if small:
         plain, weighted = legendre_table(order_count, degrees, lat_count)
@@ -643,17 +842,21 @@
             jnp.einsum("rlsi,rplc->srpic", plain, scaled, preferred_element_type=F32)
         )
 
-    returned = exchange(synthesized)
-    output, grad_total, grad_synth = activation(disco, returned, grad_output, inverse, inverse_t)
-    grad_owned = exchange(grad_synth)
-    grad_north, grad_south = neighbours(grad_total[:HALO], grad_total[lat_dev - HALO :])
-    weight_part = weight_terms(mixed, grad_total)
-
+    returned = exchange_rows(synthesized)
+    output, *blocks = activation(
+        mixed, weight_rows, returned, grad_output, inverse, inverse_t, devices, terms
+    )
+    grad_rows, blocks = blocks[:lat_dev], blocks[lat_dev:]
+    grad_north, grad_south = neighbours(grad_rows[0], grad_rows[-1])
+    part = filtered(grad_rows, None, None, back_shifts, back_taps, weight_rows, inner)
     if small:
-        gain_part, grad_coeff = spectral_adjoint(
-            place, grad_owned, plain, weighted, spectral_gain, analysed
+        grad_owned, part = lax.optimization_barrier((exchange(blocks[0]), part))
+        gain_part, grad_blocks = spectral_adjoint(
+            place, grad_owned, plain, weighted, spectral_gain, analysed, terms
         )
+        grad_bands = exchange(grad_blocks)
     else:
+        grad_owned = exchange_rows(blocks[0])
         grad_scaled = jnp.einsum(
             "rlsi,srpic->rplc", plain, opened(grad_owned), preferred_element_type=F32
         )
@@ -662,18 +865,19 @@
         grad_coeff = closed(
             jnp.einsum("rlsi,rplc->srpic", weighted, grad_analysed, preferred_element_type=F32)
         )
-
-    grad_bands = exchange(grad_coeff)
+        grad_bands = exchange_rows(grad_coeff)
+
     grad_disco = filtered(
-        grad_total, grad_north, grad_south, back_shifts, back_taps, weight_back, False
-    )
-    grad_features = final(grad_bands, forward, grad_disco)
-    grad_weight = sum_scatter_gather(weight_part).astype(F32)
-    grad_gain = sum_everywhere(gain_part)
+        grad_rows, grad_north, grad_south, back_shifts, back_taps, weight_rows, outer, part
+    )
+    grad_gain, grad_disco = sum_everywhere(gain_part, grad_disco)
+    grad_features, *grad_weight = final(grad_bands, forward, grad_disco, terms)
+    if not small:
+        grad_weight = [sum_scatter_gather(blocks[1]).astype(F32)]
     return (
         output,
         grad_features,
-        grad_weight.reshape(kernels, channels, channels),
+        grad_weight[0].reshape(kernels, channels, channels),
         grad_gain,
     )
 

time: 174 us -> 109 us (0.63)
  the two profiles are of different devices: /device:TPU:0 before, /device:TPU:4 now
where the time goes in v2:
time: 109 us; the launch traced here: 108 us
  Pallas kernels  46.9 us (43%)
  starting transfers between devices  39.8 us (37%)
  waiting for transfers between devices  15.2 us (14%)
  local copies, waits for them, and re-layouts  2.62 us (2%)
  other arithmetic  2.28 us (2%)
    all_to_all x4, starting transfers between devices, exchange(): lax.all_to_all(blocks, 'lat', split_axis=0, concat_axis=0, tiled=True)  23.6 us
    pallas_call x4, Pallas kernels, filtered(): pl.pallas_call(body, grid=(total,), in_specs=in_specs, out_specs=pl.Block...  23.1 us
    pallas_call x1, Pallas kernels, activation(): pl.pallas_call(body, grid=(lat_dev,), in_specs=[pl.BlockSpec((1, lon, wid...  10.3 us
    ppermute x2, waiting for transfers between devices, neighbours(): lax.ppermute(south_edge, 'lat', [(i, i + 1) for i in range(count - 1)])  9.24 us
    ppermute x6, starting transfers between devices, partner(): lax.ppermute(array, 'lat', [(i, i ^ by * stride) for i in range(count)])  6.31 us
    ppermute x2, starting transfers between devices, neighbours(): lax.ppermute(north_edge, 'lat', [(i + 1, i) for i in range(count - 1)])  5.51 us
    pallas_call x1, Pallas kernels, final(): pl.pallas_call(body, grid=(lat_dev,), in_specs=[first_spec, pl.BlockSpec(...  4.57 us
    ppermute x2, starting transfers between devices, neighbours(): lax.ppermute(south_edge, 'lat', [(i, i + 1) for i in range(count - 1)])  4.35 us
  transfers between devices with their start and end apart: 14, of which 6 were waited for; matrix products, arithmetic and copies ran while one was open for 2% of the time, Pallas kernels for 26%

profile of v2, /device:TPU:4, one launch (start us, length us, event | category | flops | bytes accessed | tf_op | source)
XLA Modules:
  0.0 107.7 jit_solution(7481496131705044043)
XLA Ops:
  0.7 3.8 %transform.1 = (bf16[128,768]{1,0:T(8,128)(2,1)}, bf16[1456,256]{1,0:T(8,128)(2,1)}, bf16[1456,256]{1,0:T(8,128)(2,1)}) custom-call(s32[1]{0:T(128)} %bitcast.p_ref, bf16[3,1440,256]{2,1,0:T(8,128)(2,1)} %rest_0_.3, bf16[128,1440]{1,0:T(8,128)(2,1)} %constant.36.clone.t_ref, s32[3,9]{1,0:T(4,128)} %row_ref.1, s32[3,9]{1,0:T(4,128)} %col_ref.1, ...), custom_call_target="tpu_custom_call" | custom-call | flops 283115520 | bytes 2211840 | tf_op jit(solution)/shard_map/transform/pallas_call | solution.py:243
  4.4 6.4 %all-to-all-start = ((bf16[16,8,768]{2,1,0:T(8,128)(2,1)}), bf16[16,8,768]{2,1,0:T(8,128)(2,1)S(1)}, u32[]{:S(2)}, u32[]{:S(2)}) async-start(bf16[16,8,768]{2,1,0:T(8,128)(2,1)} %bitcast.36), calls=%async_computation | async-start | bytes 393216 | tf_op jit(solution)/shard_map/all_to_all | solution.py:738
  10.8 2.0 %collective-permute-start = (bf16[1456,256]{1,0:T(8,128)(2,1)}, bf16[1456,256]{1,0:T(8,128)(2,1)S(1)}, u32[]{:S(2)}, u32[]{:S(2)}) collective-permute-start(bf16[1456,256]{1,0:T(8,128)(2,1)} %get-tuple-element.24), channel_id=1, source_target_pairs={{0,1},{1,2},{2,3},{3,4},{4,5},{5,6},{6,7},{7,8},{8,9},{9,10},{10,1... | collective-permute-start | bytes 2236424 | tf_op jit(solution)/shard_map/ppermute | solution.py:732
  12.9 3.5 %collective-permute-start.1 = (bf16[1456,256]{1,0:T(8,128)(2,1)}, bf16[1456,256]{1,0:T(8,128)(2,1)S(1)}, u32[]{:S(2)}, u32[]{:S(2)}) collective-permute-start(bf16[1456,256]{1,0:T(8,128)(2,1)} %get-tuple-element.25), channel_id=1, source_target_pairs={{1,0},{2,1},{3,2},{4,3},{5,4},{6,5},{7,6},{8,7},{9,8},{10,9},{11,1... | collective-permute-start | bytes 2236424 | tf_op jit(solution)/shard_map/ppermute | solution.py:733
  16.5 4.5 %filtered.2.rest_3_ = bf16[3,1440,768]{2,1,0:T(8,128)(2,1)} custom-call(s32[3,9]{1,0:T(4,128)S(1)} %get-tuple-element.49.shift_ref, f32[3,3,9]{2,1,0:T(4,128)S(1)} %get-tuple-element.51.tap_ref, bf16[3,1440,256]{2,1,0:T(8,128)(2,1)} %rest_0_.3), custom_call_target="tpu_custom_call" | custom-call | flops 530841600 | bytes 2949120 | tf_op jit(solution)/shard_map/filtered/pallas_call | solution.py:393
  21.0 2.4 %spectral_forward.1 = (f32[288,256]{1,0:T(8,128)}, bf16[128,768]{1,0:T(8,128)(2,1)}) custom-call(s32[1]{0:T(128)} %bitcast.p_ref, bf16[128,768]{1,0:T(8,128)(2,1)S(1)} %bitcast.31, bf16[16,288,384]{2,1,0:T(8,128)(2,1)} %constant.41.clone.a_ref, bf16[16,288,384]{2,1,0:T(8,128)(2,1)} %constant.40.clone.b_ref, f32[48,256]{1,0:T(8,128)} %g_ref.5), custom_call_target="tpu_custom_call" | custom-call | tf_op jit(solution)/shard_map/spectral_forward/pallas_call | solution.py:437
  23.5 6.0 %all-to-all-start.1 = ((bf16[16,8,768]{2,1,0:T(8,128)(2,1)}), bf16[16,8,768]{2,1,0:T(8,128)(2,1)S(1)}, u32[]{:S(2)}, u32[]{:S(2)}) async-start(bf16[16,8,768]{2,1,0:T(8,128)(2,1)} %bitcast.37), calls=%async_computation.1 | async-start | bytes 393216 | tf_op jit(solution)/shard_map/all_to_all | solution.py:738
  29.5 3.7 %collective-permute-done.rest_1_ = bf16[1456,256]{1,0:T(8,128)(2,1)S(1)} collective-permute-done((bf16[1456,256]{1,0:T(8,128)(2,1)}, bf16[1456,256]{1,0:T(8,128)(2,1)S(1)}, u32[]{:S(2)}, u32[]{:S(2)}) %collective-permute-start) | collective-permute-done | bytes 745504 | tf_op jit(solution)/shard_map/ppermute | solution.py:732
  33.2 0.9 copy-done
  34.0 0.9 copy-done.1
  34.9 5.7 %filtered.3.m_ref = bf16[3,1440,768]{2,1,0:T(8,128)(2,1)} custom-call(s32[3,9]{1,0:T(4,128)S(1)} %get-tuple-element.49.shift_ref, f32[3,3,9]{2,1,0:T(4,128)S(1)} %get-tuple-element.51.tap_ref, bf16[3,1440,256]{2,1,0:T(8,128)(2,1)} %rest_0_.3, bf16[1456,256]{1,0:T(8,128)(2,1)} %copy-done, ...), custom_call_target="tpu_custom_call", output_to_operand_aliasing={{}: (5, {})} | custom-call | flops 1061683200 | bytes 5898240 | tf_op jit(solution)/shard_map/filtered/pallas_call | solution.py:393
  40.6 10.3 %activation.1 = (bf16[3,1440,256]{2,1,0:T(8,128)(2,1)}, bf16[1440,256]{1,0:T(8,128)(2,1)}, bf16[1440,256]{1,0:T(8,128)(2,1)}, bf16[1440,256]{1,0:T(8,128)(2,1)}, bf16[16,24,768]{2,1,0:T(8,128)(2,1)}) custom-call(bf16[3,1440,768]{2,1,0:T(8,128)(2,1)} %filtered.3.m_ref, bf16[768,256]{1,0:T(8,128)(2,1)} %bitcast.33, bf16[128,768]{1,0:T(8,128)(2,1)S(1)} %bitcast.32, ...), custom_call_target="tpu_custom_call" | custom-call | flops 3963617280 | bytes 15482880 | tf_op jit(solution)/shard_map/activation/pallas_call | solution.py:610
  50.9 5.5 %all-to-all-start.2 = ((bf16[16,24,768]{2,1,0:T(8,128)(2,1)}), bf16[16,24,768]{2,1,0:T(8,128)(2,1)S(1)}, u32[]{:S(2)}, u32[]{:S(2)}) async-start(bf16[16,24,768]{2,1,0:T(8,128)(2,1)} %get-tuple-element.31), calls=%async_computation.2 | async-start | bytes 1179648 | tf_op jit(solution)/shard_map/all_to_all | solution.py:738
  56.4 0.7 fusion.9
  57.1 0.7 fusion.5
  57.8 2.0 %collective-permute-start.6 = (bf16[1440,256]{1,0:T(8,128)(2,1)}, bf16[1440,256]{1,0:T(8,128)(2,1)S(1)}, u32[]{:S(2)}, u32[]{:S(2)}) collective-permute-start(bf16[1440,256]{1,0:T(8,128)(2,1)} %get-tuple-element.32.rest_0_), channel_id=1, source_target_pairs={{1,0},{2,1},{3,2},{4,3},{5,4},{6,5},{7,6},{8,7},{9,8},{10,9},{11,1... | collective-permute-start | bytes 2211848 | tf_op jit(solution)/shard_map/ppermute | solution.py:733
  59.8 2.3 %collective-permute-start.5 = (bf16[1440,256]{1,0:T(8,128)(2,1)}, bf16[1440,256]{1,0:T(8,128)(2,1)S(1)}, u32[]{:S(2)}, u32[]{:S(2)}) collective-permute-start(bf16[1440,256]{1,0:T(8,128)(2,1)} %get-tuple-element.34.rest_2_), channel_id=1, source_target_pairs={{0,1},{1,2},{2,3},{3,4},{4,5},{5,6},{6,7},{7,8},{8,9},{9,10},{10,1... | collective-permute-start | bytes 2211848 | tf_op jit(solution)/shard_map/ppermute | solution.py:732
  62.3 5.3 %filtered_back.2.rest_6_ = bf16[3,1440,256]{2,1,0:T(8,128)(2,1)} custom-call(s32[3,27]{1,0:T(4,128)S(1)} %pad_add_fusion.shift_ref, f32[3,3,27]{2,1,0:T(4,128)S(1)} %pad_maximum_fusion.6.tap_ref, bf16[1440,256]{1,0:T(8,128)(2,1)} %get-tuple-element.32.rest_0_, bf16[1440,256]{1,0:T(8,128)(2,1)} %get-tuple-element.33.rest_1_, ...), custom_call_target="tpu_custom_call" | custom-call | flops 1097072640 | bytes 2949120 | tf_op jit(solution)/shard_map/filtered_back/pallas_call | solution.py:393
  67.7 3.1 %all-to-all-done.2.x_ref = bf16[16,24,768]{2,1,0:T(8,128)(2,1)S(1)} async-done(((bf16[16,24,768]{2,1,0:T(8,128)(2,1)}), bf16[16,24,768]{2,1,0:T(8,128)(2,1)S(1)}, u32[]{:S(2)}, u32[]{:S(2)}) %all-to-all-start.2) | async-done | bytes 589856 | tf_op jit(solution)/shard_map/all_to_all | solution.py:738
  70.7 2.7 %spectral_adjoint.1 = (f32[48,256]{1,0:T(8,128)S(1)}, bf16[16,24,768]{2,1,0:T(8,128)(2,1)}) custom-call(s32[1]{0:T(128)} %bitcast.p_ref, bf16[16,24,768]{2,1,0:T(8,128)(2,1)S(1)} %all-to-all-done.2.x_ref, bf16[16,288,384]{2,1,0:T(8,128)(2,1)} %constant.40.clone.b_ref, bf16[16,288,384]{2,1,0:T(8,128)(2,1)} %constant.41.clone.a_ref, f32[48,256]{1,0:T(8,128)} %g_ref.5, ...), custom_call_target="tpu_custom_call" | custom-call | tf_op jit(solution)/shard_map/spectral_adjoint/pallas_call | solution.py:494
  73.4 5.7 %all-to-all-start.3 = ((bf16[16,24,768]{2,1,0:T(8,128)(2,1)}), bf16[16,24,768]{2,1,0:T(8,128)(2,1)S(1)}, u32[]{:S(2)}, u32[]{:S(2)}) async-start(bf16[16,24,768]{2,1,0:T(8,128)(2,1)} %get-tuple-element.37), calls=%async_computation.3 | async-start | bytes 1179648 | tf_op jit(solution)/shard_map/all_to_all | solution.py:738
  79.3 1.7 %collective-permute-start.3 = (f32[48,256]{1,0:T(8,128)S(1)}, f32[48,256]{1,0:T(8,128)S(1)}, u32[]{:S(2)}, u32[]{:S(2)}) collective-permute-start(f32[48,256]{1,0:T(8,128)S(1)} %get-tuple-element.38), channel_id=1, source_target_pairs={{0,2},{1,3},{2,0},{3,1},{4,6},{5,7},{6,4},{7,5},{8,10},{9,11},{10,... | collective-permute-start | bytes 147464 | tf_op jit(solution)/shard_map/ppermute | solution.py:692
  81.1 5.6 %collective-permute-done.5.rest_3_ = bf16[1440,256]{1,0:T(8,128)(2,1)S(1)} collective-permute-done((bf16[1440,256]{1,0:T(8,128)(2,1)}, bf16[1440,256]{1,0:T(8,128)(2,1)S(1)}, u32[]{:S(2)}, u32[]{:S(2)}) %collective-permute-start.5) | collective-permute-done | bytes 737312 | tf_op jit(solution)/shard_map/ppermute | solution.py:732
  86.6 0.9 copy-done.3
  87.5 7.6 %filtered_back.3.d_ref = bf16[3,1440,256]{2,1,0:T(8,128)(2,1)} custom-call(s32[3,27]{1,0:T(4,128)S(1)} %pad_add_fusion.shift_ref, f32[3,3,27]{2,1,0:T(4,128)S(1)} %pad_maximum_fusion.6.tap_ref, bf16[1440,256]{1,0:T(8,128)(2,1)} %get-tuple-element.32.rest_0_, bf16[1440,256]{1,0:T(8,128)(2,1)} %get-tuple-element.33.rest_1_, ...), custom_call_target="tpu_custom_call", output_to_operand_aliasing={{}: (8, {})} | custom-call | flops 2194145280 | bytes 5898240 | tf_op jit(solution)/shard_map/filtered_back/pallas_call | solution.py:393
  95.2 3.2 %collective-permute-start.8 = (f32[48,256]{1,0:T(8,128)S(1)}, f32[48,256]{1,0:T(8,128)S(1)}, u32[]{:S(2)}, u32[]{:S(2)}) collective-permute-start(f32[48,256]{1,0:T(8,128)S(1)} %add_add_fusion.1), channel_id=1, source_target_pairs={{0,8},{1,9},{2,10},{3,11},{4,12},{5,13},{6,14},{7,15},{8,0},{9,1},... | collective-permute-start | bytes 147464 | tf_op jit(solution)/shard_map/ppermute | solution.py:692
  98.4 1.2 %collective-permute-start.7 = (f32[48,256]{1,0:T(8,128)S(1)}, f32[48,256]{1,0:T(8,128)S(1)}, u32[]{:S(2)}, u32[]{:S(2)}) collective-permute-start(f32[48,256]{1,0:T(8,128)S(1)} %add_add_fusion.1), channel_id=1, source_target_pairs={{0,4},{1,5},{2,6},{3,7},{4,0},{5,1},{6,2},{7,3},{8,12},{9,13},{10,... | collective-permute-start | bytes 147464 | tf_op jit(solution)/shard_map/ppermute | solution.py:692
  99.5 1.6 %collective-permute-done.9 = f32[48,256]{1,0:T(8,128)S(1)} collective-permute-done((f32[48,256]{1,0:T(8,128)S(1)}, f32[48,256]{1,0:T(8,128)S(1)}, u32[]{:S(2)}, u32[]{:S(2)}) %collective-permute-start.9) | collective-permute-done | bytes 49184 | tf_op jit(solution)/shard_map/ppermute | solution.py:692
  101.1 0.3 collective-permute-done.8
  101.4 1.0 collective-permute-done.7
  102.5 0.6 add_add_fusion
  103.1 4.6 %final.1 = (bf16[3,1440,256]{2,1,0:T(8,128)(2,1)}, f32[16,3,16,256]{3,2,1,0:T(8,128)}) custom-call(bf16[16,24,768]{2,1,0:T(8,128)(2,1)S(1)} %all-to-all-done.3.y_ref, bf16[1440,128]{1,0:T(8,128)(2,1)} %constant.38.clone.f_ref, bf16[3,1440,256]{2,1,0:T(8,128)(2,1)} %filtered_back.3.d_ref), custom_call_target="tpu_custom_call" | custom-call | flops 283115520 | bytes 6635520 | tf_op jit(solution)/shard_map/final/pallas_call | solution.py:669
  (32 shorter events, 0.6 us)
Async XLA Ops:
  0.6 15.8 %copy-start.4 = (bf16[3,3,9]{2,1,0:T(4,128)(2,1)S(1)}, bf16[3,3,9]{2,1,0:T(4,128)(2,1)}, u32[]{:S(2)}) copy-start(bf16[3,3,9]{2,1,0:T(4,128)(2,1)} %basis_ref.1) | copy-start | bytes 490
  0.6 15.7 %copy-start.5 = (s32[3,9]{1,0:T(4,128)S(1)}, s32[3,9]{1,0:T(4,128)}, u32[]{:S(2)}) copy-start(s32[3,9]{1,0:T(4,128)} %col_ref.1) | copy-start | bytes 328
  0.7 15.7 %copy-start.6 = (s32[3,9]{1,0:T(4,128)S(1)}, s32[3,9]{1,0:T(4,128)}, u32[]{:S(2)}) copy-start(s32[3,9]{1,0:T(4,128)} %row_ref.1) | copy-start | bytes 328
  4.4 16.6 %all-to-all-start = ((bf16[16,8,768]{2,1,0:T(8,128)(2,1)}), bf16[16,8,768]{2,1,0:T(8,128)(2,1)S(1)}, u32[]{:S(2)}, u32[]{:S(2)}) async-start(bf16[16,8,768]{2,1,0:T(8,128)(2,1)} %bitcast.36), calls=%async_computation | async-start | bytes 393216 | tf_op jit(solution)/shard_map/all_to_all | solution.py:738
  10.8 22.4 %collective-permute-start = (bf16[1456,256]{1,0:T(8,128)(2,1)}, bf16[1456,256]{1,0:T(8,128)(2,1)S(1)}, u32[]{:S(2)}, u32[]{:S(2)}) collective-permute-start(bf16[1456,256]{1,0:T(8,128)(2,1)} %get-tuple-element.24), channel_id=1, source_target_pairs={{0,1},{1,2},{2,3},{3,4},{4,5},{5,6},{6,7},{7,8},{8,9},{9,10},{10,1... | collective-permute-start | bytes 2236424 | tf_op jit(solution)/shard_map/ppermute | solution.py:732
  12.9 20.3 %collective-permute-start.1 = (bf16[1456,256]{1,0:T(8,128)(2,1)}, bf16[1456,256]{1,0:T(8,128)(2,1)S(1)}, u32[]{:S(2)}, u32[]{:S(2)}) collective-permute-start(bf16[1456,256]{1,0:T(8,128)(2,1)} %get-tuple-element.25), channel_id=1, source_target_pairs={{1,0},{2,1},{3,2},{4,3},{5,4},{6,5},{7,6},{8,7},{9,8},{10,9},{11,1... | collective-permute-start | bytes 2236424 | tf_op jit(solution)/shard_map/ppermute | solution.py:733
  23.5 17.1 %all-to-all-start.1 = ((bf16[16,8,768]{2,1,0:T(8,128)(2,1)}), bf16[16,8,768]{2,1,0:T(8,128)(2,1)S(1)}, u32[]{:S(2)}, u32[]{:S(2)}) async-start(bf16[16,8,768]{2,1,0:T(8,128)(2,1)} %bitcast.37), calls=%async_computation.1 | async-start | bytes 393216 | tf_op jit(solution)/shard_map/all_to_all | solution.py:738
  33.2 0.9 copy-start
  34.0 0.9 copy-start.1
  50.9 19.8 %all-to-all-start.2 = ((bf16[16,24,768]{2,1,0:T(8,128)(2,1)}), bf16[16,24,768]{2,1,0:T(8,128)(2,1)S(1)}, u32[]{:S(2)}, u32[]{:S(2)}) async-start(bf16[16,24,768]{2,1,0:T(8,128)(2,1)} %get-tuple-element.31), calls=%async_computation.2 | async-start | bytes 1179648 | tf_op jit(solution)/shard_map/all_to_all | solution.py:738
  57.8 23.2 %collective-permute-start.6 = (bf16[1440,256]{1,0:T(8,128)(2,1)}, bf16[1440,256]{1,0:T(8,128)(2,1)S(1)}, u32[]{:S(2)}, u32[]{:S(2)}) collective-permute-start(bf16[1440,256]{1,0:T(8,128)(2,1)} %get-tuple-element.32.rest_0_), channel_id=1, source_target_pairs={{1,0},{2,1},{3,2},{4,3},{5,4},{6,5},{7,6},{8,7},{9,8},{10,9},{11,1... | collective-permute-start | bytes 2211848 | tf_op jit(solution)/shard_map/ppermute | solution.py:733
  59.8 26.8 %collective-permute-start.5 = (bf16[1440,256]{1,0:T(8,128)(2,1)}, bf16[1440,256]{1,0:T(8,128)(2,1)S(1)}, u32[]{:S(2)}, u32[]{:S(2)}) collective-permute-start(bf16[1440,256]{1,0:T(8,128)(2,1)} %get-tuple-element.34.rest_2_), channel_id=1, source_target_pairs={{0,1},{1,2},{2,3},{3,4},{4,5},{5,6},{6,7},{7,8},{8,9},{9,10},{10,1... | collective-permute-start | bytes 2211848 | tf_op jit(solution)/shard_map/ppermute | solution.py:732
  73.4 29.7 %all-to-all-start.3 = ((bf16[16,24,768]{2,1,0:T(8,128)(2,1)}), bf16[16,24,768]{2,1,0:T(8,128)(2,1)S(1)}, u32[]{:S(2)}, u32[]{:S(2)}) async-start(bf16[16,24,768]{2,1,0:T(8,128)(2,1)} %get-tuple-element.37), calls=%async_computation.3 | async-start | bytes 1179648 | tf_op jit(solution)/shard_map/all_to_all | solution.py:738
  79.2 15.9 %collective-permute-start.4 = (f32[48,256]{1,0:T(8,128)S(1)}, f32[48,256]{1,0:T(8,128)S(1)}, u32[]{:S(2)}, u32[]{:S(2)}) collective-permute-start(f32[48,256]{1,0:T(8,128)S(1)} %get-tuple-element.38), channel_id=1, source_target_pairs={{0,3},{1,2},{2,1},{3,0},{4,7},{5,6},{6,5},{7,4},{8,11},{9,10},{10,... | collective-permute-start | bytes 147464 | tf_op jit(solution)/shard_map/ppermute | solution.py:692
  79.3 15.7 %collective-permute-start.3 = (f32[48,256]{1,0:T(8,128)S(1)}, f32[48,256]{1,0:T(8,128)S(1)}, u32[]{:S(2)}, u32[]{:S(2)}) collective-permute-start(f32[48,256]{1,0:T(8,128)S(1)} %get-tuple-element.38), channel_id=1, source_target_pairs={{0,2},{1,3},{2,0},{3,1},{4,6},{5,7},{6,4},{7,5},{8,10},{9,11},{10,... | collective-permute-start | bytes 147464 | tf_op jit(solution)/shard_map/ppermute | solution.py:692
  81.0 14.1 %collective-permute-start.2 = (f32[48,256]{1,0:T(8,128)S(1)}, f32[48,256]{1,0:T(8,128)S(1)}, u32[]{:S(2)}, u32[]{:S(2)}) collective-permute-start(f32[48,256]{1,0:T(8,128)S(1)} %get-tuple-element.38), channel_id=1, source_target_pairs={{0,1},{1,0},{2,3},{3,2},{4,5},{5,4},{6,7},{7,6},{8,9},{9,8},{10,11... | collective-permute-start | bytes 147464 | tf_op jit(solution)/shard_map/ppermute | solution.py:692
  81.0 5.6 %copy-start.2 = (bf16[1440,256]{1,0:T(8,128)(2,1)}, bf16[1440,256]{1,0:T(8,128)(2,1)S(1)}, u32[]{:S(2)}) copy-start(bf16[1440,256]{1,0:T(8,128)(2,1)S(1)} %collective-permute-done.6.rest_4_) | copy-start | bytes 2211844
  86.6 0.9 copy-start.3
  95.1 6.1 %collective-permute-start.9 = (f32[48,256]{1,0:T(8,128)S(1)}, f32[48,256]{1,0:T(8,128)S(1)}, u32[]{:S(2)}, u32[]{:S(2)}) collective-permute-start(f32[48,256]{1,0:T(8,128)S(1)} %add_add_fusion.1), channel_id=1, source_target_pairs={{0,12},{1,13},{2,14},{3,15},{4,8},{5,9},{6,10},{7,11},{8,4},{9,5},... | collective-permute-start | bytes 147464 | tf_op jit(solution)/shard_map/ppermute | solution.py:692
  95.2 6.2 %collective-permute-start.8 = (f32[48,256]{1,0:T(8,128)S(1)}, f32[48,256]{1,0:T(8,128)S(1)}, u32[]{:S(2)}, u32[]{:S(2)}) collective-permute-start(f32[48,256]{1,0:T(8,128)S(1)} %add_add_fusion.1), channel_id=1, source_target_pairs={{0,8},{1,9},{2,10},{3,11},{4,12},{5,13},{6,14},{7,15},{8,0},{9,1},... | collective-permute-start | bytes 147464 | tf_op jit(solution)/shard_map/ppermute | solution.py:692
  98.4 4.1 %collective-permute-start.7 = (f32[48,256]{1,0:T(8,128)S(1)}, f32[48,256]{1,0:T(8,128)S(1)}, u32[]{:S(2)}, u32[]{:S(2)}) collective-permute-start(f32[48,256]{1,0:T(8,128)S(1)} %add_add_fusion.1), channel_id=1, source_target_pairs={{0,4},{1,5},{2,6},{3,7},{4,0},{5,1},{6,2},{7,3},{8,12},{9,13},{10,... | collective-permute-start | bytes 147464 | tf_op jit(solution)/shard_map/ppermute | solution.py:692

commit v3 on v2

--- a/solution.py
+++ b/solution.py
@@ -205,7 +205,8 @@
             pltpu.make_async_copy(ref, to, small_sem.at[n])
             for n, (ref, to) in enumerate(zip((row_ref, col_ref, basis_ref), small_held, strict=True))
         ]
-        for copy in [*small_copies, table_copy, *copies]:
+        order = edges + tuple(i for i in range(lat_dev) if i not in edges)
+        for copy in [*small_copies, table_copy, *(copies[i] for i in order)]:
             copy.start()
         for copy in small_copies:
             copy.wait()
@@ -226,8 +227,8 @@
             )
             sent[-1].start()
         table_copy.wait()
-        for i, copy in enumerate(copies):
-            copy.wait()
+        for i in order:
+            copies[i].wait()
             for n, edge in enumerate(edges):
                 if i == edge:
                     sent.append(
@@ -379,7 +380,7 @@
         pltpu.SemaphoreType.DMA((lat_dev + 2, 3)),
     ]
     if edges:
-        operands += [in_hbm(north), in_hbm(south)]
+        operands += [north, south]
         in_specs += [ANYWHERE, ANYWHERE]
     if not keep:
         operands.append(in_hbm(weights))
@@ -646,32 +647,63 @@
 
 def final(received, forward, grad_disco, terms):
     lat_dev, lon, channels = grad_disco.shape
-    row_spec = pl.BlockSpec((1, lon, channels), lambda i: (i, 0, 0))
-    out_specs = [row_spec]
+    depth = forward.shape[1]
+
+    def body(y_ref, f_ref, d_ref, o_ref, *rest):
+        w_ref = rest[0] if terms else None
+        f_held, d_held, o_held, f_sem, d_sem, o_sem = rest[-7:-1]
+        w_held = rest[-1]
+        table = pltpu.make_async_copy(f_ref, f_held, f_sem)
+        incoming = [
+            pltpu.make_async_copy(d_ref.at[i], d_held.at[i], d_sem.at[i]) for i in range(lat_dev)
+        ]
+        outgoing = [
+            pltpu.make_async_copy(o_held.at[i], o_ref.at[i], o_sem.at[i]) for i in range(lat_dev)
+        ]
+        table.start()
+        for copy in incoming:
+            copy.start()
+        if terms:
+            for i in range(lat_dev):
+                w_held[:, i] = y_ref[:, 0:terms, i * channels : (i + 1) * channels].astype(F32)
+            outgoing.append(pltpu.make_async_copy(w_held, w_ref, o_sem.at[lat_dev]))
+            outgoing[-1].start()
+        table.wait()
+        for i in range(lat_dev):
+            lanes = slice(i * channels, (i + 1) * channels)
+            if terms:
+                bands = blocks_of(y_ref, terms, y_ref.shape[1] - terms, lanes)
+            else:
+                bands = y_ref[:, lanes]
+            incoming[i].wait()
+            for c in range(lon // CHUNK):
+                place = slice(c * CHUNK, (c + 1) * CHUNK)
+                o_held[i, place, :] = (
+                    d_held[i, place, :].astype(F32) + dot(f_held[place, :], bands)
+                ).astype(BF16)
+            outgoing[i].start()
+        for copy in outgoing:
+            copy.wait()
+
     out_shape = [pltpu.HBM((lat_dev, lon, channels), BF16)]
+    gathered = (16, 128)
     if terms:
-        devices, block_rows, _ = received.shape
-        first_spec = pl.BlockSpec((devices, block_rows, channels), lambda i: (0, 0, i))
-        out_specs.append(pl.BlockSpec((devices, 1, terms, channels), lambda i: (0, i, 0, 0)))
-        out_shape.append(pltpu.HBM((devices, lat_dev, terms, channels), F32))
-    else:
-        first_spec = pl.BlockSpec((received.shape[0], channels), lambda i: (0, i))
-    depth = forward.shape[1]
-
-    def body(y_ref, f_ref, d_ref, o_ref, *rest):
-        if terms:
-            rest[0][:, 0] = y_ref[:, 0:terms, :].astype(F32)
-            bands = blocks_of(y_ref, terms, block_rows - terms, slice(0, channels))
-        else:
-            bands = y_ref[...]
-        o_ref[0] = (d_ref[0].astype(F32) + dot(f_ref[...], bands)).astype(BF16)
-
+        gathered = (received.shape[0], lat_dev, terms, channels)
+        out_shape.append(pltpu.HBM(gathered, F32))
     return pl.pallas_call(
         body,
-        grid=(lat_dev,),
-        in_specs=[first_spec, pl.BlockSpec((lon, depth), lambda i: (0, 0)), row_spec],
-        out_specs=out_specs,
+        in_specs=[VMEM, ANYWHERE, ANYWHERE],
+        out_specs=[ANYWHERE] * len(out_shape),
         out_shape=out_shape,
+        scratch_shapes=[
+            pltpu.VMEM((lon, depth), BF16),
+            pltpu.VMEM((lat_dev, lon, channels), BF16),
+            pltpu.VMEM((lat_dev, lon, channels), BF16),
+            pltpu.SemaphoreType.DMA,
+            pltpu.SemaphoreType.DMA((lat_dev,)),
+            pltpu.SemaphoreType.DMA((lat_dev + 1,)),
+            pltpu.VMEM(gathered, F32),
+        ],
         compiler_params=params(24),
         cost_estimate=cost(2 * grad_disco.size * depth, grad_disco.size * 6),
         name="final",
@@ -714,17 +746,20 @@
     return array
 
 
-def sum_everywhere(array, between):
+def sum_everywhere(array, between, then):
     count = lax.axis_size("lat")
     plan = stages(count)
     for n, (stride, factor) in enumerate(plan):
-        if n == len(plan) - 1:
+        last = n == len(plan) - 1
+        if last:
             array, between = lax.optimization_barrier((array, between))
         parts = [array] + [partner(array, count, stride, by) for by in range(1, factor)]
+        if last:
+            parts, result = lax.optimization_barrier((parts, then(between)))
         while len(parts) > 1:
             parts = [parts[k] + parts[k + 1] for k in range(0, len(parts), 2)]
         array = parts[0]
-    return (array, between)
+    return (array, result)
 
 
 def neighbours(north_edge, south_edge):
@@ -870,8 +905,9 @@
     grad_disco = filtered(
         grad_rows, grad_north, grad_south, back_shifts, back_taps, weight_rows, outer, part
     )
-    grad_gain, grad_disco = sum_everywhere(gain_part, grad_disco)
-    grad_features, *grad_weight = final(grad_bands, forward, grad_disco, terms)
+    grad_gain, (grad_features, *grad_weight) = sum_everywhere(
+        gain_part, grad_disco, lambda held: final(grad_bands, forward, held, terms)
+    )
     if not small:
         grad_weight = [sum_scatter_gather(blocks[1]).astype(F32)]
     return (

time: 109 us -> 101 us (0.927)
  the two profiles are of different devices: /device:TPU:4 before, /device:TPU:0 now
where the time goes in v3:
time: 101 us; the launch traced here: 100 us
  Pallas kernels  45.4 us (45%)
  starting transfers between devices  40.3 us (40%)
  waiting for transfers between devices  12.8 us (13%)
    all_to_all x4, starting transfers between devices, exchange(): lax.all_to_all(blocks, 'lat', split_axis=0, concat_axis=0, tiled=True)  25.7 us
    pallas_call x4, Pallas kernels, filtered(): pl.pallas_call(body, grid=(total,), in_specs=in_specs, out_specs=pl.Block...  23 us
    all_to_all x4, waiting for transfers between devices, exchange(): lax.all_to_all(blocks, 'lat', split_axis=0, concat_axis=0, tiled=True)  11.1 us
    pallas_call x1, Pallas kernels, activation(): pl.pallas_call(body, grid=(lat_dev,), in_specs=[pl.BlockSpec((1, lon, wid...  10.3 us
    ppermute x6, starting transfers between devices, partner(): lax.ppermute(array, 'lat', [(i, i ^ by * stride) for i in range(count)])  6.58 us
    ppermute x2, starting transfers between devices, neighbours(): lax.ppermute(south_edge, 'lat', [(i, i + 1) for i in range(count - 1)])  5.42 us
    pallas_call x1, Pallas kernels, final(): pl.pallas_call(body, in_specs=[VMEM, ANYWHERE, ANYWHERE], out_specs=[ANYW...  3.66 us
    pallas_call x1, Pallas kernels, transform(): pl.pallas_call(body, in_specs=[SMEM] + [ANYWHERE] * 5, out_specs=[VMEM, A...  3.41 us
  transfers between devices with their start and end apart: 14, of which 5 were waited for; matrix products, arithmetic and copies ran while one was open for 0% of the time, Pallas kernels for 32%

profile of v3, /device:TPU:0, one launch (start us, length us, event | category | flops | bytes accessed | tf_op | source)
XLA Modules:
  0.0 100.4 jit_solution(10850917242605921955)
XLA Ops:
  0.7 3.4 %transform.1 = (bf16[128,768]{1,0:T(8,128)(2,1)}, bf16[1456,256]{1,0:T(8,128)(2,1)}, bf16[1456,256]{1,0:T(8,128)(2,1)}) custom-call(s32[1]{0:T(128)} %bitcast.p_ref, bf16[3,1440,256]{2,1,0:T(8,128)(2,1)} %rest_0_.3, bf16[128,1440]{1,0:T(8,128)(2,1)} %constant.36.clone.t_ref, s32[3,9]{1,0:T(4,128)} %row_ref.1, s32[3,9]{1,0:T(4,128)} %col_ref.1, ...), custom_call_target="tpu_custom_call" | custom-call | flops 283115520 | bytes 2211840 | tf_op jit(solution)/shard_map/transform/pallas_call | solution.py:244
  4.1 7.4 %all-to-all-start = ((bf16[16,8,768]{2,1,0:T(8,128)(2,1)}), bf16[16,8,768]{2,1,0:T(8,128)(2,1)S(1)}, u32[]{:S(2)}, u32[]{:S(2)}) async-start(bf16[16,8,768]{2,1,0:T(8,128)(2,1)} %bitcast.36), calls=%async_computation | async-start | bytes 393216 | tf_op jit(solution)/shard_map/all_to_all | solution.py:773
  11.5 2.3 %collective-permute-start = (bf16[1456,256]{1,0:T(8,128)(2,1)}, bf16[1456,256]{1,0:T(8,128)(2,1)S(1)}, u32[]{:S(2)}, u32[]{:S(2)}) collective-permute-start(bf16[1456,256]{1,0:T(8,128)(2,1)} %get-tuple-element.30), channel_id=1, source_target_pairs={{0,1},{1,2},{2,3},{3,4},{4,5},{5,6},{6,7},{7,8},{8,9},{9,10},{10,1... | collective-permute-start | bytes 2236424 | tf_op jit(solution)/shard_map/ppermute | solution.py:767
  13.8 1.3 %collective-permute-start.1 = (bf16[1456,256]{1,0:T(8,128)(2,1)}, bf16[1456,256]{1,0:T(8,128)(2,1)S(1)}, u32[]{:S(2)}, u32[]{:S(2)}) collective-permute-start(bf16[1456,256]{1,0:T(8,128)(2,1)} %get-tuple-element.31), channel_id=1, source_target_pairs={{1,0},{2,1},{3,2},{4,3},{5,4},{6,5},{7,6},{8,7},{9,8},{10,9},{11,1... | collective-permute-start | bytes 2236424 | tf_op jit(solution)/shard_map/ppermute | solution.py:768
  15.2 0.1 subtract_select_fusion
  15.3 4.5 %filtered.2.rest_3_ = bf16[3,1440,768]{2,1,0:T(8,128)(2,1)} custom-call(s32[3,9]{1,0:T(4,128)S(1)} %get-tuple-element.61.shift_ref, f32[3,3,9]{2,1,0:T(4,128)S(1)} %get-tuple-element.63.tap_ref, bf16[3,1440,256]{2,1,0:T(8,128)(2,1)} %rest_0_.3), custom_call_target="tpu_custom_call" | custom-call | flops 530841600 | bytes 2949120 | tf_op jit(solution)/shard_map/filtered/pallas_call | solution.py:394
  19.8 0.7 all-to-all-done
  20.5 2.4 %spectral_forward.1 = (f32[288,256]{1,0:T(8,128)}, bf16[128,768]{1,0:T(8,128)(2,1)}) custom-call(s32[1]{0:T(128)} %bitcast.p_ref, bf16[128,768]{1,0:T(8,128)(2,1)S(1)} %bitcast.31, bf16[16,288,384]{2,1,0:T(8,128)(2,1)} %constant.41.clone.a_ref, bf16[16,288,384]{2,1,0:T(8,128)(2,1)} %constant.40.clone.b_ref, f32[48,256]{1,0:T(8,128)} %g_ref.5), custom_call_target="tpu_custom_call" | custom-call | tf_op jit(solution)/shard_map/spectral_forward/pallas_call | solution.py:438
  22.9 7.2 %all-to-all-start.1 = ((bf16[16,8,768]{2,1,0:T(8,128)(2,1)}), bf16[16,8,768]{2,1,0:T(8,128)(2,1)S(1)}, u32[]{:S(2)}, u32[]{:S(2)}) async-start(bf16[16,8,768]{2,1,0:T(8,128)(2,1)} %bitcast.37), calls=%async_computation.1 | async-start | bytes 393216 | tf_op jit(solution)/shard_map/all_to_all | solution.py:773
  30.2 5.6 %filtered.3.m_ref = bf16[3,1440,768]{2,1,0:T(8,128)(2,1)} custom-call(s32[3,9]{1,0:T(4,128)S(1)} %get-tuple-element.61.shift_ref, f32[3,3,9]{2,1,0:T(4,128)S(1)} %get-tuple-element.63.tap_ref, bf16[3,1440,256]{2,1,0:T(8,128)(2,1)} %rest_0_.3, bf16[1456,256]{1,0:T(8,128)(2,1)S(1)} %collective-permute-done.rest_1_, ...), custom_call_target="tpu_custom_call", output_to_operand_aliasing={{}: (5, {})} | custom-call | flops 1061683200 | bytes 5898240 | tf_op jit(solution)/shard_map/filtered/pallas_call | solution.py:394
  35.7 3.4 %all-to-all-done.1 = bf16[16,8,768]{2,1,0:T(8,128)(2,1)S(1)} async-done(((bf16[16,8,768]{2,1,0:T(8,128)(2,1)}), bf16[16,8,768]{2,1,0:T(8,128)(2,1)S(1)}, u32[]{:S(2)}, u32[]{:S(2)}) %all-to-all-start.1) | async-done | bytes 196640 | tf_op jit(solution)/shard_map/all_to_all | solution.py:773
  39.1 10.3 %activation.1 = (bf16[3,1440,256]{2,1,0:T(8,128)(2,1)}, bf16[1440,256]{1,0:T(8,128)(2,1)}, bf16[1440,256]{1,0:T(8,128)(2,1)}, bf16[1440,256]{1,0:T(8,128)(2,1)}, bf16[16,24,768]{2,1,0:T(8,128)(2,1)}) custom-call(bf16[3,1440,768]{2,1,0:T(8,128)(2,1)} %filtered.3.m_ref, bf16[768,256]{1,0:T(8,128)(2,1)} %bitcast.33, bf16[128,768]{1,0:T(8,128)(2,1)S(1)} %bitcast.32, ...), custom_call_target="tpu_custom_call" | custom-call | flops 3963617280 | bytes 15482880 | tf_op jit(solution)/shard_map/activation/pallas_call | solution.py:611
  49.4 6.7 %all-to-all-start.2 = ((bf16[16,24,768]{2,1,0:T(8,128)(2,1)}), bf16[16,24,768]{2,1,0:T(8,128)(2,1)S(1)}, u32[]{:S(2)}, u32[]{:S(2)}) async-start(bf16[16,24,768]{2,1,0:T(8,128)(2,1)} %get-tuple-element.37), calls=%async_computation.2 | async-start | bytes 1179648 | tf_op jit(solution)/shard_map/all_to_all | solution.py:773
  56.1 1.3 %collective-permute-start.6 = (bf16[1440,256]{1,0:T(8,128)(2,1)}, bf16[1440,256]{1,0:T(8,128)(2,1)S(1)}, u32[]{:S(2)}, u32[]{:S(2)}) collective-permute-start(bf16[1440,256]{1,0:T(8,128)(2,1)} %get-tuple-element.38.rest_0_), channel_id=1, source_target_pairs={{1,0},{2,1},{3,2},{4,3},{5,4},{6,5},{7,6},{8,7},{9,8},{10,9},{11,1... | collective-permute-start | bytes 2211848 | tf_op jit(solution)/shard_map/ppermute | solution.py:768
  57.4 3.1 %collective-permute-start.5 = (bf16[1440,256]{1,0:T(8,128)(2,1)}, bf16[1440,256]{1,0:T(8,128)(2,1)S(1)}, u32[]{:S(2)}, u32[]{:S(2)}) collective-permute-start(bf16[1440,256]{1,0:T(8,128)(2,1)} %get-tuple-element.40.rest_2_), channel_id=1, source_target_pairs={{0,1},{1,2},{2,3},{3,4},{4,5},{5,6},{6,7},{7,8},{8,9},{9,10},{10,1... | collective-permute-start | bytes 2211848 | tf_op jit(solution)/shard_map/ppermute | solution.py:767
  60.5 0.1 pad_add_fusion.shift_ref
  60.6 0.1 pad_maximum_fusion.6.tap_ref
  60.7 5.3 %filtered_back.2.rest_6_ = bf16[3,1440,256]{2,1,0:T(8,128)(2,1)} custom-call(s32[3,27]{1,0:T(4,128)S(1)} %pad_add_fusion.shift_ref, f32[3,3,27]{2,1,0:T(4,128)S(1)} %pad_maximum_fusion.6.tap_ref, bf16[1440,256]{1,0:T(8,128)(2,1)} %get-tuple-element.38.rest_0_, bf16[1440,256]{1,0:T(8,128)(2,1)} %get-tuple-element.39.rest_1_, ...), custom_call_target="tpu_custom_call" | custom-call | flops 1097072640 | bytes 2949120 | tf_op jit(solution)/shard_map/filtered_back/pallas_call | solution.py:394
  66.0 5.6 %all-to-all-done.2.x_ref = bf16[16,24,768]{2,1,0:T(8,128)(2,1)S(1)} async-done(((bf16[16,24,768]{2,1,0:T(8,128)(2,1)}), bf16[16,24,768]{2,1,0:T(8,128)(2,1)S(1)}, u32[]{:S(2)}, u32[]{:S(2)}) %all-to-all-start.2) | async-done | bytes 589856 | tf_op jit(solution)/shard_map/all_to_all | solution.py:773
  71.6 2.7 %spectral_adjoint.1 = (f32[48,256]{1,0:T(8,128)S(1)}, bf16[16,24,768]{2,1,0:T(8,128)(2,1)}) custom-call(s32[1]{0:T(128)} %bitcast.p_ref, bf16[16,24,768]{2,1,0:T(8,128)(2,1)S(1)} %all-to-all-done.2.x_ref, bf16[16,288,384]{2,1,0:T(8,128)(2,1)} %constant.40.clone.b_ref, bf16[16,288,384]{2,1,0:T(8,128)(2,1)} %constant.41.clone.a_ref, f32[48,256]{1,0:T(8,128)} %g_ref.5, ...), custom_call_target="tpu_custom_call" | custom-call | tf_op jit(solution)/shard_map/spectral_adjoint/pallas_call | solution.py:495
  74.3 4.5 %all-to-all-start.3 = ((bf16[16,24,768]{2,1,0:T(8,128)(2,1)}), bf16[16,24,768]{2,1,0:T(8,128)(2,1)S(1)}, u32[]{:S(2)}, u32[]{:S(2)}) async-start(bf16[16,24,768]{2,1,0:T(8,128)(2,1)} %get-tuple-element.46), calls=%async_computation.3 | async-start | bytes 1179648 | tf_op jit(solution)/shard_map/all_to_all | solution.py:773
  78.8 1.7 %collective-permute-start.4 = (f32[48,256]{1,0:T(8,128)S(1)}, f32[48,256]{1,0:T(8,128)S(1)}, u32[]{:S(2)}, u32[]{:S(2)}) collective-permute-start(f32[48,256]{1,0:T(8,128)S(1)} %get-tuple-element.43), channel_id=1, source_target_pairs={{0,3},{1,2},{2,1},{3,0},{4,7},{5,6},{6,5},{7,4},{8,11},{9,10},{10,... | collective-permute-start | bytes 147464 | tf_op jit(solution)/shard_map/ppermute | solution.py:724
  80.5 0.4 collective-permute-start.3
  80.9 0.0 collective-permute-start.2
  80.9 0.0 collective-permute-done.6.rest_4_
  80.9 7.5 %filtered_back.3.d_ref = bf16[3,1440,256]{2,1,0:T(8,128)(2,1)} custom-call(s32[3,27]{1,0:T(4,128)S(1)} %pad_add_fusion.shift_ref, f32[3,3,27]{2,1,0:T(4,128)S(1)} %pad_maximum_fusion.6.tap_ref, bf16[1440,256]{1,0:T(8,128)(2,1)} %get-tuple-element.38.rest_0_, bf16[1440,256]{1,0:T(8,128)(2,1)} %get-tuple-element.39.rest_1_, ...), custom_call_target="tpu_custom_call", output_to_operand_aliasing={{}: (8, {})} | custom-call | flops 2194145280 | bytes 5898240 | tf_op jit(solution)/shard_map/filtered_back/pallas_call | solution.py:394
  88.6 3.7 %collective-permute-start.9 = (f32[48,256]{1,0:T(8,128)S(1)}, f32[48,256]{1,0:T(8,128)S(1)}, u32[]{:S(2)}, u32[]{:S(2)}) collective-permute-start(f32[48,256]{1,0:T(8,128)S(1)} %add_add_fusion.1), channel_id=1, source_target_pairs={{0,12},{1,13},{2,14},{3,15},{4,8},{5,9},{6,10},{7,11},{8,4},{9,5},... | collective-permute-start | bytes 147464 | tf_op jit(solution)/shard_map/ppermute | solution.py:724
  92.2 0.8 collective-permute-start.7
  93.0 1.3 %all-to-all-done.3.y_ref = bf16[16,24,768]{2,1,0:T(8,128)(2,1)S(1)} async-done(((bf16[16,24,768]{2,1,0:T(8,128)(2,1)}), bf16[16,24,768]{2,1,0:T(8,128)(2,1)S(1)}, u32[]{:S(2)}, u32[]{:S(2)}) %all-to-all-start.3) | async-done | bytes 589856 | tf_op jit(solution)/shard_map/all_to_all | solution.py:773
  94.3 3.7 %final.1 = (bf16[3,1440,256]{2,1,0:T(8,128)(2,1)}, f32[16,3,16,256]{3,2,1,0:T(8,128)}) custom-call(bf16[16,24,768]{2,1,0:T(8,128)(2,1)S(1)} %all-to-all-done.3.y_ref, bf16[1440,128]{1,0:T(8,128)(2,1)} %constant.38.clone.f_ref, bf16[3,1440,256]{2,1,0:T(8,128)(2,1)} %filtered_back.3.d_ref), custom_call_target="tpu_custom_call" | custom-call | flops 283115520 | bytes 6635520 | tf_op jit(solution)/shard_map/final/pallas_call | solution.py:693
  98.0 1.7 %collective-permute-done.8 = f32[48,256]{1,0:T(8,128)S(1)} collective-permute-done((f32[48,256]{1,0:T(8,128)S(1)}, f32[48,256]{1,0:T(8,128)S(1)}, u32[]{:S(2)}, u32[]{:S(2)}) %collective-permute-start.8) | collective-permute-done | bytes 49184 | tf_op jit(solution)/shard_map/ppermute | solution.py:724
  99.7 0.6 add_add_fusion
  (24 shorter events, 0.1 us)
Async XLA Ops:
  0.6 14.6 %copy-start = (bf16[3,3,9]{2,1,0:T(4,128)(2,1)S(1)}, bf16[3,3,9]{2,1,0:T(4,128)(2,1)}, u32[]{:S(2)}) copy-start(bf16[3,3,9]{2,1,0:T(4,128)(2,1)} %basis_ref.1) | copy-start | bytes 490
  0.6 14.5 %copy-start.1 = (s32[3,9]{1,0:T(4,128)S(1)}, s32[3,9]{1,0:T(4,128)}, u32[]{:S(2)}) copy-start(s32[3,9]{1,0:T(4,128)} %col_ref.1) | copy-start | bytes 328
  0.7 14.5 %copy-start.2 = (s32[3,9]{1,0:T(4,128)S(1)}, s32[3,9]{1,0:T(4,128)}, u32[]{:S(2)}) copy-start(s32[3,9]{1,0:T(4,128)} %row_ref.1) | copy-start | bytes 328
  4.1 16.4 %all-to-all-start = ((bf16[16,8,768]{2,1,0:T(8,128)(2,1)}), bf16[16,8,768]{2,1,0:T(8,128)(2,1)S(1)}, u32[]{:S(2)}, u32[]{:S(2)}) async-start(bf16[16,8,768]{2,1,0:T(8,128)(2,1)} %bitcast.36), calls=%async_computation | async-start | bytes 393216 | tf_op jit(solution)/shard_map/all_to_all | solution.py:773
  11.5 18.6 %collective-permute-start = (bf16[1456,256]{1,0:T(8,128)(2,1)}, bf16[1456,256]{1,0:T(8,128)(2,1)S(1)}, u32[]{:S(2)}, u32[]{:S(2)}) collective-permute-start(bf16[1456,256]{1,0:T(8,128)(2,1)} %get-tuple-element.30), channel_id=1, source_target_pairs={{0,1},{1,2},{2,3},{3,4},{4,5},{5,6},{6,7},{7,8},{8,9},{9,10},{10,1... | collective-permute-start | bytes 2236424 | tf_op jit(solution)/shard_map/ppermute | solution.py:767
  13.8 16.3 %collective-permute-start.1 = (bf16[1456,256]{1,0:T(8,128)(2,1)}, bf16[1456,256]{1,0:T(8,128)(2,1)S(1)}, u32[]{:S(2)}, u32[]{:S(2)}) collective-permute-start(bf16[1456,256]{1,0:T(8,128)(2,1)} %get-tuple-element.31), channel_id=1, source_target_pairs={{1,0},{2,1},{3,2},{4,3},{5,4},{6,5},{7,6},{8,7},{9,8},{10,9},{11,1... | collective-permute-start | bytes 2236424 | tf_op jit(solution)/shard_map/ppermute | solution.py:768
  22.9 16.2 %all-to-all-start.1 = ((bf16[16,8,768]{2,1,0:T(8,128)(2,1)}), bf16[16,8,768]{2,1,0:T(8,128)(2,1)S(1)}, u32[]{:S(2)}, u32[]{:S(2)}) async-start(bf16[16,8,768]{2,1,0:T(8,128)(2,1)} %bitcast.37), calls=%async_computation.1 | async-start | bytes 393216 | tf_op jit(solution)/shard_map/all_to_all | solution.py:773
  49.4 22.3 %all-to-all-start.2 = ((bf16[16,24,768]{2,1,0:T(8,128)(2,1)}), bf16[16,24,768]{2,1,0:T(8,128)(2,1)S(1)}, u32[]{:S(2)}, u32[]{:S(2)}) async-start(bf16[16,24,768]{2,1,0:T(8,128)(2,1)} %get-tuple-element.37), calls=%async_computation.2 | async-start | bytes 1179648 | tf_op jit(solution)/shard_map/all_to_all | solution.py:773
  56.1 24.8 %collective-permute-start.6 = (bf16[1440,256]{1,0:T(8,128)(2,1)}, bf16[1440,256]{1,0:T(8,128)(2,1)S(1)}, u32[]{:S(2)}, u32[]{:S(2)}) collective-permute-start(bf16[1440,256]{1,0:T(8,128)(2,1)} %get-tuple-element.38.rest_0_), channel_id=1, source_target_pairs={{1,0},{2,1},{3,2},{4,3},{5,4},{6,5},{7,6},{8,7},{9,8},{10,9},{11,1... | collective-permute-start | bytes 2211848 | tf_op jit(solution)/shard_map/ppermute | solution.py:768
  57.4 23.5 %collective-permute-start.5 = (bf16[1440,256]{1,0:T(8,128)(2,1)}, bf16[1440,256]{1,0:T(8,128)(2,1)S(1)}, u32[]{:S(2)}, u32[]{:S(2)}) collective-permute-start(bf16[1440,256]{1,0:T(8,128)(2,1)} %get-tuple-element.40.rest_2_), channel_id=1, source_target_pairs={{0,1},{1,2},{2,3},{3,4},{4,5},{5,6},{6,7},{7,8},{8,9},{9,10},{10,1... | collective-permute-start | bytes 2211848 | tf_op jit(solution)/shard_map/ppermute | solution.py:767
  74.3 20.0 %all-to-all-start.3 = ((bf16[16,24,768]{2,1,0:T(8,128)(2,1)}), bf16[16,24,768]{2,1,0:T(8,128)(2,1)S(1)}, u32[]{:S(2)}, u32[]{:S(2)}) async-start(bf16[16,24,768]{2,1,0:T(8,128)(2,1)} %get-tuple-element.46), calls=%async_computation.3 | async-start | bytes 1179648 | tf_op jit(solution)/shard_map/all_to_all | solution.py:773
  78.8 9.7 %collective-permute-start.4 = (f32[48,256]{1,0:T(8,128)S(1)}, f32[48,256]{1,0:T(8,128)S(1)}, u32[]{:S(2)}, u32[]{:S(2)}) collective-permute-start(f32[48,256]{1,0:T(8,128)S(1)} %get-tuple-element.43), channel_id=1, source_target_pairs={{0,3},{1,2},{2,1},{3,0},{4,7},{5,6},{6,5},{7,4},{8,11},{9,10},{10,... | collective-permute-start | bytes 147464 | tf_op jit(solution)/shard_map/ppermute | solution.py:724
  80.5 8.0 %collective-permute-start.3 = (f32[48,256]{1,0:T(8,128)S(1)}, f32[48,256]{1,0:T(8,128)S(1)}, u32[]{:S(2)}, u32[]{:S(2)}) collective-permute-start(f32[48,256]{1,0:T(8,128)S(1)} %get-tuple-element.43), channel_id=1, source_target_pairs={{0,2},{1,3},{2,0},{3,1},{4,6},{5,7},{6,4},{7,5},{8,10},{9,11},{10,... | collective-permute-start | bytes 147464 | tf_op jit(solution)/shard_map/ppermute | solution.py:724
  80.9 7.6 %collective-permute-start.2 = (f32[48,256]{1,0:T(8,128)S(1)}, f32[48,256]{1,0:T(8,128)S(1)}, u32[]{:S(2)}, u32[]{:S(2)}) collective-permute-start(f32[48,256]{1,0:T(8,128)S(1)} %get-tuple-element.43), channel_id=1, source_target_pairs={{0,1},{1,0},{2,3},{3,2},{4,5},{5,4},{6,7},{7,6},{8,9},{9,8},{10,11... | collective-permute-start | bytes 147464 | tf_op jit(solution)/shard_map/ppermute | solution.py:724
  88.6 9.5 %collective-permute-start.9 = (f32[48,256]{1,0:T(8,128)S(1)}, f32[48,256]{1,0:T(8,128)S(1)}, u32[]{:S(2)}, u32[]{:S(2)}) collective-permute-start(f32[48,256]{1,0:T(8,128)S(1)} %add_add_fusion.1), channel_id=1, source_target_pairs={{0,12},{1,13},{2,14},{3,15},{4,8},{5,9},{6,10},{7,11},{8,4},{9,5},... | collective-permute-start | bytes 147464 | tf_op jit(solution)/shard_map/ppermute | solution.py:724
  92.2 7.5 %collective-permute-start.8 = (f32[48,256]{1,0:T(8,128)S(1)}, f32[48,256]{1,0:T(8,128)S(1)}, u32[]{:S(2)}, u32[]{:S(2)}) collective-permute-start(f32[48,256]{1,0:T(8,128)S(1)} %add_add_fusion.1), channel_id=1, source_target_pairs={{0,8},{1,9},{2,10},{3,11},{4,12},{5,13},{6,14},{7,15},{8,0},{9,1},... | collective-permute-start | bytes 147464 | tf_op jit(solution)/shard_map/ppermute | solution.py:724
  92.2 7.5 %collective-permute-start.7 = (f32[48,256]{1,0:T(8,128)S(1)}, f32[48,256]{1,0:T(8,128)S(1)}, u32[]{:S(2)}, u32[]{:S(2)}) collective-permute-start(f32[48,256]{1,0:T(8,128)S(1)} %add_add_fusion.1), channel_id=1, source_target_pairs={{0,4},{1,5},{2,6},{3,7},{4,0},{5,1},{6,2},{7,3},{8,12},{9,13},{10,... | collective-permute-start | bytes 147464 | tf_op jit(solution)/shard_map/ppermute | solution.py:724

commit v4 on v3

--- a/solution.py
+++ b/solution.py
@@ -220,20 +220,25 @@
             for k in range(kernels):
                 wide[2 + k : 3 + k, 0:taps] = basis_held[k, edge : edge + 1, :].astype(F32)
             meta[n] = wide[...].astype(BF16)
+        far = lax.rem(p_ref[0], 2)
+        near = 1 - far
+        for e, away in enumerate((near, far)):
             sent.append(
                 pltpu.make_async_copy(
-                    meta.at[n], edge_refs[n].at[pl.ds(lon, META)], edge_sem.at[n, 1]
+                    meta.at[away], edge_refs[e].at[pl.ds(lon, META)], edge_sem.at[e, 1]
                 )
             )
             sent[-1].start()
         table_copy.wait()
-        for i in order:
+        for n, i in enumerate(order):
             copies[i].wait()
-            for n, edge in enumerate(edges):
-                if i == edge:
+            if n == 1:
+                for e, away in enumerate((near, far)):
                     sent.append(
                         pltpu.make_async_copy(
-                            held.at[i], edge_refs[n].at[pl.ds(0, lon)], edge_sem.at[n, 0]
+                            held.at[away * (lat_dev - 1)],
+                            edge_refs[e].at[pl.ds(0, lon)],
+                            edge_sem.at[e, 0],
                         )
                     )
                     sent[-1].start()
@@ -275,8 +280,8 @@
     )
 
 
-def filtered(middle, north, south, shifts, taps, weights, rows, before=None):
-    first, stride, total = rows
+def filtered(order, middle, near, far, shifts, taps, weights, before=None):
+    total = order.shape[0] - 1
     lat_dev = shifts.shape[0]
     lon, channels = middle[0].shape[-2:]
     kernels = taps.shape[0]
@@ -284,51 +289,65 @@
     wide = kernels * channels
     per = PER
     chunk = per * STEP
-    edges = north is not None
     keep = weights is None
-
-    def body(shift_ref, tap_ref, *rest):
+    beyond = [array for array in (near, far) if array is not None]
+
+    def body(order_ref, shift_ref, tap_ref, *rest):
         rest = list(rest)
         mid_refs = [rest.pop(0) for _ in middle]
-        if len(middle) == 1:
-            mid_refs = [mid_refs[0].at[i] for i in range(lat_dev)]
-        north_ref, south_ref = (rest.pop(0), rest.pop(0)) if edges else (None, None)
+        beyond_refs = [rest.pop(0) for _ in beyond]
         w_ref = None if keep else rest.pop(0)
         if before is not None:
             rest.pop(0)
-        out_ref, ext, sem = rest[:3]
-        mixed_ref = None if keep else rest[3]
+        out_ref, ext, sem, held, out_sem = rest[:5]
+        mixed_ref = None if keep else rest[5]
         step_id = pl.program_id(0)
-        row = first + stride * step_id
+        odd = order_ref[0]
+        row = order_ref[1 + step_id]
+
+        sources = []
+        if len(middle) == 1:
+            sources += [(mid_refs[0].at[i], i + 1) for i in range(1, lat_dev - 1)]
+            if far is None:
+                i = (1 - odd) * (lat_dev - 1)
+                sources.append((mid_refs[0].at[i], i + 1))
+            if near is None:
+                i = odd * (lat_dev - 1)
+                sources.append((mid_refs[0].at[i], i + 1))
+        else:
+            sources += [(mid_refs[i], i + 1) for i in range(1, lat_dev - 1)]
+            sources.append((mid_refs[0], 1 + (1 - odd) * (lat_dev - 1)))
+            sources.append((mid_refs[-1], 1 + odd * (lat_dev - 1)))
+        if near is not None:
+            sources.append((beyond_refs[0], (1 - odd) * (lat_dev + 1)))
+        if far is not None:
+            sources.append((beyond_refs[-1], odd * (lat_dev + 1)))
 
         def copies(which):
-            made = []
-            for e in which:
-                src = (
-                    north_ref if e == 0 else south_ref if e == lat_dev + 1 else mid_refs[e - 1]
+            return [
+                pltpu.make_async_copy(
+                    src.at[pl.ds(a, size)], ext.at[to, pl.ds(b, size)], sem.at[s, n]
                 )
+                for s, (src, to) in list(enumerate(sources))[which]
                 for n, (a, b, size) in enumerate(
                     ((0, SPAN, lon), (lon - SPAN, 0, SPAN), (0, lon + SPAN, SPAN))
-                ):
-                    made.append(
-                        pltpu.make_async_copy(
-                            src.at[pl.ds(a, size)], ext.at[e, pl.ds(b, size)], sem.at[e, n]
-                        )
-                    )
-            return made
-
-        needed = []
-        seen = set()
-        for g in range(total):
-            now = [e for e in range(first + stride * g, first + stride * g + 3) if e not in seen]
-            seen.update(now)
-            needed.append(now)
+                )
+            ]
+
+        late = -1 if far is not None and total > 1 else len(sources)
+
+        def outgoing(g, place):
+            size = lon // 2
+            return pltpu.make_async_copy(
+                held.at[g, pl.ds(place * size, size)],
+                out_ref.at[order_ref[1 + g], pl.ds(place * size, size)],
+                out_sem.at[g, place],
+            )
 
         @pl.when(step_id == 0)
         def _():
-            for now in needed:
-                for copy in copies(now):
-                    copy.start()
+            for copy in copies(slice(None)):
+                copy.start()
 
         across = lax.broadcasted_iota(jnp.int32, (STEP, 3 * WIN), 1)
         down = lax.broadcasted_iota(jnp.int32, (STEP, 3 * WIN), 0)
@@ -340,11 +359,16 @@
                 band[k] = band[k] + jnp.where(hit, tap_ref[k, row, t], 0.0)
         band = jnp.concatenate(band, axis=0).astype(BF16)
 
-        for g, now in enumerate(needed):
-
-            @pl.when(step_id == g)
-            def _(now=now):
-                for copy in copies(now):
+        @pl.when(step_id == 0)
+        def _():
+            for copy in copies(slice(None, late)):
+                copy.wait()
+
+        if late == -1:
+
+            @pl.when(step_id == total - 1)
+            def _():
+                for copy in copies(slice(late, None)):
                     copy.wait()
 
         for c in range(lon // chunk):
@@ -358,11 +382,11 @@
                     part = sums[k * STEP : (k + 1) * STEP]
                     lanes = slice(k * channels, (k + 1) * channels)
                     if keep:
-                        out_ref[0, start : start + STEP, lanes] = part
+                        held[step_id, start : start + STEP, lanes] = part
                     else:
                         mixed_ref[c % 2, b * STEP : (b + 1) * STEP, lanes] = part
             if not keep:
-                out_ref[0, c * chunk : (c + 1) * chunk, :] = sum(
+                held[step_id, c * chunk : (c + 1) * chunk, :] = sum(
                     lax.dot_general(
                         mixed_ref[c % 2, :, k * channels : (k + 1) * channels],
                         w_ref[k * channels : (k + 1) * channels, :],
@@ -371,17 +395,24 @@
                     )
                     for k in range(kernels)
                 ).astype(BF16)
+            if (c + 1) * chunk * 2 % lon == 0:
+                outgoing(step_id, (c + 1) * chunk * 2 // lon - 1).start()
+
+        @pl.when(step_id == total - 1)
+        def _():
+            for g in range(total):
+                for place in range(2):
+                    outgoing(g, place).wait()
 
     depth = wide if keep else channels
-    operands = [shifts, taps, *(in_hbm(array) for array in middle)]
-    in_specs = [SMEM, SMEM] + [ANYWHERE] * len(middle)
+    operands = [order, shifts, taps, *(in_hbm(array) for array in middle), *beyond]
+    in_specs = [SMEM, SMEM] + [ANYWHERE] * (len(middle) + len(beyond))
     scratch = [
         pltpu.VMEM((lat_dev + 2, lon + 2 * SPAN, channels), BF16),
         pltpu.SemaphoreType.DMA((lat_dev + 2, 3)),
+        pltpu.VMEM((total, lon, depth), BF16),
+        pltpu.SemaphoreType.DMA((total, 2)),
     ]
-    if edges:
-        operands += [north, south]
-        in_specs += [ANYWHERE, ANYWHERE]
     if not keep:
         operands.append(in_hbm(weights))
         in_specs.append(every(wide, channels))
@@ -394,11 +425,11 @@
     return pl.pallas_call(
         body,
         grid=(total,),
-        in_specs=in_specs,
-        out_specs=pl.BlockSpec((1, lon, depth), lambda g: (first + stride * g, 0, 0)),
+        in_specs=[SMEM] + in_specs,
+        out_specs=ANYWHERE,
+        scratch_shapes=scratch,
         out_shape=pltpu.HBM((lat_dev, lon, depth), BF16),
         input_output_aliases=aliases,
-        scratch_shapes=scratch,
         compiler_params=params(24),
         cost_estimate=cost(
             2 * total * lon * channels * (wide * (0 if keep else 1) + 3 * WIN * kernels),
@@ -525,7 +556,7 @@
     )
 
 
-def activation(mixed, weights, returned, grad_output, inverse, inverse_t, devices, terms):
+def activation(position, mixed, weights, returned, grad_output, inverse, inverse_t, devices, terms):
     lat_dev, lon, wide = mixed.shape
     channels = grad_output.shape[2]
     group_rows = returned.shape[0]
@@ -533,7 +564,7 @@
     chunk = CHUNK
     piece = wide // devices // lat_dev
 
-    def body(m_ref, w_ref, y_ref, g_ref, inv_ref, invt_ref, *rest):
+    def body(p_ref, m_ref, w_ref, y_ref, g_ref, inv_ref, invt_ref, *rest):
         o_ref, row_refs = rest[0], rest[1 : 1 + lat_dev]
         rest = rest[1 + lat_dev :]
         acc, held, sem = rest[-3:]
@@ -548,11 +579,14 @@
             slope = half + value * (1.0 - half) * (2.0 * ROOT + 6.0 * ROOT * CUBE * square)
             o_ref[0, place, :] = value.astype(BF16)
             gt_ref[place, :] = (g_ref[0, place, :].astype(F32) * slope).astype(BF16)
+        odd = lax.rem(p_ref[0], 2)
         for i in range(lat_dev):
-
-            @pl.when(row == i)
-            def _(i=i):
-                pltpu.make_async_copy(held.at[i], row_refs[i], sem.at[i]).start()
+            for side in range(2):
+                to = i if side == 1 else lat_dev - 1 - i
+
+                @pl.when((row == i) & (odd == side))
+                def _(i=i, to=to):
+                    pltpu.make_async_copy(held.at[i], row_refs[to], sem.at[i]).start()
 
         spectrum = dot(invt_ref[...], gt_ref[...])
         part = dot(jnp.transpose(gt_ref[...]), m_ref[0])
@@ -612,6 +646,7 @@
         body,
         grid=(lat_dev,),
         in_specs=[
+            SMEM,
             pl.BlockSpec((1, lon, wide), lambda i: (i, 0, 0)),
             every(wide, channels),
             column_spec,
@@ -636,6 +671,7 @@
         ),
         name="activation",
     )(
+        position,
         in_hbm(mixed),
         in_hbm(weights),
         returned,
@@ -762,11 +798,12 @@
     return (array, result)
 
 
-def neighbours(north_edge, south_edge):
+def paired(near_row, far_row):
     count = lax.axis_size("lat")
-    from_north = lax.ppermute(south_edge, "lat", [(i, i + 1) for i in range(count - 1)])
-    from_south = lax.ppermute(north_edge, "lat", [(i + 1, i) for i in range(count - 1)])
-    return (from_north, from_south)
+    near = lax.ppermute(near_row, "lat", [(i, i ^ 1) for i in range(count)])
+    across = [(i, i + 1) for i in range(1, count - 1, 2)]
+    far = lax.ppermute(far_row, "lat", across + [(b, a) for a, b in across])
+    return (near, far)
 
 
 def exchange(blocks):
@@ -803,13 +840,12 @@
         and piece % 16 == 0
     )
     terms = piece if small else 0
-    inner = (1, 1, lat_dev - 2)
-    outer = (0, lat_dev - 1, 2)
-
-    coefficients, first_row, last_row = transform(
+    inner = tuple(range(1, lat_dev - 1))
+
+    coefficients, near_row, far_row = transform(
         place, features, forward_t, disco_rows, disco_cols, disco_basis
     )
-    north, south = neighbours(first_row, last_row)
+    near, far = paired(near_row, far_row)
     owned = exchange_rows(coefficients)
 
     band_rows = position * lat_dev + jnp.arange(lat_dev, dtype=jnp.int32)[:, None]
@@ -817,9 +853,17 @@
     offsets = disco_rows - band_rows
     shifts = (offsets + 1) * WIN + SPAN + disco_cols
     weight_rows = disco_weight.reshape(wide, channels)
-    mixed = filtered([features], None, None, shifts, basis, None, inner)
+    odd = position % 2
+    near_id = (1 - odd) * (lat_dev - 1)
+    far_id = odd * (lat_dev - 1)
+
+    def order_of(*rows):
+        return jnp.stack([odd, *rows]).astype(jnp.int32)
+
+    mixed = filtered(order_of(*inner), [features], None, None, shifts, basis, None)
     owned, mixed = lax.optimization_barrier((owned, mixed))
-    mixed = filtered([features], north, south, shifts, basis, None, outer, mixed)
+    mixed = filtered(order_of(near_id), [features], near, None, shifts, basis, None, mixed)
+    mixed = filtered(order_of(far_id), [features], None, far, shifts, basis, None, mixed)
 
     packed = jnp.concatenate(
         [
@@ -829,12 +873,10 @@
         ],
         axis=1,
     )
+    near_taps = near[None, lon : lon + 2 + kernels, :taps].astype(F32)
+    far_taps = far[None, lon : lon + 2 + kernels, :taps].astype(F32)
     packed_all = jnp.concatenate(
-        [
-            north[None, lon : lon + 2 + kernels, :taps].astype(F32),
-            packed,
-            south[None, lon : lon + 2 + kernels, :taps].astype(F32),
-        ],
+        [jnp.where(odd == 1, near_taps, far_taps), packed, jnp.where(odd == 1, far_taps, near_taps)],
         axis=0,
     )
     back_shifts = []
@@ -879,11 +921,13 @@
 
     returned = exchange_rows(synthesized)
     output, *blocks = activation(
-        mixed, weight_rows, returned, grad_output, inverse, inverse_t, devices, terms
+        place, mixed, weight_rows, returned, grad_output, inverse, inverse_t, devices, terms
     )
     grad_rows, blocks = blocks[:lat_dev], blocks[lat_dev:]
-    grad_north, grad_south = neighbours(grad_rows[0], grad_rows[-1])
-    part = filtered(grad_rows, None, None, back_shifts, back_taps, weight_rows, inner)
+    grad_near, grad_far = paired(grad_rows[0], grad_rows[-1])
+    part = filtered(
+        order_of(*inner), grad_rows, None, None, back_shifts, back_taps, weight_rows
+    )
     if small:
         grad_owned, part = lax.optimization_barrier((exchange(blocks[0]), part))
         gain_part, grad_blocks = spectral_adjoint(
@@ -903,7 +947,14 @@
         grad_bands = exchange_rows(grad_coeff)
 
     grad_disco = filtered(
-        grad_rows, grad_north, grad_south, back_shifts, back_taps, weight_rows, outer, part
+        order_of(near_id, far_id),
+        grad_rows,
+        grad_near,
+        grad_far,
+        back_shifts,
+        back_taps,
+        weight_rows,
+        part,
     )
     grad_gain, (grad_features, *grad_weight) = sum_everywhere(
         gain_part, grad_disco, lambda held: final(grad_bands, forward, held, terms)

time: 101 us -> 99.7 us (0.987)
  starting transfers between devices: 40.3 us -> 35.8 us
  Pallas kernels: 45.4 us -> 47.5 us
    ppermute x4, starting transfers between devices: 8.01 us -> 5.16 us  [the longest x2 3.76 us: paired(): near = lax.ppermute(near_row, 'lat', [(i, i ^ 1) for i in range(count)])]
    pallas_call x5 -> x6, Pallas kernels: 33.2 us -> 35 us  [the longest x5 24.8 us: filtered(): pl.pallas_call(body, grid=(total,), in_specs=[SMEM] + in_specs, out_specs...]
    all_to_all x4, starting transfers between devices: 25.7 us -> 24 us  [exchange(): lax.all_to_all(blocks, 'lat', split_axis=0, concat_axis=0, tiled=True)]
  transfers between devices with their start and end apart: 14 -> 14, of which waited for: 5 -> 5; matrix products, arithmetic and copies ran while one was open for 0% -> 1% of each run, Pallas kernels for 32% -> 34%
where the time goes in v4:
time: 99.7 us; the launch traced here: 98.9 us
  Pallas kernels  47.5 us (48%)
  starting transfers between devices  35.8 us (36%)
  waiting for transfers between devices  13.4 us (13%)
  other arithmetic  1.22 us (1%)
    pallas_call x5, Pallas kernels, filtered(): pl.pallas_call(body, grid=(total,), in_specs=[SMEM] + in_specs, out_specs...  24.8 us
    all_to_all x4, starting transfers between devices, exchange(): lax.all_to_all(blocks, 'lat', split_axis=0, concat_axis=0, tiled=True)  24 us
    all_to_all x4, waiting for transfers between devices, exchange(): lax.all_to_all(blocks, 'lat', split_axis=0, concat_axis=0, tiled=True)  11.7 us
    pallas_call x1, Pallas kernels, activation(): pl.pallas_call(body, grid=(lat_dev,), in_specs=[SMEM, pl.BlockSpec((1, lo...  10.2 us
    ppermute x6, starting transfers between devices, partner(): lax.ppermute(array, 'lat', [(i, i ^ by * stride) for i in range(count)])  6.67 us
    ppermute x2, starting transfers between devices, paired(): near = lax.ppermute(near_row, 'lat', [(i, i ^ 1) for i in range(count)])  3.76 us
    pallas_call x1, Pallas kernels, transform(): pl.pallas_call(body, in_specs=[SMEM] + [ANYWHERE] * 5, out_specs=[VMEM, A...  3.67 us
    pallas_call x1, Pallas kernels, final(): pl.pallas_call(body, in_specs=[VMEM, ANYWHERE, ANYWHERE], out_specs=[ANYW...  3.66 us
  transfers between devices with their start and end apart: 14, of which 5 were waited for; matrix products, arithmetic and copies ran while one was open for 1% of the time, Pallas kernels for 34%

profile of v4, /device:TPU:0, one launch (start us, length us, event | category | flops | bytes accessed | tf_op | source)
XLA Modules:
  0.0 98.9 jit_solution(9977071462332142065)
XLA Ops:
  0.7 3.7 %transform.1 = (bf16[128,768]{1,0:T(8,128)(2,1)}, bf16[1456,256]{1,0:T(8,128)(2,1)}, bf16[1456,256]{1,0:T(8,128)(2,1)}) custom-call(s32[1]{0:T(128)} %bitcast.p_ref, bf16[3,1440,256]{2,1,0:T(8,128)(2,1)} %rest_0_.5, bf16[128,1440]{1,0:T(8,128)(2,1)} %constant.51.clone.t_ref, s32[3,9]{1,0:T(4,128)} %row_ref.1, s32[3,9]{1,0:T(4,128)} %col_ref.1, ...), custom_call_target="tpu_custom_call" | custom-call | flops 283115520 | bytes 2211840 | tf_op jit(solution)/shard_map/transform/pallas_call | solution.py:249
  4.3 7.4 %all-to-all-start = ((bf16[16,8,768]{2,1,0:T(8,128)(2,1)}), bf16[16,8,768]{2,1,0:T(8,128)(2,1)S(1)}, u32[]{:S(2)}, u32[]{:S(2)}) async-start(bf16[16,8,768]{2,1,0:T(8,128)(2,1)} %bitcast.33), calls=%async_computation | async-start | bytes 393216 | tf_op jit(solution)/shard_map/all_to_all | solution.py:810
  11.7 0.7 collective-permute-start
  12.5 3.3 %collective-permute-start.1 = (bf16[1456,256]{1,0:T(8,128)(2,1)}, bf16[1456,256]{1,0:T(8,128)(2,1)S(1)}, u32[]{:S(2)}, u32[]{:S(2)}) collective-permute-start(bf16[1456,256]{1,0:T(8,128)(2,1)} %get-tuple-element.31), channel_id=1, source_target_pairs={{0,1},{1,0},{2,3},{3,2},{4,5},{5,4},{6,7},{7,6},{8,9},{9,8},{10,11... | collective-permute-start | bytes 2236424 | tf_op jit(solution)/shard_map/ppermute | solution.py:803
  15.8 0.1 subtract_select_fusion
  15.9 4.3 %filtered.3.rest_2_ = bf16[3,1440,768]{2,1,0:T(8,128)(2,1)} custom-call(s32[2]{0:T(128)S(1)} %pad_add_fusion.3.order_ref, s32[3,9]{1,0:T(4,128)S(1)} %get-tuple-element.63.shift_ref, f32[3,3,9]{2,1,0:T(4,128)S(1)} %get-tuple-element.65.tap_ref, bf16[3,1440,256]{2,1,0:T(8,128)(2,1)} %rest_0_.5), custom_call_target="tpu_custom_call" | custom-call | flops 530841600 | bytes 2949120 | tf_op jit(solution)/shard_map/filtered/pallas_call | solution.py:425
  20.2 0.5 all-to-all-done
  20.8 2.4 %spectral_forward.1 = (f32[288,256]{1,0:T(8,128)}, bf16[128,768]{1,0:T(8,128)(2,1)}) custom-call(s32[1]{0:T(128)} %bitcast.p_ref, bf16[128,768]{1,0:T(8,128)(2,1)S(1)} %bitcast.28, bf16[16,288,384]{2,1,0:T(8,128)(2,1)} %constant.56.clone.a_ref, bf16[16,288,384]{2,1,0:T(8,128)(2,1)} %constant.55.clone.b_ref, f32[48,256]{1,0:T(8,128)} %g_ref.5), custom_call_target="tpu_custom_call" | custom-call | tf_op jit(solution)/shard_map/spectral_forward/pallas_call | solution.py:469
  23.1 4.1 %all-to-all-start.1 = ((bf16[16,8,768]{2,1,0:T(8,128)(2,1)}), bf16[16,8,768]{2,1,0:T(8,128)(2,1)S(1)}, u32[]{:S(2)}, u32[]{:S(2)}) async-start(bf16[16,8,768]{2,1,0:T(8,128)(2,1)} %bitcast.34), calls=%async_computation.1 | async-start | bytes 393216 | tf_op jit(solution)/shard_map/all_to_all | solution.py:810
  27.4 4.1 %filtered.4.rest_2_ = bf16[3,1440,768]{2,1,0:T(8,128)(2,1)} custom-call(s32[2]{0:T(128)S(1)} %pad_add_fusion.2.order_ref, s32[3,9]{1,0:T(4,128)S(1)} %get-tuple-element.63.shift_ref, f32[3,3,9]{2,1,0:T(4,128)S(1)} %get-tuple-element.65.tap_ref, bf16[3,1440,256]{2,1,0:T(8,128)(2,1)} %rest_0_.5, ...), custom_call_target="tpu_custom_call", output_to_operand_aliasing={{}: (5, {})} | custom-call | flops 530841600 | bytes 2949120 | tf_op jit(solution)/shard_map/filtered/pallas_call | solution.py:425
  31.5 4.1 %filtered.5.m_ref = bf16[3,1440,768]{2,1,0:T(8,128)(2,1)} custom-call(s32[2]{0:T(128)S(1)} %pad_add_fusion.1.order_ref, s32[3,9]{1,0:T(4,128)S(1)} %get-tuple-element.63.shift_ref, f32[3,3,9]{2,1,0:T(4,128)S(1)} %get-tuple-element.65.tap_ref, bf16[3,1440,256]{2,1,0:T(8,128)(2,1)} %rest_0_.5, ...), custom_call_target="tpu_custom_call", output_to_operand_aliasing={{}: (5, {})} | custom-call | flops 530841600 | bytes 2949120 | tf_op jit(solution)/shard_map/filtered/pallas_call | solution.py:425
  35.6 0.7 all-to-all-done.1
  36.3 10.2 %activation.1 = (bf16[3,1440,256]{2,1,0:T(8,128)(2,1)}, bf16[1440,256]{1,0:T(8,128)(2,1)}, bf16[1440,256]{1,0:T(8,128)(2,1)}, bf16[1440,256]{1,0:T(8,128)(2,1)}, bf16[16,24,768]{2,1,0:T(8,128)(2,1)}) custom-call(s32[1]{0:T(128)} %bitcast.p_ref, bf16[3,1440,768]{2,1,0:T(8,128)(2,1)} %filtered.5.m_ref, bf16[768,256]{1,0:T(8,128)(2,1)} %bitcast.30, ...), custom_call_target="tpu_custom_call" | custom-call | flops 3963617280 | bytes 15482880 | tf_op jit(solution)/shard_map/activation/pallas_call | solution.py:645
  46.5 8.0 %all-to-all-start.2 = ((bf16[16,24,768]{2,1,0:T(8,128)(2,1)}), bf16[16,24,768]{2,1,0:T(8,128)(2,1)S(1)}, u32[]{:S(2)}, u32[]{:S(2)}) async-start(bf16[16,24,768]{2,1,0:T(8,128)(2,1)} %get-tuple-element.37), calls=%async_computation.2 | async-start | bytes 1179648 | tf_op jit(solution)/shard_map/all_to_all | solution.py:810
  54.6 0.5 collective-permute-start.5
  55.0 0.7 collective-permute-start.6
  55.8 0.1 pad_add_fusion.shift_ref
  55.9 0.1 pad_maximum_fusion.6.tap_ref
  55.9 5.2 %filtered_back.2.rest_6_ = bf16[3,1440,256]{2,1,0:T(8,128)(2,1)} custom-call(s32[2]{0:T(128)S(1)} %pad_add_fusion.3.order_ref, s32[3,27]{1,0:T(4,128)S(1)} %pad_add_fusion.shift_ref, f32[3,3,27]{2,1,0:T(4,128)S(1)} %pad_maximum_fusion.6.tap_ref, bf16[1440,256]{1,0:T(8,128)(2,1)} %get-tuple-element.38.rest_0_, bf16[1440,256]{1,0:T(8,128)(2,1)} %get-tuple-element.39.rest_1_, ...), custom_call_target="tpu_custom_call" | custom-call | flops 1097072640 | bytes 2949120 | tf_op jit(solution)/shard_map/filtered_back/pallas_call | solution.py:425
  61.1 9.0 %all-to-all-done.2.x_ref = bf16[16,24,768]{2,1,0:T(8,128)(2,1)S(1)} async-done(((bf16[16,24,768]{2,1,0:T(8,128)(2,1)}), bf16[16,24,768]{2,1,0:T(8,128)(2,1)S(1)}, u32[]{:S(2)}, u32[]{:S(2)}) %all-to-all-start.2) | async-done | bytes 589856 | tf_op jit(solution)/shard_map/all_to_all | solution.py:810
  70.1 2.7 %spectral_adjoint.1 = (f32[48,256]{1,0:T(8,128)S(1)}, bf16[16,24,768]{2,1,0:T(8,128)(2,1)}) custom-call(s32[1]{0:T(128)} %bitcast.p_ref, bf16[16,24,768]{2,1,0:T(8,128)(2,1)S(1)} %all-to-all-done.2.x_ref, bf16[16,288,384]{2,1,0:T(8,128)(2,1)} %constant.55.clone.b_ref, bf16[16,288,384]{2,1,0:T(8,128)(2,1)} %constant.56.clone.a_ref, f32[48,256]{1,0:T(8,128)} %g_ref.5, ...), custom_call_target="tpu_custom_call" | custom-call | tf_op jit(solution)/shard_map/spectral_adjoint/pallas_call | solution.py:526
  72.8 4.5 %all-to-all-start.3 = ((bf16[16,24,768]{2,1,0:T(8,128)(2,1)}), bf16[16,24,768]{2,1,0:T(8,128)(2,1)S(1)}, u32[]{:S(2)}, u32[]{:S(2)}) async-start(bf16[16,24,768]{2,1,0:T(8,128)(2,1)} %get-tuple-element.46), calls=%async_computation.3 | async-start | bytes 1179648 | tf_op jit(solution)/shard_map/all_to_all | solution.py:810
  77.3 0.1 pad_add_fusion.4.order_ref
  77.4 1.7 %collective-permute-start.4 = (f32[48,256]{1,0:T(8,128)S(1)}, f32[48,256]{1,0:T(8,128)S(1)}, u32[]{:S(2)}, u32[]{:S(2)}) collective-permute-start(f32[48,256]{1,0:T(8,128)S(1)} %get-tuple-element.43), channel_id=1, source_target_pairs={{0,3},{1,2},{2,1},{3,0},{4,7},{5,6},{6,5},{7,4},{8,11},{9,10},{10,... | collective-permute-start | bytes 147464 | tf_op jit(solution)/shard_map/ppermute | solution.py:760
  79.0 0.4 collective-permute-start.3
  79.5 7.3 %filtered_back.3.d_ref = bf16[3,1440,256]{2,1,0:T(8,128)(2,1)} custom-call(s32[3]{0:T(128)S(1)} %pad_add_fusion.4.order_ref, s32[3,27]{1,0:T(4,128)S(1)} %pad_add_fusion.shift_ref, f32[3,3,27]{2,1,0:T(4,128)S(1)} %pad_maximum_fusion.6.tap_ref, bf16[1440,256]{1,0:T(8,128)(2,1)} %get-tuple-element.38.rest_0_, ...), custom_call_target="tpu_custom_call", output_to_operand_aliasing={{}: (9, {})} | custom-call | flops 2194145280 | bytes 5898240 | tf_op jit(solution)/shard_map/filtered_back/pallas_call | solution.py:425
  86.8 4.0 %collective-permute-start.9 = (f32[48,256]{1,0:T(8,128)S(1)}, f32[48,256]{1,0:T(8,128)S(1)}, u32[]{:S(2)}, u32[]{:S(2)}) collective-permute-start(f32[48,256]{1,0:T(8,128)S(1)} %add_add_fusion.1), channel_id=1, source_target_pairs={{0,12},{1,13},{2,14},{3,15},{4,8},{5,9},{6,10},{7,11},{8,4},{9,5},... | collective-permute-start | bytes 147464 | tf_op jit(solution)/shard_map/ppermute | solution.py:760
  90.7 0.6 collective-permute-start.7
  91.4 1.5 %all-to-all-done.3.y_ref = bf16[16,24,768]{2,1,0:T(8,128)(2,1)S(1)} async-done(((bf16[16,24,768]{2,1,0:T(8,128)(2,1)}), bf16[16,24,768]{2,1,0:T(8,128)(2,1)S(1)}, u32[]{:S(2)}, u32[]{:S(2)}) %all-to-all-start.3) | async-done | bytes 589856 | tf_op jit(solution)/shard_map/all_to_all | solution.py:810
  92.8 3.7 %final.1 = (bf16[3,1440,256]{2,1,0:T(8,128)(2,1)}, f32[16,3,16,256]{3,2,1,0:T(8,128)}) custom-call(bf16[16,24,768]{2,1,0:T(8,128)(2,1)S(1)} %all-to-all-done.3.y_ref, bf16[1440,128]{1,0:T(8,128)(2,1)} %constant.53.clone.f_ref, bf16[3,1440,256]{2,1,0:T(8,128)(2,1)} %filtered_back.3.d_ref), custom_call_target="tpu_custom_call" | custom-call | flops 283115520 | bytes 6635520 | tf_op jit(solution)/shard_map/final/pallas_call | solution.py:729
  96.5 1.7 %collective-permute-done.8 = f32[48,256]{1,0:T(8,128)S(1)} collective-permute-done((f32[48,256]{1,0:T(8,128)S(1)}, f32[48,256]{1,0:T(8,128)S(1)}, u32[]{:S(2)}, u32[]{:S(2)}) %collective-permute-start.8) | collective-permute-done | bytes 49184 | tf_op jit(solution)/shard_map/ppermute | solution.py:760
  98.2 0.6 add_add_fusion
  (28 shorter events, 0.3 us)
Async XLA Ops:
  0.6 15.3 %copy-start = (bf16[3,3,9]{2,1,0:T(4,128)(2,1)S(1)}, bf16[3,3,9]{2,1,0:T(4,128)(2,1)}, u32[]{:S(2)}) copy-start(bf16[3,3,9]{2,1,0:T(4,128)(2,1)} %basis_ref.1) | copy-start | bytes 490
  0.6 15.1 %copy-start.1 = (s32[3,9]{1,0:T(4,128)S(1)}, s32[3,9]{1,0:T(4,128)}, u32[]{:S(2)}) copy-start(s32[3,9]{1,0:T(4,128)} %col_ref.1) | copy-start | bytes 328
  0.7 15.1 %copy-start.2 = (s32[3,9]{1,0:T(4,128)S(1)}, s32[3,9]{1,0:T(4,128)}, u32[]{:S(2)}) copy-start(s32[3,9]{1,0:T(4,128)} %row_ref.1) | copy-start | bytes 328
  4.3 16.4 %all-to-all-start = ((bf16[16,8,768]{2,1,0:T(8,128)(2,1)}), bf16[16,8,768]{2,1,0:T(8,128)(2,1)S(1)}, u32[]{:S(2)}, u32[]{:S(2)}) async-start(bf16[16,8,768]{2,1,0:T(8,128)(2,1)} %bitcast.33), calls=%async_computation | async-start | bytes 393216 | tf_op jit(solution)/shard_map/all_to_all | solution.py:810
  11.7 19.8 %collective-permute-start = (bf16[1456,256]{1,0:T(8,128)(2,1)}, bf16[1456,256]{1,0:T(8,128)(2,1)S(1)}, u32[]{:S(2)}, u32[]{:S(2)}) collective-permute-start(bf16[1456,256]{1,0:T(8,128)(2,1)} %get-tuple-element.30), channel_id=1, source_target_pairs={{1,2},{3,4},{5,6},{7,8},{9,10},{11,12},{13,14},{2,1},{4,3},{6,5},{... | collective-permute-start | bytes 2236424 | tf_op jit(solution)/shard_map/ppermute | solution.py:805
  12.5 15.0 %collective-permute-start.1 = (bf16[1456,256]{1,0:T(8,128)(2,1)}, bf16[1456,256]{1,0:T(8,128)(2,1)S(1)}, u32[]{:S(2)}, u32[]{:S(2)}) collective-permute-start(bf16[1456,256]{1,0:T(8,128)(2,1)} %get-tuple-element.31), channel_id=1, source_target_pairs={{0,1},{1,0},{2,3},{3,2},{4,5},{5,4},{6,7},{7,6},{8,9},{9,8},{10,11... | collective-permute-start | bytes 2236424 | tf_op jit(solution)/shard_map/ppermute | solution.py:803
  23.1 13.1 %all-to-all-start.1 = ((bf16[16,8,768]{2,1,0:T(8,128)(2,1)}), bf16[16,8,768]{2,1,0:T(8,128)(2,1)S(1)}, u32[]{:S(2)}, u32[]{:S(2)}) async-start(bf16[16,8,768]{2,1,0:T(8,128)(2,1)} %bitcast.34), calls=%async_computation.1 | async-start | bytes 393216 | tf_op jit(solution)/shard_map/all_to_all | solution.py:810
  46.5 23.6 %all-to-all-start.2 = ((bf16[16,24,768]{2,1,0:T(8,128)(2,1)}), bf16[16,24,768]{2,1,0:T(8,128)(2,1)S(1)}, u32[]{:S(2)}, u32[]{:S(2)}) async-start(bf16[16,24,768]{2,1,0:T(8,128)(2,1)} %get-tuple-element.37), calls=%async_computation.2 | async-start | bytes 1179648 | tf_op jit(solution)/shard_map/all_to_all | solution.py:810
  54.6 24.9 %collective-permute-start.5 = (bf16[1440,256]{1,0:T(8,128)(2,1)}, bf16[1440,256]{1,0:T(8,128)(2,1)S(1)}, u32[]{:S(2)}, u32[]{:S(2)}) collective-permute-start(bf16[1440,256]{1,0:T(8,128)(2,1)} %get-tuple-element.38.rest_0_), channel_id=1, source_target_pairs={{0,1},{1,0},{2,3},{3,2},{4,5},{5,4},{6,7},{7,6},{8,9},{9,8},{10,11... | collective-permute-start | bytes 2211848 | tf_op jit(solution)/shard_map/ppermute | solution.py:803
  55.0 24.4 %collective-permute-start.6 = (bf16[1440,256]{1,0:T(8,128)(2,1)}, bf16[1440,256]{1,0:T(8,128)(2,1)S(1)}, u32[]{:S(2)}, u32[]{:S(2)}) collective-permute-start(bf16[1440,256]{1,0:T(8,128)(2,1)} %get-tuple-element.40.rest_2_), channel_id=1, source_target_pairs={{1,2},{3,4},{5,6},{7,8},{9,10},{11,12},{13,14},{2,1},{4,3},{6,5},{... | collective-permute-start | bytes 2211848 | tf_op jit(solution)/shard_map/ppermute | solution.py:805
  72.8 20.0 %all-to-all-start.3 = ((bf16[16,24,768]{2,1,0:T(8,128)(2,1)}), bf16[16,24,768]{2,1,0:T(8,128)(2,1)S(1)}, u32[]{:S(2)}, u32[]{:S(2)}) async-start(bf16[16,24,768]{2,1,0:T(8,128)(2,1)} %get-tuple-element.46), calls=%async_computation.3 | async-start | bytes 1179648 | tf_op jit(solution)/shard_map/all_to_all | solution.py:810
  77.4 9.3 %collective-permute-start.4 = (f32[48,256]{1,0:T(8,128)S(1)}, f32[48,256]{1,0:T(8,128)S(1)}, u32[]{:S(2)}, u32[]{:S(2)}) collective-permute-start(f32[48,256]{1,0:T(8,128)S(1)} %get-tuple-element.43), channel_id=1, source_target_pairs={{0,3},{1,2},{2,1},{3,0},{4,7},{5,6},{6,5},{7,4},{8,11},{9,10},{10,... | collective-permute-start | bytes 147464 | tf_op jit(solution)/shard_map/ppermute | solution.py:760
  79.0 7.7 %collective-permute-start.3 = (f32[48,256]{1,0:T(8,128)S(1)}, f32[48,256]{1,0:T(8,128)S(1)}, u32[]{:S(2)}, u32[]{:S(2)}) collective-permute-start(f32[48,256]{1,0:T(8,128)S(1)} %get-tuple-element.43), channel_id=1, source_target_pairs={{0,2},{1,3},{2,0},{3,1},{4,6},{5,7},{6,4},{7,5},{8,10},{9,11},{10,... | collective-permute-start | bytes 147464 | tf_op jit(solution)/shard_map/ppermute | solution.py:760
  79.4 7.3 %collective-permute-start.2 = (f32[48,256]{1,0:T(8,128)S(1)}, f32[48,256]{1,0:T(8,128)S(1)}, u32[]{:S(2)}, u32[]{:S(2)}) collective-permute-start(f32[48,256]{1,0:T(8,128)S(1)} %get-tuple-element.43), channel_id=1, source_target_pairs={{0,1},{1,0},{2,3},{3,2},{4,5},{5,4},{6,7},{7,6},{8,9},{9,8},{10,11... | collective-permute-start | bytes 147464 | tf_op jit(solution)/shard_map/ppermute | solution.py:760
  86.8 9.7 %collective-permute-start.9 = (f32[48,256]{1,0:T(8,128)S(1)}, f32[48,256]{1,0:T(8,128)S(1)}, u32[]{:S(2)}, u32[]{:S(2)}) collective-permute-start(f32[48,256]{1,0:T(8,128)S(1)} %add_add_fusion.1), channel_id=1, source_target_pairs={{0,12},{1,13},{2,14},{3,15},{4,8},{5,9},{6,10},{7,11},{8,4},{9,5},... | collective-permute-start | bytes 147464 | tf_op jit(solution)/shard_map/ppermute | solution.py:760
  90.7 7.5 %collective-permute-start.8 = (f32[48,256]{1,0:T(8,128)S(1)}, f32[48,256]{1,0:T(8,128)S(1)}, u32[]{:S(2)}, u32[]{:S(2)}) collective-permute-start(f32[48,256]{1,0:T(8,128)S(1)} %add_add_fusion.1), channel_id=1, source_target_pairs={{0,8},{1,9},{2,10},{3,11},{4,12},{5,13},{6,14},{7,15},{8,0},{9,1},... | collective-permute-start | bytes 147464 | tf_op jit(solution)/shard_map/ppermute | solution.py:760
  90.7 7.5 %collective-permute-start.7 = (f32[48,256]{1,0:T(8,128)S(1)}, f32[48,256]{1,0:T(8,128)S(1)}, u32[]{:S(2)}, u32[]{:S(2)}) collective-permute-start(f32[48,256]{1,0:T(8,128)S(1)} %add_add_fusion.1), channel_id=1, source_target_pairs={{0,4},{1,5},{2,6},{3,7},{4,0},{5,1},{6,2},{7,3},{8,12},{9,13},{10,... | collective-permute-start | bytes 147464 | tf_op jit(solution)/shard_map/ppermute | solution.py:760

commit v5 on v4

--- a/solution.py
+++ b/solution.py
@@ -789,9 +789,11 @@
         last = n == len(plan) - 1
         if last:
             array, between = lax.optimization_barrier((array, between))
-        parts = [array] + [partner(array, count, stride, by) for by in range(1, factor)]
+        sent = lax.optimization_barrier(array.astype(BF16))
+        parts = [sent] + [partner(sent, count, stride, by) for by in range(1, factor)]
         if last:
             parts, result = lax.optimization_barrier((parts, then(between)))
+        parts = [part.astype(F32) for part in parts]
         while len(parts) > 1:
             parts = [parts[k] + parts[k + 1] for k in range(0, len(parts), 2)]
         array = parts[0]

time: 99.7 us -> 98.4 us (0.987)
  waiting for transfers between devices: 13.4 us -> 11.9 us
    ppermute x6, waiting for transfers between devices: 1.71 us -> 0.02 us  [partner(): lax.ppermute(array, 'lat', [(i, i ^ by * stride) for i in range(count)])]
  transfers between devices with their start and end apart: 14 -> 14, of which waited for: 5 -> 4; matrix products, arithmetic and copies ran while one was open for 1% -> 1% of each run, Pallas kernels for 34% -> 35%
where the time goes in v5:
time: 98.4 us; the launch traced here: 97.2 us
  Pallas kernels  47.5 us (48%)
  starting transfers between devices  35.7 us (36%)
  waiting for transfers between devices  11.9 us (12%)
  other arithmetic  1.23 us (1%)
    pallas_call x5, Pallas kernels, filtered(): pl.pallas_call(body, grid=(total,), in_specs=[SMEM] + in_specs, out_specs...  24.8 us
    all_to_all x4, starting transfers between devices, exchange(): lax.all_to_all(blocks, 'lat', split_axis=0, concat_axis=0, tiled=True)  24 us
    all_to_all x4, waiting for transfers between devices, exchange(): lax.all_to_all(blocks, 'lat', split_axis=0, concat_axis=0, tiled=True)  11.8 us
    pallas_call x1, Pallas kernels, activation(): pl.pallas_call(body, grid=(lat_dev,), in_specs=[SMEM, pl.BlockSpec((1, lo...  10.2 us
    ppermute x6, starting transfers between devices, partner(): lax.ppermute(array, 'lat', [(i, i ^ by * stride) for i in range(count)])  6.54 us
    ppermute x2, starting transfers between devices, paired(): near = lax.ppermute(near_row, 'lat', [(i, i ^ 1) for i in range(count)])  3.76 us
    pallas_call x1, Pallas kernels, transform(): pl.pallas_call(body, in_specs=[SMEM] + [ANYWHERE] * 5, out_specs=[VMEM, A...  3.67 us
    pallas_call x1, Pallas kernels, final(): pl.pallas_call(body, in_specs=[VMEM, ANYWHERE, ANYWHERE], out_specs=[ANYW...  3.66 us
  transfers between devices with their start and end apart: 14, of which 4 were waited for; matrix products, arithmetic and copies ran while one was open for 1% of the time, Pallas kernels for 35%

profile of v5, /device:TPU:0, one launch (start us, length us, event | category | flops | bytes accessed | tf_op | source)
XLA Modules:
  0.0 97.2 jit_solution(12940847118901681243)
XLA Ops:
  0.7 3.7 %transform.1 = (bf16[128,768]{1,0:T(8,128)(2,1)}, bf16[1456,256]{1,0:T(8,128)(2,1)}, bf16[1456,256]{1,0:T(8,128)(2,1)}) custom-call(s32[1]{0:T(128)} %bitcast.p_ref, bf16[3,1440,256]{2,1,0:T(8,128)(2,1)} %rest_0_.5, bf16[128,1440]{1,0:T(8,128)(2,1)} %constant.51.clone.t_ref, s32[3,9]{1,0:T(4,128)} %row_ref.1, s32[3,9]{1,0:T(4,128)} %col_ref.1, ...), custom_call_target="tpu_custom_call" | custom-call | flops 283115520 | bytes 2211840 | tf_op jit(solution)/shard_map/transform/pallas_call | solution.py:249
  4.3 7.4 %all-to-all-start = ((bf16[16,8,768]{2,1,0:T(8,128)(2,1)}), bf16[16,8,768]{2,1,0:T(8,128)(2,1)S(1)}, u32[]{:S(2)}, u32[]{:S(2)}) async-start(bf16[16,8,768]{2,1,0:T(8,128)(2,1)} %bitcast.33), calls=%async_computation | async-start | bytes 393216 | tf_op jit(solution)/shard_map/all_to_all | solution.py:812
  11.7 0.7 collective-permute-start
  12.5 3.3 %collective-permute-start.1 = (bf16[1456,256]{1,0:T(8,128)(2,1)}, bf16[1456,256]{1,0:T(8,128)(2,1)S(1)}, u32[]{:S(2)}, u32[]{:S(2)}) collective-permute-start(bf16[1456,256]{1,0:T(8,128)(2,1)} %get-tuple-element.31), channel_id=1, source_target_pairs={{0,1},{1,0},{2,3},{3,2},{4,5},{5,4},{6,7},{7,6},{8,9},{9,8},{10,11... | collective-permute-start | bytes 2236424 | tf_op jit(solution)/shard_map/ppermute | solution.py:805
  15.8 0.1 subtract_select_fusion
  15.9 4.3 %filtered.3.rest_2_ = bf16[3,1440,768]{2,1,0:T(8,128)(2,1)} custom-call(s32[2]{0:T(128)S(1)} %pad_add_fusion.3.order_ref, s32[3,9]{1,0:T(4,128)S(1)} %get-tuple-element.63.shift_ref, f32[3,3,9]{2,1,0:T(4,128)S(1)} %get-tuple-element.65.tap_ref, bf16[3,1440,256]{2,1,0:T(8,128)(2,1)} %rest_0_.5), custom_call_target="tpu_custom_call" | custom-call | flops 530841600 | bytes 2949120 | tf_op jit(solution)/shard_map/filtered/pallas_call | solution.py:425
  20.2 0.5 all-to-all-done
  20.8 2.4 %spectral_forward.1 = (f32[288,256]{1,0:T(8,128)}, bf16[128,768]{1,0:T(8,128)(2,1)}) custom-call(s32[1]{0:T(128)} %bitcast.p_ref, bf16[128,768]{1,0:T(8,128)(2,1)S(1)} %bitcast.28, bf16[16,288,384]{2,1,0:T(8,128)(2,1)} %constant.56.clone.a_ref, bf16[16,288,384]{2,1,0:T(8,128)(2,1)} %constant.55.clone.b_ref, f32[48,256]{1,0:T(8,128)} %g_ref.5), custom_call_target="tpu_custom_call" | custom-call | tf_op jit(solution)/shard_map/spectral_forward/pallas_call | solution.py:469
  23.1 4.1 %all-to-all-start.1 = ((bf16[16,8,768]{2,1,0:T(8,128)(2,1)}), bf16[16,8,768]{2,1,0:T(8,128)(2,1)S(1)}, u32[]{:S(2)}, u32[]{:S(2)}) async-start(bf16[16,8,768]{2,1,0:T(8,128)(2,1)} %bitcast.34), calls=%async_computation.1 | async-start | bytes 393216 | tf_op jit(solution)/shard_map/all_to_all | solution.py:812
  27.3 0.1 pad_add_fusion.2.order_ref
  27.4 4.1 %filtered.4.rest_2_ = bf16[3,1440,768]{2,1,0:T(8,128)(2,1)} custom-call(s32[2]{0:T(128)S(1)} %pad_add_fusion.2.order_ref, s32[3,9]{1,0:T(4,128)S(1)} %get-tuple-element.63.shift_ref, f32[3,3,9]{2,1,0:T(4,128)S(1)} %get-tuple-element.65.tap_ref, bf16[3,1440,256]{2,1,0:T(8,128)(2,1)} %rest_0_.5, ...), custom_call_target="tpu_custom_call", output_to_operand_aliasing={{}: (5, {})} | custom-call | flops 530841600 | bytes 2949120 | tf_op jit(solution)/shard_map/filtered/pallas_call | solution.py:425
  31.5 4.1 %filtered.5.m_ref = bf16[3,1440,768]{2,1,0:T(8,128)(2,1)} custom-call(s32[2]{0:T(128)S(1)} %pad_add_fusion.1.order_ref, s32[3,9]{1,0:T(4,128)S(1)} %get-tuple-element.63.shift_ref, f32[3,3,9]{2,1,0:T(4,128)S(1)} %get-tuple-element.65.tap_ref, bf16[3,1440,256]{2,1,0:T(8,128)(2,1)} %rest_0_.5, ...), custom_call_target="tpu_custom_call", output_to_operand_aliasing={{}: (5, {})} | custom-call | flops 530841600 | bytes 2949120 | tf_op jit(solution)/shard_map/filtered/pallas_call | solution.py:425
  35.6 0.7 all-to-all-done.1
  36.3 10.2 %activation.1 = (bf16[3,1440,256]{2,1,0:T(8,128)(2,1)}, bf16[1440,256]{1,0:T(8,128)(2,1)}, bf16[1440,256]{1,0:T(8,128)(2,1)}, bf16[1440,256]{1,0:T(8,128)(2,1)}, bf16[16,24,768]{2,1,0:T(8,128)(2,1)}) custom-call(s32[1]{0:T(128)} %bitcast.p_ref, bf16[3,1440,768]{2,1,0:T(8,128)(2,1)} %filtered.5.m_ref, bf16[768,256]{1,0:T(8,128)(2,1)} %bitcast.30, ...), custom_call_target="tpu_custom_call" | custom-call | flops 3963617280 | bytes 15482880 | tf_op jit(solution)/shard_map/activation/pallas_call | solution.py:645
  46.5 8.0 %all-to-all-start.2 = ((bf16[16,24,768]{2,1,0:T(8,128)(2,1)}), bf16[16,24,768]{2,1,0:T(8,128)(2,1)S(1)}, u32[]{:S(2)}, u32[]{:S(2)}) async-start(bf16[16,24,768]{2,1,0:T(8,128)(2,1)} %get-tuple-element.37), calls=%async_computation.2 | async-start | bytes 1179648 | tf_op jit(solution)/shard_map/all_to_all | solution.py:812
  54.6 0.5 collective-permute-start.5
  55.0 0.7 collective-permute-start.6
  55.8 0.1 pad_add_fusion.shift_ref
  55.9 0.1 pad_maximum_fusion.6.tap_ref
  55.9 5.2 %filtered_back.2.rest_6_ = bf16[3,1440,256]{2,1,0:T(8,128)(2,1)} custom-call(s32[2]{0:T(128)S(1)} %pad_add_fusion.3.order_ref, s32[3,27]{1,0:T(4,128)S(1)} %pad_add_fusion.shift_ref, f32[3,3,27]{2,1,0:T(4,128)S(1)} %pad_maximum_fusion.6.tap_ref, bf16[1440,256]{1,0:T(8,128)(2,1)} %get-tuple-element.38.rest_0_, bf16[1440,256]{1,0:T(8,128)(2,1)} %get-tuple-element.39.rest_1_, ...), custom_call_target="tpu_custom_call" | custom-call | flops 1097072640 | bytes 2949120 | tf_op jit(solution)/shard_map/filtered_back/pallas_call | solution.py:425
  61.1 9.0 %all-to-all-done.2.x_ref = bf16[16,24,768]{2,1,0:T(8,128)(2,1)S(1)} async-done(((bf16[16,24,768]{2,1,0:T(8,128)(2,1)}), bf16[16,24,768]{2,1,0:T(8,128)(2,1)S(1)}, u32[]{:S(2)}, u32[]{:S(2)}) %all-to-all-start.2) | async-done | bytes 589856 | tf_op jit(solution)/shard_map/all_to_all | solution.py:812
  70.1 2.7 %spectral_adjoint.1 = (f32[48,256]{1,0:T(8,128)S(1)}, bf16[16,24,768]{2,1,0:T(8,128)(2,1)}) custom-call(s32[1]{0:T(128)} %bitcast.p_ref, bf16[16,24,768]{2,1,0:T(8,128)(2,1)S(1)} %all-to-all-done.2.x_ref, bf16[16,288,384]{2,1,0:T(8,128)(2,1)} %constant.55.clone.b_ref, bf16[16,288,384]{2,1,0:T(8,128)(2,1)} %constant.56.clone.a_ref, f32[48,256]{1,0:T(8,128)} %g_ref.5, ...), custom_call_target="tpu_custom_call" | custom-call | tf_op jit(solution)/shard_map/spectral_adjoint/pallas_call | solution.py:526
  72.8 4.5 %all-to-all-start.3 = ((bf16[16,24,768]{2,1,0:T(8,128)(2,1)}), bf16[16,24,768]{2,1,0:T(8,128)(2,1)S(1)}, u32[]{:S(2)}, u32[]{:S(2)}) async-start(bf16[16,24,768]{2,1,0:T(8,128)(2,1)} %get-tuple-element.46), calls=%async_computation.3 | async-start | bytes 1179648 | tf_op jit(solution)/shard_map/all_to_all | solution.py:812
  77.3 0.1 pad_add_fusion.4.order_ref
  77.4 1.7 %collective-permute-start.4 = (bf16[48,256]{1,0:T(8,128)(2,1)S(1)}, bf16[48,256]{1,0:T(8,128)(2,1)S(1)}, u32[]{:S(2)}, u32[]{:S(2)}) collective-permute-start(bf16[48,256]{1,0:T(8,128)(2,1)S(1)} %convert_element_type.66), channel_id=1, source_target_pairs={{0,3},{1,2},{2,1},{3,0},{4,7},{5,6},{6,5},{7,4},{8,11},{9,10},{10,... | collective-permute-start | bytes 73736 | tf_op jit(solution)/shard_map/ppermute | solution.py:760
  79.1 0.4 collective-permute-start.3
  79.5 7.3 %filtered_back.3.d_ref = bf16[3,1440,256]{2,1,0:T(8,128)(2,1)} custom-call(s32[3]{0:T(128)S(1)} %pad_add_fusion.4.order_ref, s32[3,27]{1,0:T(4,128)S(1)} %pad_add_fusion.shift_ref, f32[3,3,27]{2,1,0:T(4,128)S(1)} %pad_maximum_fusion.6.tap_ref, bf16[1440,256]{1,0:T(8,128)(2,1)} %get-tuple-element.38.rest_0_, ...), custom_call_target="tpu_custom_call", output_to_operand_aliasing={{}: (9, {})} | custom-call | flops 2194145280 | bytes 5898240 | tf_op jit(solution)/shard_map/filtered_back/pallas_call | solution.py:425
  86.8 3.6 %collective-permute-start.9 = (bf16[48,256]{1,0:T(8,128)(2,1)S(1)}, bf16[48,256]{1,0:T(8,128)(2,1)S(1)}, u32[]{:S(2)}, u32[]{:S(2)}) collective-permute-start(bf16[48,256]{1,0:T(8,128)(2,1)S(1)} %add_add_fusion.1), channel_id=1, source_target_pairs={{0,12},{1,13},{2,14},{3,15},{4,8},{5,9},{6,10},{7,11},{8,4},{9,5},... | collective-permute-start | bytes 73736 | tf_op jit(solution)/shard_map/ppermute | solution.py:760
  90.4 0.9 collective-permute-start.7
  91.2 1.6 %all-to-all-done.3.y_ref = bf16[16,24,768]{2,1,0:T(8,128)(2,1)S(1)} async-done(((bf16[16,24,768]{2,1,0:T(8,128)(2,1)}), bf16[16,24,768]{2,1,0:T(8,128)(2,1)S(1)}, u32[]{:S(2)}, u32[]{:S(2)}) %all-to-all-start.3) | async-done | bytes 589856 | tf_op jit(solution)/shard_map/all_to_all | solution.py:812
  92.8 3.7 %final.1 = (bf16[3,1440,256]{2,1,0:T(8,128)(2,1)}, f32[16,3,16,256]{3,2,1,0:T(8,128)}) custom-call(bf16[16,24,768]{2,1,0:T(8,128)(2,1)S(1)} %all-to-all-done.3.y_ref, bf16[1440,128]{1,0:T(8,128)(2,1)} %constant.53.clone.f_ref, bf16[3,1440,256]{2,1,0:T(8,128)(2,1)} %filtered_back.3.d_ref), custom_call_target="tpu_custom_call" | custom-call | flops 283115520 | bytes 6635520 | tf_op jit(solution)/shard_map/final/pallas_call | solution.py:729
  96.5 0.6 add_add_fusion
  (29 shorter events, 0.3 us)
Async XLA Ops:
  0.6 15.3 %copy-start = (bf16[3,3,9]{2,1,0:T(4,128)(2,1)S(1)}, bf16[3,3,9]{2,1,0:T(4,128)(2,1)}, u32[]{:S(2)}) copy-start(bf16[3,3,9]{2,1,0:T(4,128)(2,1)} %basis_ref.1) | copy-start | bytes 490
  0.6 15.1 %copy-start.1 = (s32[3,9]{1,0:T(4,128)S(1)}, s32[3,9]{1,0:T(4,128)}, u32[]{:S(2)}) copy-start(s32[3,9]{1,0:T(4,128)} %col_ref.1) | copy-start | bytes 328
  0.7 15.1 %copy-start.2 = (s32[3,9]{1,0:T(4,128)S(1)}, s32[3,9]{1,0:T(4,128)}, u32[]{:S(2)}) copy-start(s32[3,9]{1,0:T(4,128)} %row_ref.1) | copy-start | bytes 328
  4.3 16.4 %all-to-all-start = ((bf16[16,8,768]{2,1,0:T(8,128)(2,1)}), bf16[16,8,768]{2,1,0:T(8,128)(2,1)S(1)}, u32[]{:S(2)}, u32[]{:S(2)}) async-start(bf16[16,8,768]{2,1,0:T(8,128)(2,1)} %bitcast.33), calls=%async_computation | async-start | bytes 393216 | tf_op jit(solution)/shard_map/all_to_all | solution.py:812
  11.7 19.8 %collective-permute-start = (bf16[1456,256]{1,0:T(8,128)(2,1)}, bf16[1456,256]{1,0:T(8,128)(2,1)S(1)}, u32[]{:S(2)}, u32[]{:S(2)}) collective-permute-start(bf16[1456,256]{1,0:T(8,128)(2,1)} %get-tuple-element.30), channel_id=1, source_target_pairs={{1,2},{3,4},{5,6},{7,8},{9,10},{11,12},{13,14},{2,1},{4,3},{6,5},{... | collective-permute-start | bytes 2236424 | tf_op jit(solution)/shard_map/ppermute | solution.py:807
  12.5 15.0 %collective-permute-start.1 = (bf16[1456,256]{1,0:T(8,128)(2,1)}, bf16[1456,256]{1,0:T(8,128)(2,1)S(1)}, u32[]{:S(2)}, u32[]{:S(2)}) collective-permute-start(bf16[1456,256]{1,0:T(8,128)(2,1)} %get-tuple-element.31), channel_id=1, source_target_pairs={{0,1},{1,0},{2,3},{3,2},{4,5},{5,4},{6,7},{7,6},{8,9},{9,8},{10,11... | collective-permute-start | bytes 2236424 | tf_op jit(solution)/shard_map/ppermute | solution.py:805
  23.1 13.1 %all-to-all-start.1 = ((bf16[16,8,768]{2,1,0:T(8,128)(2,1)}), bf16[16,8,768]{2,1,0:T(8,128)(2,1)S(1)}, u32[]{:S(2)}, u32[]{:S(2)}) async-start(bf16[16,8,768]{2,1,0:T(8,128)(2,1)} %bitcast.34), calls=%async_computation.1 | async-start | bytes 393216 | tf_op jit(solution)/shard_map/all_to_all | solution.py:812
  46.5 23.6 %all-to-all-start.2 = ((bf16[16,24,768]{2,1,0:T(8,128)(2,1)}), bf16[16,24,768]{2,1,0:T(8,128)(2,1)S(1)}, u32[]{:S(2)}, u32[]{:S(2)}) async-start(bf16[16,24,768]{2,1,0:T(8,128)(2,1)} %get-tuple-element.37), calls=%async_computation.2 | async-start | bytes 1179648 | tf_op jit(solution)/shard_map/all_to_all | solution.py:812
  54.6 24.9 %collective-permute-start.5 = (bf16[1440,256]{1,0:T(8,128)(2,1)}, bf16[1440,256]{1,0:T(8,128)(2,1)S(1)}, u32[]{:S(2)}, u32[]{:S(2)}) collective-permute-start(bf16[1440,256]{1,0:T(8,128)(2,1)} %get-tuple-element.38.rest_0_), channel_id=1, source_target_pairs={{0,1},{1,0},{2,3},{3,2},{4,5},{5,4},{6,7},{7,6},{8,9},{9,8},{10,11... | collective-permute-start | bytes 2211848 | tf_op jit(solution)/shard_map/ppermute | solution.py:805
  55.0 24.4 %collective-permute-start.6 = (bf16[1440,256]{1,0:T(8,128)(2,1)}, bf16[1440,256]{1,0:T(8,128)(2,1)S(1)}, u32[]{:S(2)}, u32[]{:S(2)}) collective-permute-start(bf16[1440,256]{1,0:T(8,128)(2,1)} %get-tuple-element.40.rest_2_), channel_id=1, source_target_pairs={{1,2},{3,4},{5,6},{7,8},{9,10},{11,12},{13,14},{2,1},{4,3},{6,5},{... | collective-permute-start | bytes 2211848 | tf_op jit(solution)/shard_map/ppermute | solution.py:807
  72.8 20.0 %all-to-all-start.3 = ((bf16[16,24,768]{2,1,0:T(8,128)(2,1)}), bf16[16,24,768]{2,1,0:T(8,128)(2,1)S(1)}, u32[]{:S(2)}, u32[]{:S(2)}) async-start(bf16[16,24,768]{2,1,0:T(8,128)(2,1)} %get-tuple-element.46), calls=%async_computation.3 | async-start | bytes 1179648 | tf_op jit(solution)/shard_map/all_to_all | solution.py:812
  77.4 9.4 %collective-permute-start.4 = (bf16[48,256]{1,0:T(8,128)(2,1)S(1)}, bf16[48,256]{1,0:T(8,128)(2,1)S(1)}, u32[]{:S(2)}, u32[]{:S(2)}) collective-permute-start(bf16[48,256]{1,0:T(8,128)(2,1)S(1)} %convert_element_type.66), channel_id=1, source_target_pairs={{0,3},{1,2},{2,1},{3,0},{4,7},{5,6},{6,5},{7,4},{8,11},{9,10},{10,... | collective-permute-start | bytes 73736 | tf_op jit(solution)/shard_map/ppermute | solution.py:760
  79.1 7.7 %collective-permute-start.3 = (bf16[48,256]{1,0:T(8,128)(2,1)S(1)}, bf16[48,256]{1,0:T(8,128)(2,1)S(1)}, u32[]{:S(2)}, u32[]{:S(2)}) collective-permute-start(bf16[48,256]{1,0:T(8,128)(2,1)S(1)} %convert_element_type.66), channel_id=1, source_target_pairs={{0,2},{1,3},{2,0},{3,1},{4,6},{5,7},{6,4},{7,5},{8,10},{9,11},{10,... | collective-permute-start | bytes 73736 | tf_op jit(solution)/shard_map/ppermute | solution.py:760
  79.5 7.3 %collective-permute-start.2 = (bf16[48,256]{1,0:T(8,128)(2,1)S(1)}, bf16[48,256]{1,0:T(8,128)(2,1)S(1)}, u32[]{:S(2)}, u32[]{:S(2)}) collective-permute-start(bf16[48,256]{1,0:T(8,128)(2,1)S(1)} %convert_element_type.66), channel_id=1, source_target_pairs={{0,1},{1,0},{2,3},{3,2},{4,5},{5,4},{6,7},{7,6},{8,9},{9,8},{10,11... | collective-permute-start | bytes 73736 | tf_op jit(solution)/shard_map/ppermute | solution.py:760
  86.8 9.7 %collective-permute-start.9 = (bf16[48,256]{1,0:T(8,128)(2,1)S(1)}, bf16[48,256]{1,0:T(8,128)(2,1)S(1)}, u32[]{:S(2)}, u32[]{:S(2)}) collective-permute-start(bf16[48,256]{1,0:T(8,128)(2,1)S(1)} %add_add_fusion.1), channel_id=1, source_target_pairs={{0,12},{1,13},{2,14},{3,15},{4,8},{5,9},{6,10},{7,11},{8,4},{9,5},... | collective-permute-start | bytes 73736 | tf_op jit(solution)/shard_map/ppermute | solution.py:760
  90.4 6.2 %collective-permute-start.8 = (bf16[48,256]{1,0:T(8,128)(2,1)S(1)}, bf16[48,256]{1,0:T(8,128)(2,1)S(1)}, u32[]{:S(2)}, u32[]{:S(2)}) collective-permute-start(bf16[48,256]{1,0:T(8,128)(2,1)S(1)} %add_add_fusion.1), channel_id=1, source_target_pairs={{0,8},{1,9},{2,10},{3,11},{4,12},{5,13},{6,14},{7,15},{8,0},{9,1},... | collective-permute-start | bytes 73736 | tf_op jit(solution)/shard_map/ppermute | solution.py:760
  90.4 6.2 %collective-permute-start.7 = (bf16[48,256]{1,0:T(8,128)(2,1)S(1)}, bf16[48,256]{1,0:T(8,128)(2,1)S(1)}, u32[]{:S(2)}, u32[]{:S(2)}) collective-permute-start(bf16[48,256]{1,0:T(8,128)(2,1)S(1)} %add_add_fusion.1), channel_id=1, source_target_pairs={{0,4},{1,5},{2,6},{3,7},{4,0},{5,1},{6,2},{7,3},{8,12},{9,13},{10,... | collective-permute-start | bytes 73736 | tf_op jit(solution)/shard_map/ppermute | solution.py:760

commit v6 on v5

--- a/solution.py
+++ b/solution.py
@@ -323,15 +323,19 @@
         if far is not None:
             sources.append((beyond_refs[-1], odd * (lat_dev + 1)))
 
-        def copies(which):
+        cut = lon // chunk // 2 * chunk + 2 * SPAN + STEP // 3
+        pieces = (
+            ((lon - SPAN, 0, SPAN), (0, SPAN, cut)),
+            ((cut, SPAN + cut, lon - cut), (0, lon + SPAN, SPAN)),
+        )
+
+        def copies(which, half):
             return [
                 pltpu.make_async_copy(
-                    src.at[pl.ds(a, size)], ext.at[to, pl.ds(b, size)], sem.at[s, n]
+                    src.at[pl.ds(a, size)], ext.at[to, pl.ds(b, size)], sem.at[s, 2 * half + n]
                 )
                 for s, (src, to) in list(enumerate(sources))[which]
-                for n, (a, b, size) in enumerate(
-                    ((0, SPAN, lon), (lon - SPAN, 0, SPAN), (0, lon + SPAN, SPAN))
-                )
+                for n, (a, b, size) in enumerate(pieces[half])
             ]
 
         late = -1 if far is not None and total > 1 else len(sources)
@@ -346,8 +350,9 @@
 
         @pl.when(step_id == 0)
         def _():
-            for copy in copies(slice(None)):
-                copy.start()
+            for half in range(2):
+                for copy in copies(slice(None), half):
+                    copy.start()
 
         across = lax.broadcasted_iota(jnp.int32, (STEP, 3 * WIN), 1)
         down = lax.broadcasted_iota(jnp.int32, (STEP, 3 * WIN), 0)
@@ -361,17 +366,26 @@
 
         @pl.when(step_id == 0)
         def _():
-            for copy in copies(slice(None, late)):
-                copy.wait()
+            for half in range(1 if keep else 2):
+                for copy in copies(slice(None, late), half):
+                    copy.wait()
 
         if late == -1:
 
             @pl.when(step_id == total - 1)
             def _():
-                for copy in copies(slice(late, None)):
-                    copy.wait()
+                for half in range(2):
+                    for copy in copies(slice(late, None), half):
+                        copy.wait()
 
         for c in range(lon // chunk):
+            if keep and c == lon // chunk // 2:
+
+                @pl.when(step_id == 0)
+                def _():
+                    for copy in copies(slice(None, late), 1):
+                        copy.wait()
+
             for b in range(per):
                 start = c * chunk + b * STEP
                 window = jnp.concatenate(
@@ -409,7 +423,7 @@
     in_specs = [SMEM, SMEM] + [ANYWHERE] * (len(middle) + len(beyond))
     scratch = [
         pltpu.VMEM((lat_dev + 2, lon + 2 * SPAN, channels), BF16),
-        pltpu.SemaphoreType.DMA((lat_dev + 2, 3)),
+        pltpu.SemaphoreType.DMA((lat_dev + 2, 4)),
         pltpu.VMEM((total, lon, depth), BF16),
         pltpu.SemaphoreType.DMA((total, 2)),
     ]

time: 98.4 us -> 98.4 us (level)
  transfers between devices with their start and end apart: 14 -> 14, of which waited for: 4 -> 4; matrix products, arithmetic and copies ran while one was open for 1% -> 1% of each run, Pallas kernels for 35% -> 34%
where the time goes in v6:
time: 98.4 us; the launch traced here: 97.1 us
  Pallas kernels  47.3 us (48%)
  starting transfers between devices  35.6 us (36%)
  waiting for transfers between devices  12.1 us (12%)
  other arithmetic  1.23 us (1%)
    pallas_call x5, Pallas kernels, filtered(): pl.pallas_call(body, grid=(total,), in_specs=[SMEM] + in_specs, out_specs...  24.6 us
    all_to_all x4, starting transfers between devices, exchange(): lax.all_to_all(blocks, 'lat', split_axis=0, concat_axis=0, tiled=True)  23.9 us
    all_to_all x4, waiting for transfers between devices, exchange(): lax.all_to_all(blocks, 'lat', split_axis=0, concat_axis=0, tiled=True)  12 us
    pallas_call x1, Pallas kernels, activation(): pl.pallas_call(body, grid=(lat_dev,), in_specs=[SMEM, pl.BlockSpec((1, lo...  10.2 us
    ppermute x6, starting transfers between devices, partner(): lax.ppermute(array, 'lat', [(i, i ^ by * stride) for i in range(count)])  6.54 us
    ppermute x2, starting transfers between devices, paired(): near = lax.ppermute(near_row, 'lat', [(i, i ^ 1) for i in range(count)])  3.76 us
    pallas_call x1, Pallas kernels, transform(): pl.pallas_call(body, in_specs=[SMEM] + [ANYWHERE] * 5, out_specs=[VMEM, A...  3.67 us
    pallas_call x1, Pallas kernels, final(): pl.pallas_call(body, in_specs=[VMEM, ANYWHERE, ANYWHERE], out_specs=[ANYW...  3.66 us
  transfers between devices with their start and end apart: 14, of which 4 were waited for; matrix products, arithmetic and copies ran while one was open for 1% of the time, Pallas kernels for 34%

profile of v6, /device:TPU:0, one launch (start us, length us, event | category | flops | bytes accessed | tf_op | source)
XLA Modules:
  0.0 97.1 jit_solution(3135931078954638026)
XLA Ops:
  0.7 3.7 %transform.1 = (bf16[128,768]{1,0:T(8,128)(2,1)}, bf16[1456,256]{1,0:T(8,128)(2,1)}, bf16[1456,256]{1,0:T(8,128)(2,1)}) custom-call(s32[1]{0:T(128)} %bitcast.p_ref, bf16[3,1440,256]{2,1,0:T(8,128)(2,1)} %rest_0_.5, bf16[128,1440]{1,0:T(8,128)(2,1)} %constant.51.clone.t_ref, s32[3,9]{1,0:T(4,128)} %row_ref.1, s32[3,9]{1,0:T(4,128)} %col_ref.1, ...), custom_call_target="tpu_custom_call" | custom-call | flops 283115520 | bytes 2211840 | tf_op jit(solution)/shard_map/transform/pallas_call | solution.py:249
  4.3 7.4 %all-to-all-start = ((bf16[16,8,768]{2,1,0:T(8,128)(2,1)}), bf16[16,8,768]{2,1,0:T(8,128)(2,1)S(1)}, u32[]{:S(2)}, u32[]{:S(2)}) async-start(bf16[16,8,768]{2,1,0:T(8,128)(2,1)} %bitcast.33), calls=%async_computation | async-start | bytes 393216 | tf_op jit(solution)/shard_map/all_to_all | solution.py:826
  11.7 0.7 collective-permute-start
  12.5 3.3 %collective-permute-start.1 = (bf16[1456,256]{1,0:T(8,128)(2,1)}, bf16[1456,256]{1,0:T(8,128)(2,1)S(1)}, u32[]{:S(2)}, u32[]{:S(2)}) collective-permute-start(bf16[1456,256]{1,0:T(8,128)(2,1)} %get-tuple-element.31), channel_id=1, source_target_pairs={{0,1},{1,0},{2,3},{3,2},{4,5},{5,4},{6,7},{7,6},{8,9},{9,8},{10,11... | collective-permute-start | bytes 2236424 | tf_op jit(solution)/shard_map/ppermute | solution.py:819
  15.8 0.1 subtract_select_fusion
  15.9 4.1 %filtered.3.rest_2_ = bf16[3,1440,768]{2,1,0:T(8,128)(2,1)} custom-call(s32[2]{0:T(128)S(1)} %pad_add_fusion.3.order_ref, s32[3,9]{1,0:T(4,128)S(1)} %get-tuple-element.63.shift_ref, f32[3,3,9]{2,1,0:T(4,128)S(1)} %get-tuple-element.65.tap_ref, bf16[3,1440,256]{2,1,0:T(8,128)(2,1)} %rest_0_.5), custom_call_target="tpu_custom_call" | custom-call | flops 530841600 | bytes 2949120 | tf_op jit(solution)/shard_map/filtered/pallas_call | solution.py:439
  20.0 0.7 all-to-all-done
  20.8 2.4 %spectral_forward.1 = (f32[288,256]{1,0:T(8,128)}, bf16[128,768]{1,0:T(8,128)(2,1)}) custom-call(s32[1]{0:T(128)} %bitcast.p_ref, bf16[128,768]{1,0:T(8,128)(2,1)S(1)} %bitcast.28, bf16[16,288,384]{2,1,0:T(8,128)(2,1)} %constant.56.clone.a_ref, bf16[16,288,384]{2,1,0:T(8,128)(2,1)} %constant.55.clone.b_ref, f32[48,256]{1,0:T(8,128)} %g_ref.5), custom_call_target="tpu_custom_call" | custom-call | tf_op jit(solution)/shard_map/spectral_forward/pallas_call | solution.py:483
  23.1 3.9 %all-to-all-start.1 = ((bf16[16,8,768]{2,1,0:T(8,128)(2,1)}), bf16[16,8,768]{2,1,0:T(8,128)(2,1)S(1)}, u32[]{:S(2)}, u32[]{:S(2)}) async-start(bf16[16,8,768]{2,1,0:T(8,128)(2,1)} %bitcast.34), calls=%async_computation.1 | async-start | bytes 393216 | tf_op jit(solution)/shard_map/all_to_all | solution.py:826
  27.1 0.1 pad_add_fusion.2.order_ref
  27.3 4.0 %filtered.4.rest_2_ = bf16[3,1440,768]{2,1,0:T(8,128)(2,1)} custom-call(s32[2]{0:T(128)S(1)} %pad_add_fusion.2.order_ref, s32[3,9]{1,0:T(4,128)S(1)} %get-tuple-element.63.shift_ref, f32[3,3,9]{2,1,0:T(4,128)S(1)} %get-tuple-element.65.tap_ref, bf16[3,1440,256]{2,1,0:T(8,128)(2,1)} %rest_0_.5, ...), custom_call_target="tpu_custom_call", output_to_operand_aliasing={{}: (5, {})} | custom-call | flops 530841600 | bytes 2949120 | tf_op jit(solution)/shard_map/filtered/pallas_call | solution.py:439
  31.3 4.0 %filtered.5.m_ref = bf16[3,1440,768]{2,1,0:T(8,128)(2,1)} custom-call(s32[2]{0:T(128)S(1)} %pad_add_fusion.1.order_ref, s32[3,9]{1,0:T(4,128)S(1)} %get-tuple-element.63.shift_ref, f32[3,3,9]{2,1,0:T(4,128)S(1)} %get-tuple-element.65.tap_ref, bf16[3,1440,256]{2,1,0:T(8,128)(2,1)} %rest_0_.5, ...), custom_call_target="tpu_custom_call", output_to_operand_aliasing={{}: (5, {})} | custom-call | flops 530841600 | bytes 2949120 | tf_op jit(solution)/shard_map/filtered/pallas_call | solution.py:439
  35.2 0.9 all-to-all-done.1
  36.1 10.2 %activation.1 = (bf16[3,1440,256]{2,1,0:T(8,128)(2,1)}, bf16[1440,256]{1,0:T(8,128)(2,1)}, bf16[1440,256]{1,0:T(8,128)(2,1)}, bf16[1440,256]{1,0:T(8,128)(2,1)}, bf16[16,24,768]{2,1,0:T(8,128)(2,1)}) custom-call(s32[1]{0:T(128)} %bitcast.p_ref, bf16[3,1440,768]{2,1,0:T(8,128)(2,1)} %filtered.5.m_ref, bf16[768,256]{1,0:T(8,128)(2,1)} %bitcast.30, ...), custom_call_target="tpu_custom_call" | custom-call | flops 3963617280 | bytes 15482880 | tf_op jit(solution)/shard_map/activation/pallas_call | solution.py:659
  46.4 8.1 %all-to-all-start.2 = ((bf16[16,24,768]{2,1,0:T(8,128)(2,1)}), bf16[16,24,768]{2,1,0:T(8,128)(2,1)S(1)}, u32[]{:S(2)}, u32[]{:S(2)}) async-start(bf16[16,24,768]{2,1,0:T(8,128)(2,1)} %get-tuple-element.37), calls=%async_computation.2 | async-start | bytes 1179648 | tf_op jit(solution)/shard_map/all_to_all | solution.py:826
  54.5 0.5 collective-permute-start.5
  54.9 0.7 collective-permute-start.6
  55.7 0.1 pad_add_fusion.shift_ref
  55.8 0.1 pad_maximum_fusion.6.tap_ref
  55.8 5.2 %filtered_back.2.rest_6_ = bf16[3,1440,256]{2,1,0:T(8,128)(2,1)} custom-call(s32[2]{0:T(128)S(1)} %pad_add_fusion.3.order_ref, s32[3,27]{1,0:T(4,128)S(1)} %pad_add_fusion.shift_ref, f32[3,3,27]{2,1,0:T(4,128)S(1)} %pad_maximum_fusion.6.tap_ref, bf16[1440,256]{1,0:T(8,128)(2,1)} %get-tuple-element.38.rest_0_, bf16[1440,256]{1,0:T(8,128)(2,1)} %get-tuple-element.39.rest_1_, ...), custom_call_target="tpu_custom_call" | custom-call | flops 1097072640 | bytes 2949120 | tf_op jit(solution)/shard_map/filtered_back/pallas_call | solution.py:439
  61.0 9.0 %all-to-all-done.2.x_ref = bf16[16,24,768]{2,1,0:T(8,128)(2,1)S(1)} async-done(((bf16[16,24,768]{2,1,0:T(8,128)(2,1)}), bf16[16,24,768]{2,1,0:T(8,128)(2,1)S(1)}, u32[]{:S(2)}, u32[]{:S(2)}) %all-to-all-start.2) | async-done | bytes 589856 | tf_op jit(solution)/shard_map/all_to_all | solution.py:826
  70.0 2.7 %spectral_adjoint.1 = (f32[48,256]{1,0:T(8,128)S(1)}, bf16[16,24,768]{2,1,0:T(8,128)(2,1)}) custom-call(s32[1]{0:T(128)} %bitcast.p_ref, bf16[16,24,768]{2,1,0:T(8,128)(2,1)S(1)} %all-to-all-done.2.x_ref, bf16[16,288,384]{2,1,0:T(8,128)(2,1)} %constant.55.clone.b_ref, bf16[16,288,384]{2,1,0:T(8,128)(2,1)} %constant.56.clone.a_ref, f32[48,256]{1,0:T(8,128)} %g_ref.5, ...), custom_call_target="tpu_custom_call" | custom-call | tf_op jit(solution)/shard_map/spectral_adjoint/pallas_call | solution.py:540
  72.7 4.5 %all-to-all-start.3 = ((bf16[16,24,768]{2,1,0:T(8,128)(2,1)}), bf16[16,24,768]{2,1,0:T(8,128)(2,1)S(1)}, u32[]{:S(2)}, u32[]{:S(2)}) async-start(bf16[16,24,768]{2,1,0:T(8,128)(2,1)} %get-tuple-element.46), calls=%async_computation.3 | async-start | bytes 1179648 | tf_op jit(solution)/shard_map/all_to_all | solution.py:826
  77.2 0.1 pad_add_fusion.4.order_ref
  77.3 1.7 %collective-permute-start.4 = (bf16[48,256]{1,0:T(8,128)(2,1)S(1)}, bf16[48,256]{1,0:T(8,128)(2,1)S(1)}, u32[]{:S(2)}, u32[]{:S(2)}) collective-permute-start(bf16[48,256]{1,0:T(8,128)(2,1)S(1)} %convert_element_type.66), channel_id=1, source_target_pairs={{0,3},{1,2},{2,1},{3,0},{4,7},{5,6},{6,5},{7,4},{8,11},{9,10},{10,... | collective-permute-start | bytes 73736 | tf_op jit(solution)/shard_map/ppermute | solution.py:774
  79.0 0.4 collective-permute-start.3
  79.4 7.4 %filtered_back.3.d_ref = bf16[3,1440,256]{2,1,0:T(8,128)(2,1)} custom-call(s32[3]{0:T(128)S(1)} %pad_add_fusion.4.order_ref, s32[3,27]{1,0:T(4,128)S(1)} %pad_add_fusion.shift_ref, f32[3,3,27]{2,1,0:T(4,128)S(1)} %pad_maximum_fusion.6.tap_ref, bf16[1440,256]{1,0:T(8,128)(2,1)} %get-tuple-element.38.rest_0_, ...), custom_call_target="tpu_custom_call", output_to_operand_aliasing={{}: (9, {})} | custom-call | flops 2194145280 | bytes 5898240 | tf_op jit(solution)/shard_map/filtered_back/pallas_call | solution.py:439
  86.8 3.6 %collective-permute-start.9 = (bf16[48,256]{1,0:T(8,128)(2,1)S(1)}, bf16[48,256]{1,0:T(8,128)(2,1)S(1)}, u32[]{:S(2)}, u32[]{:S(2)}) collective-permute-start(bf16[48,256]{1,0:T(8,128)(2,1)S(1)} %add_add_fusion.1), channel_id=1, source_target_pairs={{0,12},{1,13},{2,14},{3,15},{4,8},{5,9},{6,10},{7,11},{8,4},{9,5},... | collective-permute-start | bytes 73736 | tf_op jit(solution)/shard_map/ppermute | solution.py:774
  90.4 0.9 collective-permute-start.7
  91.3 1.4 %all-to-all-done.3.y_ref = bf16[16,24,768]{2,1,0:T(8,128)(2,1)S(1)} async-done(((bf16[16,24,768]{2,1,0:T(8,128)(2,1)}), bf16[16,24,768]{2,1,0:T(8,128)(2,1)S(1)}, u32[]{:S(2)}, u32[]{:S(2)}) %all-to-all-start.3) | async-done | bytes 589856 | tf_op jit(solution)/shard_map/all_to_all | solution.py:826
  92.7 3.7 %final.1 = (bf16[3,1440,256]{2,1,0:T(8,128)(2,1)}, f32[16,3,16,256]{3,2,1,0:T(8,128)}) custom-call(bf16[16,24,768]{2,1,0:T(8,128)(2,1)S(1)} %all-to-all-done.3.y_ref, bf16[1440,128]{1,0:T(8,128)(2,1)} %constant.53.clone.f_ref, bf16[3,1440,256]{2,1,0:T(8,128)(2,1)} %filtered_back.3.d_ref), custom_call_target="tpu_custom_call" | custom-call | flops 283115520 | bytes 6635520 | tf_op jit(solution)/shard_map/final/pallas_call | solution.py:743
  96.4 0.6 add_add_fusion
  (29 shorter events, 0.3 us)
Async XLA Ops:
  0.6 15.3 %copy-start = (bf16[3,3,9]{2,1,0:T(4,128)(2,1)S(1)}, bf16[3,3,9]{2,1,0:T(4,128)(2,1)}, u32[]{:S(2)}) copy-start(bf16[3,3,9]{2,1,0:T(4,128)(2,1)} %basis_ref.1) | copy-start | bytes 490
  0.6 15.1 %copy-start.1 = (s32[3,9]{1,0:T(4,128)S(1)}, s32[3,9]{1,0:T(4,128)}, u32[]{:S(2)}) copy-start(s32[3,9]{1,0:T(4,128)} %col_ref.1) | copy-start | bytes 328
  0.7 15.1 %copy-start.2 = (s32[3,9]{1,0:T(4,128)S(1)}, s32[3,9]{1,0:T(4,128)}, u32[]{:S(2)}) copy-start(s32[3,9]{1,0:T(4,128)} %row_ref.1) | copy-start | bytes 328
  4.3 16.4 %all-to-all-start = ((bf16[16,8,768]{2,1,0:T(8,128)(2,1)}), bf16[16,8,768]{2,1,0:T(8,128)(2,1)S(1)}, u32[]{:S(2)}, u32[]{:S(2)}) async-start(bf16[16,8,768]{2,1,0:T(8,128)(2,1)} %bitcast.33), calls=%async_computation | async-start | bytes 393216 | tf_op jit(solution)/shard_map/all_to_all | solution.py:826
  11.7 19.5 %collective-permute-start = (bf16[1456,256]{1,0:T(8,128)(2,1)}, bf16[1456,256]{1,0:T(8,128)(2,1)S(1)}, u32[]{:S(2)}, u32[]{:S(2)}) collective-permute-start(bf16[1456,256]{1,0:T(8,128)(2,1)} %get-tuple-element.30), channel_id=1, source_target_pairs={{1,2},{3,4},{5,6},{7,8},{9,10},{11,12},{13,14},{2,1},{4,3},{6,5},{... | collective-permute-start | bytes 2236424 | tf_op jit(solution)/shard_map/ppermute | solution.py:821
  12.5 14.8 %collective-permute-start.1 = (bf16[1456,256]{1,0:T(8,128)(2,1)}, bf16[1456,256]{1,0:T(8,128)(2,1)S(1)}, u32[]{:S(2)}, u32[]{:S(2)}) collective-permute-start(bf16[1456,256]{1,0:T(8,128)(2,1)} %get-tuple-element.31), channel_id=1, source_target_pairs={{0,1},{1,0},{2,3},{3,2},{4,5},{5,4},{6,7},{7,6},{8,9},{9,8},{10,11... | collective-permute-start | bytes 2236424 | tf_op jit(solution)/shard_map/ppermute | solution.py:819
  23.1 12.9 %all-to-all-start.1 = ((bf16[16,8,768]{2,1,0:T(8,128)(2,1)}), bf16[16,8,768]{2,1,0:T(8,128)(2,1)S(1)}, u32[]{:S(2)}, u32[]{:S(2)}) async-start(bf16[16,8,768]{2,1,0:T(8,128)(2,1)} %bitcast.34), calls=%async_computation.1 | async-start | bytes 393216 | tf_op jit(solution)/shard_map/all_to_all | solution.py:826
  46.4 23.7 %all-to-all-start.2 = ((bf16[16,24,768]{2,1,0:T(8,128)(2,1)}), bf16[16,24,768]{2,1,0:T(8,128)(2,1)S(1)}, u32[]{:S(2)}, u32[]{:S(2)}) async-start(bf16[16,24,768]{2,1,0:T(8,128)(2,1)} %get-tuple-element.37), calls=%async_computation.2 | async-start | bytes 1179648 | tf_op jit(solution)/shard_map/all_to_all | solution.py:826
  54.5 24.9 %collective-permute-start.5 = (bf16[1440,256]{1,0:T(8,128)(2,1)}, bf16[1440,256]{1,0:T(8,128)(2,1)S(1)}, u32[]{:S(2)}, u32[]{:S(2)}) collective-permute-start(bf16[1440,256]{1,0:T(8,128)(2,1)} %get-tuple-element.38.rest_0_), channel_id=1, source_target_pairs={{0,1},{1,0},{2,3},{3,2},{4,5},{5,4},{6,7},{7,6},{8,9},{9,8},{10,11... | collective-permute-start | bytes 2211848 | tf_op jit(solution)/shard_map/ppermute | solution.py:819
  54.9 24.4 %collective-permute-start.6 = (bf16[1440,256]{1,0:T(8,128)(2,1)}, bf16[1440,256]{1,0:T(8,128)(2,1)S(1)}, u32[]{:S(2)}, u32[]{:S(2)}) collective-permute-start(bf16[1440,256]{1,0:T(8,128)(2,1)} %get-tuple-element.40.rest_2_), channel_id=1, source_target_pairs={{1,2},{3,4},{5,6},{7,8},{9,10},{11,12},{13,14},{2,1},{4,3},{6,5},{... | collective-permute-start | bytes 2211848 | tf_op jit(solution)/shard_map/ppermute | solution.py:821
  72.7 20.0 %all-to-all-start.3 = ((bf16[16,24,768]{2,1,0:T(8,128)(2,1)}), bf16[16,24,768]{2,1,0:T(8,128)(2,1)S(1)}, u32[]{:S(2)}, u32[]{:S(2)}) async-start(bf16[16,24,768]{2,1,0:T(8,128)(2,1)} %get-tuple-element.46), calls=%async_computation.3 | async-start | bytes 1179648 | tf_op jit(solution)/shard_map/all_to_all | solution.py:826
  77.3 9.5 %collective-permute-start.4 = (bf16[48,256]{1,0:T(8,128)(2,1)S(1)}, bf16[48,256]{1,0:T(8,128)(2,1)S(1)}, u32[]{:S(2)}, u32[]{:S(2)}) collective-permute-start(bf16[48,256]{1,0:T(8,128)(2,1)S(1)} %convert_element_type.66), channel_id=1, source_target_pairs={{0,3},{1,2},{2,1},{3,0},{4,7},{5,6},{6,5},{7,4},{8,11},{9,10},{10,... | collective-permute-start | bytes 73736 | tf_op jit(solution)/shard_map/ppermute | solution.py:774
  79.0 7.8 %collective-permute-start.3 = (bf16[48,256]{1,0:T(8,128)(2,1)S(1)}, bf16[48,256]{1,0:T(8,128)(2,1)S(1)}, u32[]{:S(2)}, u32[]{:S(2)}) collective-permute-start(bf16[48,256]{1,0:T(8,128)(2,1)S(1)} %convert_element_type.66), channel_id=1, source_target_pairs={{0,2},{1,3},{2,0},{3,1},{4,6},{5,7},{6,4},{7,5},{8,10},{9,11},{10,... | collective-permute-start | bytes 73736 | tf_op jit(solution)/shard_map/ppermute | solution.py:774
  79.4 7.4 %collective-permute-start.2 = (bf16[48,256]{1,0:T(8,128)(2,1)S(1)}, bf16[48,256]{1,0:T(8,128)(2,1)S(1)}, u32[]{:S(2)}, u32[]{:S(2)}) collective-permute-start(bf16[48,256]{1,0:T(8,128)(2,1)S(1)} %convert_element_type.66), channel_id=1, source_target_pairs={{0,1},{1,0},{2,3},{3,2},{4,5},{5,4},{6,7},{7,6},{8,9},{9,8},{10,11... | collective-permute-start | bytes 73736 | tf_op jit(solution)/shard_map/ppermute | solution.py:774
  86.8 9.6 %collective-permute-start.9 = (bf16[48,256]{1,0:T(8,128)(2,1)S(1)}, bf16[48,256]{1,0:T(8,128)(2,1)S(1)}, u32[]{:S(2)}, u32[]{:S(2)}) collective-permute-start(bf16[48,256]{1,0:T(8,128)(2,1)S(1)} %add_add_fusion.1), channel_id=1, source_target_pairs={{0,12},{1,13},{2,14},{3,15},{4,8},{5,9},{6,10},{7,11},{8,4},{9,5},... | collective-permute-start | bytes 73736 | tf_op jit(solution)/shard_map/ppermute | solution.py:774
  90.4 6.0 %collective-permute-start.8 = (bf16[48,256]{1,0:T(8,128)(2,1)S(1)}, bf16[48,256]{1,0:T(8,128)(2,1)S(1)}, u32[]{:S(2)}, u32[]{:S(2)}) collective-permute-start(bf16[48,256]{1,0:T(8,128)(2,1)S(1)} %add_add_fusion.1), channel_id=1, source_target_pairs={{0,8},{1,9},{2,10},{3,11},{4,12},{5,13},{6,14},{7,15},{8,0},{9,1},... | collective-permute-start | bytes 73736 | tf_op jit(solution)/shard_map/ppermute | solution.py:774
  90.4 6.0 %collective-permute-start.7 = (bf16[48,256]{1,0:T(8,128)(2,1)S(1)}, bf16[48,256]{1,0:T(8,128)(2,1)S(1)}, u32[]{:S(2)}, u32[]{:S(2)}) collective-permute-start(bf16[48,256]{1,0:T(8,128)(2,1)S(1)} %add_add_fusion.1), channel_id=1, source_target_pairs={{0,4},{1,5},{2,6},{3,7},{4,0},{5,1},{6,2},{7,3},{8,12},{9,13},{10,... | collective-permute-start | bytes 73736 | tf_op jit(solution)/shard_map/ppermute | solution.py:774
